TPU v7x, 32 devices: a whole 2x2x4 slice. The times are simulated.
32 devices in a mesh: row: 8 (over z, y), ga: 4 (over x, core).
Axes of the slice: x: 2, y: 2, z: 4, core: 2. Of those that a mesh axis runs over, the one named last changes fastest.
Arguments:
- fine_feats: bfloat16 [3584, 64, 512], P(('row', 'ga')), may hold values from -6 to 6
- fine_child: int32 [3584], P(('row', 'ga')), may hold values from -1 to 255, as said below
- parent_block: int32 [256], P(('row', 'ga')), may hold values from 0 to 63, as said below
- w_parent: bfloat16 [64, 128], replicated, may hold values from -2 to 2
- w_root_in: bfloat16 [128, 256], replicated, may hold values from -1.5 to 1.5
- w_root: bfloat16 [256, 256, 3, 3, 3], P('ga'), may hold values from -0.15625 to 0.15625
- root_bias: float32 [256], P('ga'), may hold values from -0.5 to 0.5
- w_down: bfloat16 [256, 128], replicated, may hold values from -0.375 to 0.375
- w_skip: bfloat16 [128, 64], replicated, may hold values from -0.5 to 0.5
Outputs:
- fine_out: bfloat16 [3584, 64, 512], P(('row', 'ga'))
- root_features: bfloat16 [256, 32, 32, 32], P('ga', 'row')
Inputs may be any that keep to these rules, and one draw needn't show every extreme that they name: `fine_child`: parents i * 8 to (i + 1) * 8 - 1 of a region belong to the region's device of ga index i. Over the slots of a region every child index 0 to 255 appears exactly once. The slots of one device hold at most 28 children of one device's parents, and in every region some device holds exactly 28 children of each device's parents. `parent_block`: the parents of one region have distinct places.
All inputs are finite; a program needn't handle non-finite values.
Results may differ from a plain program's by a relative error of at most 0.013.
Values may be sent and summed in bfloat16 or wider, within the bound.
No kernel may reach another device: no remote copies, remote signals or barrier semaphores. Data moves between devices by JAX's collectives and lax.ppermute only.
A program may use at most 128 MiB of HBM per device.

v0:
```python
import jax
import jax.numpy as jnp
from jax import lax
from jax.sharding import PartitionSpec as P

B = 8
RXY = 32
RZ_REG = 4


def extended(cells, sides, width):
    for axis, dim in sides:
        count = lax.axis_size(axis)
        ends = count - 1
        head = lax.slice_in_dim(cells, 0, width, axis=dim)
        tail = lax.slice_in_dim(cells, cells.shape[dim] - width, cells.shape[dim], axis=dim)
        cells = jnp.concatenate(
            [
                lax.ppermute(tail, axis, [(i, (i + 1) % count) for i in range(ends)]),
                cells,
                lax.ppermute(head, axis, [((i + 1) % count, i) for i in range(ends)]),
            ],
            axis=dim,
        )
    return cells


def pool_pairs(values, half_edge):
    row_count, channel_count, voxel_count = values.shape
    cube = values.astype(jnp.float32).reshape(
        row_count, channel_count, half_edge, 2, half_edge, 2, half_edge, 2
    )
    return jnp.mean(cube, axis=(3, 5, 7)).reshape(row_count, channel_count, half_edge**3)


def upsample_pairs(values, half_edge):
    row_count, channel_count, voxel_count = values.shape
    cube = values.reshape(row_count, channel_count, half_edge, 1, half_edge, 1, half_edge, 1)
    cube = jnp.broadcast_to(
        cube, (row_count, channel_count, half_edge, 2, half_edge, 2, half_edge, 2)
    )
    return cube.reshape(row_count, channel_count, 8 * voxel_count)


def join_octants(octants, half_edge):
    parent_count = octants.shape[0]
    channel_count = octants.shape[2]
    cube = octants.reshape(parent_count, 2, 2, 2, channel_count, half_edge, half_edge, half_edge)
    cube = cube.transpose(0, 4, 1, 5, 2, 6, 3, 7)
    return cube.reshape(parent_count, channel_count, 8 * half_edge**3)


def split_octants(bricks, half_edge):
    parent_count = bricks.shape[0]
    channel_count = bricks.shape[1]
    cube = bricks.reshape(parent_count, channel_count, 2, half_edge, 2, half_edge, 2, half_edge)
    cube = cube.transpose(0, 2, 4, 6, 1, 3, 5, 7)
    return cube.reshape(parent_count, 8, channel_count, half_edge**3)


def project(values, weights):
    return jnp.einsum("pcv,cd->pdv", values, weights, preferred_element_type=jnp.float32)


def shards(
    fine_feats, fine_child, parent_block, w_parent, w_root_in, w_root, root_bias, w_down, w_skip
):
    groups = lax.axis_size("ga")
    half_edge = B // 2
    octant_voxels = half_edge**3
    slot_count = fine_feats.shape[0]
    fine_width = fine_feats.shape[1]
    parent_count = parent_block.shape[0]
    child_count = 8 * parent_count
    octant_width = fine_width * octant_voxels
    live_slot = fine_child >= 0
    pooled = (
        pool_pairs(fine_feats, half_edge).astype(jnp.bfloat16).reshape(slot_count, octant_width)
    )
    capacity = slot_count // groups
    owner_member = fine_child // child_count
    owner_hot = (
        (owner_member[:, None] == jnp.arange(groups, dtype=jnp.int32)[None, :]) & live_slot[:, None]
    ).astype(jnp.int32)
    slot_rank = jnp.sum(jnp.cumsum(owner_hot, axis=0) * owner_hot, axis=1) - 1
    outbound = jnp.where(live_slot, owner_member * capacity + slot_rank, groups * capacity)
    parcels = (
        jnp.zeros((groups * capacity + 1, octant_width), jnp.bfloat16).at[outbound].set(pooled)[:-1]
    )
    labels = (
        jnp.full((groups * capacity + 1,), -1, jnp.int32)
        .at[outbound]
        .set(fine_child % child_count)[:-1]
    )
    arrived, arrived_labels = (
        lax.all_to_all(parcels, "ga", split_axis=0, concat_axis=0, tiled=True),
        lax.all_to_all(labels, "ga", split_axis=0, concat_axis=0, tiled=True),
    )
    landing = jnp.where(arrived_labels >= 0, arrived_labels, child_count).astype(jnp.int32)
    octant_table = (
        jnp.zeros((child_count + 1, octant_width), jnp.bfloat16).at[landing].set(arrived)[:-1]
    )
    bricks = join_octants(
        octant_table.reshape(parent_count, 8, fine_width, octant_voxels), half_edge
    )
    parent_hidden = jax.nn.relu(project(bricks, w_parent)).astype(jnp.bfloat16)
    parent_pool = pool_pairs(parent_hidden, half_edge).astype(jnp.bfloat16)
    region_pool, region_blocks = (
        lax.all_gather(parent_pool, "ga", axis=0, tiled=True),
        lax.all_gather(parent_block, "ga", axis=0, tiled=True),
    )
    region_input = project(region_pool, w_root_in).astype(jnp.bfloat16)
    root_width = region_input.shape[1]
    block_side = RXY // half_edge
    block_layers = RZ_REG // half_edge
    block_total = block_layers * block_side * block_side
    placed = (
        jnp.zeros((block_total, root_width, octant_voxels), jnp.bfloat16)
        .at[region_blocks]
        .set(region_input)
    )
    slab = placed.reshape(
        block_layers, block_side, block_side, root_width, half_edge, half_edge, half_edge
    )
    slab = slab.transpose(3, 0, 4, 1, 5, 2, 6).reshape(root_width, RZ_REG, RXY, RXY)
    channel_share = w_root.shape[0]
    padded = extended(slab, (("row", 1),), 1)
    convolved = lax.conv_general_dilated(
        padded[None],
        w_root,
        (1, 1, 1),
        ((0, 0), (1, 1), (1, 1)),
        dimension_numbers=("NCDHW", "OIDHW", "NCDHW"),
        preferred_element_type=jnp.float32,
    )[0]
    root_local = jax.nn.relu(convolved + root_bias[:, None, None, None]).astype(jnp.bfloat16)
    local_blocks = root_local.reshape(
        channel_share, block_layers, half_edge, block_side, half_edge, block_side, half_edge
    )
    local_blocks = local_blocks.transpose(1, 3, 5, 0, 2, 4, 6).reshape(
        block_total, channel_share, octant_voxels
    )
    parent_root = lax.all_to_all(
        local_blocks[region_blocks], "ga", split_axis=0, concat_axis=1, tiled=True
    )
    lifted = project(parent_root, w_down)
    parent_decoded = jax.nn.relu(
        parent_hidden.astype(jnp.float32) + upsample_pairs(lifted, half_edge)
    ).astype(jnp.bfloat16)
    skip_octants = jnp.einsum(
        "pocv,cd->podv",
        split_octants(parent_decoded, half_edge),
        w_skip,
        preferred_element_type=jnp.float32,
    )
    skip_octants = skip_octants.astype(jnp.bfloat16).reshape(child_count, octant_width)
    returning = jnp.where(
        (arrived_labels >= 0)[:, None], skip_octants[jnp.maximum(arrived_labels, 0)], 0
    )
    home_octants = lax.all_to_all(returning, "ga", split_axis=0, concat_axis=0, tiled=True)
    fine_skip = jnp.where(
        live_slot[:, None], home_octants[jnp.minimum(outbound, groups * capacity - 1)], 0
    )
    fine_skip = fine_skip.reshape(slot_count, fine_width, octant_voxels).astype(jnp.float32)
    fine_out = (fine_feats.astype(jnp.float32) + upsample_pairs(fine_skip, half_edge)).astype(
        jnp.bfloat16
    )
    return (fine_out, root_local)


def solution(mesh):
    return jax.shard_map(
        shards,
        mesh=mesh,
        in_specs=(
            P(("row", "ga"), None, None),
            P(("row", "ga")),
            P(("row", "ga")),
            P(),
            P(),
            P("ga", None, None, None, None),
            P("ga"),
            P(),
            P(),
        ),
        out_specs=(P(("row", "ga"), None, None), P("ga", "row", None, None)),
        check_vma=False,
    )
```

profile of v0, /device:TPU:25, one launch (start us, length us, event | category | flops | bytes accessed | tf_op | source)
XLA Modules:
  0.0 286.8 jit_solution(15808322436689214598)
XLA Ops:
  0.6 0.7 broadcast_compare_fusion.1
  1.4 0.7 and_select_fusion.1
  2.5 0.7 compare_select_fusion
  3.2 0.9 scatter_custom_fusion
  4.1 0.7 all_to_all.35
  4.8 3.9 %all-to-all-start = ((s32[4,28,1]{1,2,0:T(1,128)}), s32[4,28,1]{1,2,0:T(1,128)S(1)}, u32[]{:S(2)}, u32[]{:S(2)}) async-start(s32[4,28,1]{1,2,0:T(1,128)} %bitcast), calls=%async_computation | async-start | bytes 4096 | tf_op jit(solution)/shard_map/all_to_all | solution.py:97
  8.6 13.3 %copy.95 = bf16[112,64,512]{0,1,2:T(8,128)(2,1)} copy(bf16[112,64,512]{2,1,0:T(8,128)(2,1)} %param.9) | data formatting | bytes 14680064 | tf_op args[0]
  21.9 5.8 %reduce_sum.28 = f32[112,64,4,4,4]{0,1,4,3,2:T(8,128)S(1)} reduce(bf16[112,64,4,2,4,2,4,2]{0,1,7,6,5,4,3,2:T(8,128)(2,1)} %bitcast.96, f32[]{:T(128)} %constant.66.clone.1), dimensions={3,5,7}, to_apply=%region_3.4 | reduce | flops 3211264 | bytes 9175044 | tf_op jit(solution)/shard_map/reduce_sum | solution.py:33
  27.9 0.8 copy.97
  28.8 0.5 copy.98
  29.3 2.1 scatter_custom_fusion.1
  31.5 1.2 all_to_all.38
  32.7 3.5 %all-to-all-start.1 = ((bf16[4,28,4096]{2,1,0:T(8,128)(2,1)}), bf16[4,28,4096]{2,1,0:T(8,128)(2,1)S(1)}, u32[]{:S(2)}, u32[]{:S(2)}) async-start(bf16[4,28,4096]{2,1,0:T(8,128)(2,1)} %all_to_all.38), calls=%async_computation.1 | async-start | bytes 2097152 | tf_op jit(solution)/shard_map/all_to_all | solution.py:96
  36.2 0.6 dynamic-slice
  37.7 12.2 %all-reduce = s32[32]{0:T(128)S(1)} all-reduce(s32[32]{0:T(128)S(1)} %dynamic-update-slice), channel_id=1, replica_groups=mesh['row'=8,'ga'=4] {'ga'}, use_global_device_ids=true, to_apply=%add | all-reduce | flops 32 | bytes 256
  49.9 0.5 broadcast.184
  50.4 0.7 reduce.3
  51.4 12.7 %scatter_custom_fusion.2 = bf16[65,4096]{1,0:T(8,128)(2,1)S(1)} fusion(s32[112]{0:T(128)S(1)} %get-tuple-element.17, bf16[112,4096]{1,0:T(8,128)(2,1)S(1)} %reshape.207, bf16[]{:T(256)} %constant.64.clone.1), kind=kCustom, calls=%fused_computation.42 | custom fusion | bytes 532482 | tf_op jit(solution)/shard_map/scatter | solution.py:101
  64.1 37.2 %reshape_reshape.3 = bf16[8,2,2,2,64,4,4,4]{7,6,5,4,3,2,1,0:T(4,128)(2,1)} reshape(bf16[64,4096]{1,0:T(8,128)(2,1)S(1)} %slice.29) | data formatting | bytes 1048576 | tf_op jit(solution)/shard_map/reshape;reshape | solution.py:48
  101.4 25.4 %copy.99 = bf16[8,64,2,4,2,4,2,4]{1,0,7,6,5,4,3,2:T(8,128)(2,1)} copy(bf16[8,64,2,4,2,4,2,4]{7,5,3,1,6,4,2,0:T(4,128)(2,1)} %bitcast.97) | data formatting | bytes 1048576 | tf_op jit(solution)/shard_map/transpose | solution.py:49
  126.8 1.6 fusion.19
  128.5 1.7 reduce_sum.29
  130.2 7.3 %all_gather.7 = bf16[32,128,64]{1,2,0:T(8,128)(2,1)S(1)} all-gather(bf16[8,128,64]{1,2,0:T(8,128)(2,1)S(1)} %bitcast.114), channel_id=1, replica_groups=mesh['row'=8,'ga'=4] {'ga'}, dimensions={0}, use_global_device_ids=true | all-gather | bytes 655360 | tf_op jit(solution)/shard_map/all_gather | solution.py:109
  137.5 1.4 fusion.20
  138.9 1.6 broadcast_in_dim.78
  140.5 5.2 %scatter_fusion = bf16[64,256,64]{1,2,0:T(8,128)(2,1)} fusion(bf16[64,256,64]{1,2,0:T(8,128)(2,1)} %broadcast_in_dim.78, s32[32]{0:T(128)S(1)} %compare_select_fusion.1, bf16[32,256,64]{1,2,0:T(8,128)(2,1)} %fusion.20), kind=kCustom, calls=%fused_computation.6 | custom fusion | bytes 3145856 | tf_op jit(solution)/shard_map/scatter | solution.py:120
  145.7 4.0 %reshape.143 = bf16[1,8,8,256,4,4,4]{3,6,5,4,2,1,0:T(4,128)(2,1)} reshape(bf16[64,256,64]{1,2,0:T(8,128)(2,1)} %scatter_fusion) | data formatting | bytes 4194304 | tf_op jit(solution)/shard_map/reshape | solution.py:122
  149.7 3.2 %copy.101 = bf16[1,8,8,256,4,4,4]{3,4,6,2,5,1,0:T(4,128)(2,1)S(1)} copy(bf16[1,8,8,256,4,4,4]{3,6,5,4,2,1,0:T(4,128)(2,1)} %reshape.143) | data formatting | bytes 4194304 | tf_op jit(solution)/shard_map/reshape | solution.py:122
  152.9 2.3 fusion.41
  155.3 3.2 %collective-permute-start = (bf16[256,1,32,32]{0,3,2,1:T(8,128)(2,1)S(1)}, bf16[256,1,32,32]{0,3,2,1:T(8,128)(2,1)S(1)}, u32[]{:S(2)}, u32[]{:S(2)}) collective-permute-start(bf16[256,1,32,32]{0,3,2,1:T(8,128)(2,1)S(1)} %copy.102), channel_id=1, source_target_pairs={{0,4},{4,8},{8,12},{12,16},{16,20},{20,24},{24,28},{1,5},{5,9},{9,... | collective-permute-start | bytes 1572872 | tf_op jit(solution)/shard_map/ppermute | solution.py:19
  158.6 3.0 %collective-permute-start.1 = (bf16[256,1,32,32]{0,3,2,1:T(8,128)(2,1)S(1)}, bf16[256,1,32,32]{0,3,2,1:T(8,128)(2,1)S(1)}, u32[]{:S(2)}, u32[]{:S(2)}) collective-permute-start(bf16[256,1,32,32]{0,3,2,1:T(8,128)(2,1)S(1)} %copy.103), channel_id=1, source_target_pairs={{4,0},{8,4},{12,8},{16,12},{20,16},{24,20},{28,24},{5,1},{9,5},{13... | collective-permute-start | bytes 1572872 | tf_op jit(solution)/shard_map/ppermute | solution.py:21
  161.6 9.9 %collective-permute-done = bf16[256,1,32,32]{0,3,2,1:T(8,128)(2,1)S(1)} collective-permute-done((bf16[256,1,32,32]{0,3,2,1:T(8,128)(2,1)S(1)}, bf16[256,1,32,32]{0,3,2,1:T(8,128)(2,1)S(1)}, u32[]{:S(2)}, u32[]{:S(2)}) %collective-permute-start) | collective-permute-done | bytes 524320 | tf_op jit(solution)/shard_map/ppermute | solution.py:19
  171.5 1.0 copy.104
  172.5 10.6 %collective-permute-done.1 = bf16[256,1,32,32]{0,3,2,1:T(8,128)(2,1)S(1)} collective-permute-done((bf16[256,1,32,32]{0,3,2,1:T(8,128)(2,1)S(1)}, bf16[256,1,32,32]{0,3,2,1:T(8,128)(2,1)S(1)}, u32[]{:S(2)}, u32[]{:S(2)}) %collective-permute-start.1) | collective-permute-done | bytes 524320 | tf_op jit(solution)/shard_map/ppermute | solution.py:21
  183.2 1.0 copy.105
  184.2 3.5 %maximum_bitcast_fusion = bf16[256,6,32,1,32]{0,1,4,2,3:T(8,128)(2,1)S(1)} fusion(bf16[256,1,32,32]{0,1,3,2:T(2,128)(2,1)S(1)} %copy.105, bf16[256,4,32,32]{0,1,3,2:T(4,128)(2,1)S(1)} %bitcast.101, bf16[256,1,32,32]{0,1,3,2:T(2,128)(2,1)S(1)} %copy.104), kind=kLoop, calls=%fused_computation.17 | loop fusion | flops 9437184 | bytes 6291456 | tf_op jit(solution)/shard_map/broadcast_in_dim | solution.py:129
  187.7 1.3 pad
  189.0 0.8 copy.108
  190.5 20.2 %fusion.16 = f32[4,32,8,5,64]{4,2,3,1,0:T(8,128)S(1)} fusion(bf16[64,256,3,3,3]{1,0,4,3,2:T(8,128)(2,1)S(1)} %copy-done, bf16[256,6,32,1,7,2]{0,4,5,2,1,3:T(8,128)(2,1)S(1)} %slice.32, bf16[256,6,32,1,8,5]{0,4,5,2,1,3:T(8,128)(2,1)S(1)} %copy.108, pred[8,5]{0,1:T(8,128)(4,1)S(1)} %copy-done.11), kind=kOutput, calls=%fused_computation.30 | convolution fusion | flops 4452319232 | bytes 7503912 | tf_op jit(solution)/shard_map/conv_general_dilated | solution.py:128
  210.7 0.5 copy.109
  211.4 1.3 copy-done.2
  212.7 2.3 fusion.15
  215.0 3.1 %copy.111 = bf16[64,64,64]{2,1,0:T(8,128)(2,1)} copy(bf16[64,64,64]{1,0,2:T(8,128)(2,1)} %bitcast.108) | data formatting | bytes 1048576 | tf_op jit(solution)/shard_map/reshape | solution.py:140
  218.1 1.9 gather_fusion
  220.0 1.1 reshape.248
  221.1 3.8 %all-to-all-start.2 = ((bf16[4,2,16384]{2,1,0:T(2,128)(2,1)}), bf16[4,2,16384]{2,1,0:T(2,128)(2,1)S(1)}, u32[]{:S(2)}, u32[]{:S(2)}) async-start(bf16[4,2,16384]{2,1,0:T(2,128)(2,1)} %reshape.248), calls=%async_computation.2 | async-start | bytes 524288 | tf_op jit(solution)/shard_map/all_to_all | solution.py:143
  224.9 5.1 %all-to-all-done.2 = bf16[4,2,16384]{2,1,0:T(2,128)(2,1)S(1)} async-done(((bf16[4,2,16384]{2,1,0:T(2,128)(2,1)}), bf16[4,2,16384]{2,1,0:T(2,128)(2,1)S(1)}, u32[]{:S(2)}, u32[]{:S(2)}) %all-to-all-start.2) | async-done | bytes 262176 | tf_op jit(solution)/shard_map/all_to_all | solution.py:143
  231.3 0.7 broadcast_in_dim.82
  232.3 0.5 copy.113
  233.1 0.4 fusion.21
  233.5 0.7 copy.114
  234.1 0.8 reshape.149
  235.0 1.1 gather_fusion.1
  236.1 1.2 gather.15
  237.2 2.5 broadcast_select_fusion
  239.8 5.1 %all-to-all-start.3 = ((bf16[4,28,4096]{2,1,0:T(8,128)(2,1)}), bf16[4,28,4096]{2,1,0:T(8,128)(2,1)}, u32[]{:S(2)}, u32[]{:S(2)}) async-start(bf16[4,28,4096]{2,1,0:T(8,128)(2,1)} %broadcast_select_fusion), calls=%async_computation.3 | async-start | bytes 2097152 | tf_op jit(solution)/shard_map/all_to_all | solution.py:160
  245.1 1.4 copy.118
  246.5 12.0 %all-to-all-done.3 = bf16[4,28,4096]{2,1,0:T(8,128)(2,1)} async-done(((bf16[4,28,4096]{2,1,0:T(8,128)(2,1)}), bf16[4,28,4096]{2,1,0:T(8,128)(2,1)}, u32[]{:S(2)}, u32[]{:S(2)}) %all-to-all-start.3) | async-done | bytes 917536 | tf_op jit(solution)/shard_map/all_to_all | solution.py:160
  258.6 1.4 all_to_all.46
  260.0 1.1 gather_fusion.2
  261.1 1.3 copy.115
  262.4 2.0 fusion.22
  264.4 8.9 %fusion = bf16[112,64,512]{0,1,2:T(8,128)(2,1)} fusion(f32[112,64,4,4,4]{0,1,4,3,2:T(8,128)S(1)} %fusion.22, bf16[112,64,512]{0,1,2:T(8,128)(2,1)} %copy.95), kind=kLoop, calls=%fused_computation.8 | loop fusion | flops 11010048 | bytes 16515072 | tf_op jit(solution)/shard_map/convert_element_type | solution.py:165
  273.2 13.4 %copy.117 = bf16[112,64,512]{2,1,0:T(8,128)(2,1)} copy(bf16[112,64,512]{0,1,2:T(8,128)(2,1)} %fusion) | data formatting | bytes 14680064
  (54 shorter events, 4.5 us)
Async XLA Ops:
  0.6 189.6 %copy-start = (bf16[64,256,3,3,3]{1,0,4,3,2:T(8,128)(2,1)S(1)}, bf16[64,256,3,3,3]{1,0,4,3,2:T(8,128)(2,1)}, u32[]{:S(2)}) copy-start(bf16[64,256,3,3,3]{1,0,4,3,2:T(8,128)(2,1)} %param.14) | copy-start | bytes 2654212
  4.8 27.9 %all-to-all-start = ((s32[4,28,1]{1,2,0:T(1,128)}), s32[4,28,1]{1,2,0:T(1,128)S(1)}, u32[]{:S(2)}, u32[]{:S(2)}) async-start(s32[4,28,1]{1,2,0:T(1,128)} %bitcast), calls=%async_computation | async-start | bytes 4096 | tf_op jit(solution)/shard_map/all_to_all | solution.py:97
  31.5 4.7 %copy-start.10 = (u32[32]{0:T(128)S(1)}, u32[32]{0:T(128)}, u32[]{:S(2)}) copy-start(u32[32]{0:T(128)} %constant.79) | copy-start | bytes 388
  31.5 6.0 %copy-start.9 = (s32[8]{0:T(128)S(1)}, s32[8]{0:T(128)}, u32[]{:S(2)}) copy-start(s32[8]{0:T(128)} %param.11) | copy-start | bytes 100
  32.7 18.5 %all-to-all-start.1 = ((bf16[4,28,4096]{2,1,0:T(8,128)(2,1)}), bf16[4,28,4096]{2,1,0:T(8,128)(2,1)S(1)}, u32[]{:S(2)}, u32[]{:S(2)}) async-start(bf16[4,28,4096]{2,1,0:T(8,128)(2,1)} %all_to_all.38), calls=%async_computation.1 | async-start | bytes 2097152 | tf_op jit(solution)/shard_map/all_to_all | solution.py:96
  101.4 25.4 %copy-start.6 = (bf16[64,128]{1,0:T(8,128)(2,1)S(1)}, bf16[64,128]{1,0:T(8,128)(2,1)}, u32[]{:S(2)}) copy-start(bf16[64,128]{1,0:T(8,128)(2,1)} %param.12) | copy-start | bytes 49156
  128.4 9.1 %copy-start.4 = (bf16[128,256]{1,0:T(8,128)(2,1)S(1)}, bf16[128,256]{1,0:T(8,128)(2,1)}, u32[]{:S(2)}) copy-start(bf16[128,256]{1,0:T(8,128)(2,1)} %param.13) | copy-start | bytes 196612
  155.3 16.2 %collective-permute-start = (bf16[256,1,32,32]{0,3,2,1:T(8,128)(2,1)S(1)}, bf16[256,1,32,32]{0,3,2,1:T(8,128)(2,1)S(1)}, u32[]{:S(2)}, u32[]{:S(2)}) collective-permute-start(bf16[256,1,32,32]{0,3,2,1:T(8,128)(2,1)S(1)} %copy.102), channel_id=1, source_target_pairs={{0,4},{4,8},{8,12},{12,16},{16,20},{20,24},{24,28},{1,5},{5,9},{9,... | collective-permute-start | bytes 1572872 | tf_op jit(solution)/shard_map/ppermute | solution.py:19
  158.6 24.6 %collective-permute-start.1 = (bf16[256,1,32,32]{0,3,2,1:T(8,128)(2,1)S(1)}, bf16[256,1,32,32]{0,3,2,1:T(8,128)(2,1)S(1)}, u32[]{:S(2)}, u32[]{:S(2)}) collective-permute-start(bf16[256,1,32,32]{0,3,2,1:T(8,128)(2,1)S(1)} %copy.103), channel_id=1, source_target_pairs={{4,0},{8,4},{12,8},{16,12},{20,16},{24,20},{28,24},{5,1},{9,5},{13... | collective-permute-start | bytes 1572872 | tf_op jit(solution)/shard_map/ppermute | solution.py:21
  189.8 0.7 copy-start.11
  211.2 1.5 copy-start.2
  211.2 1.5 copy-start.8
  219.9 11.1 %copy-start.5 = (bf16[256,128]{1,0:T(8,128)(2,1)S(1)}, bf16[256,128]{1,0:T(8,128)(2,1)}, u32[]{:S(2)}) copy-start(bf16[256,128]{1,0:T(8,128)(2,1)} %param.16) | copy-start | bytes 196612
  221.1 9.0 %all-to-all-start.2 = ((bf16[4,2,16384]{2,1,0:T(2,128)(2,1)}), bf16[4,2,16384]{2,1,0:T(2,128)(2,1)S(1)}, u32[]{:S(2)}, u32[]{:S(2)}) async-start(bf16[4,2,16384]{2,1,0:T(2,128)(2,1)} %reshape.248), calls=%async_computation.2 | async-start | bytes 524288 | tf_op jit(solution)/shard_map/all_to_all | solution.py:143
  232.3 0.7 copy-start.7
  237.2 7.6 %copy-start.3 = (f32[4,32,8,5,64]{4,1,3,2,0:T(8,128)S(1)}, f32[4,32,8,5,64]{4,1,3,2,0:T(8,128)}, u32[]{:S(2)}) copy-start(f32[4,32,8,5,64]{4,1,3,2,0:T(8,128)} %copy-done.2) | copy-start | bytes 3932164
  239.8 18.8 %all-to-all-start.3 = ((bf16[4,28,4096]{2,1,0:T(8,128)(2,1)}), bf16[4,28,4096]{2,1,0:T(8,128)(2,1)}, u32[]{:S(2)}, u32[]{:S(2)}) async-start(bf16[4,28,4096]{2,1,0:T(8,128)(2,1)} %broadcast_select_fusion), calls=%async_computation.3 | async-start | bytes 2097152 | tf_op jit(solution)/shard_map/all_to_all | solution.py:160
  273.2 13.4 %copy-start.1 = (bf16[64,256,3,3,3]{1,0,4,3,2:T(8,128)(2,1)S(1)}, bf16[64,256,3,3,3]{1,0,4,3,2:T(8,128)(2,1)}, u32[]{:S(2)}) copy-start(bf16[64,256,3,3,3]{1,0,4,3,2:T(8,128)(2,1)} %param.14) | copy-start | bytes 2654212
where the time goes:
time: 292 us; the launch traced here: 287 us
  local copies, waits for them, and re-layouts  151 us (52%)
  waiting for transfers between devices  37.7 us (13%)
  other arithmetic  30.7 us (11%)
  matrix products  23.8 us (8%)
  starting transfers between devices  22.5 us (8%)
  blocking collectives  19.5 us (7%)
    another operation x1, local copies, waits for them, and re-layouts, join_octants(): octants.reshape(parent_count, 2, 2, 2, channel_count, half_edge, half_edg...  37.2 us
    unnamed x33, local copies, waits for them, and re-layouts  32.1 us
    transpose x1, local copies, waits for them, and re-layouts, join_octants(): cube = cube.transpose(0, 4, 1, 5, 2, 6, 3, 7)  25.4 us
    conv_general_dilated x1, matrix products, shards(): lax.conv_general_dilated(padded[None], w_root, (1, 1, 1), ((0, 0), (1, 1)...  20.2 us
    scatter x1, local copies, waits for them, and re-layouts, shards(): jnp.zeros((child_count + 1, octant_width), jnp.bfloat16).at[landing]  12.7 us
    unnamed x1, blocking collectives  12.2 us
    all_to_all x1, waiting for transfers between devices, shards(): lax.all_to_all(returning, 'ga', split_axis=0, concat_axis=0, tiled=True)  12 us
    ppermute x1, waiting for transfers between devices, extended(): lax.ppermute(head, axis, [((i + 1) % count, i) for i in range(ends)])  10.6 us
  transfers between devices with their start and end apart: 6, of which 4 were waited for; matrix products, arithmetic and copies ran while one was open for 10% of the time, Pallas kernels for 0%

commit v1 on v0

v1 whole, which is shorter than its diff:
```python
import functools

import jax
import jax.numpy as jnp
from jax import lax
from jax.experimental import pallas as pl
from jax.experimental.pallas import tpu as pltpu
from jax.sharding import PartitionSpec as P

B = 8
RXY = 32
RZ_REG = 4

HALF = B // 2
OCT = RXY // 2
LAYERS = RZ_REG // 2
PLANE = OCT * OCT
BORDERED = PLANE + 2 * OCT
SUBS = 8
META = 16
BF16 = jnp.bfloat16
F32 = jnp.float32
VMEM = pl.BlockSpec(memory_space=pltpu.VMEM)
SMEM = pl.BlockSpec(memory_space=pltpu.SMEM)


def params(mib):
    return pltpu.CompilerParams(vmem_limit_bytes=mib << 20)


def cost(macs, moved):
    return pl.CostEstimate(flops=2 * macs, bytes_accessed=moved, transcendentals=0)


def iota(shape, axis):
    return lax.broadcasted_iota(jnp.int32, shape, axis)


def dot(left, right):
    return jnp.dot(left, right, preferred_element_type=F32)


def dot_nt(left, right):
    return lax.dot_general(left, right, (((1,), (1,)), ((), ())), preferred_element_type=F32)


def hidden_voxel(fine):
    z, y, x = fine // (B * B), fine // B % B, fine % B
    low = z // 2 % 2 * 4 + y // 2 % 2 * 2 + x // 2 % 2
    high = z // HALF * 4 + y // HALF * 2 + x // HALF
    return low * SUBS + high


def fine_in_kernel(
    child_ref, block_ref, fine_ref, w_ref, hidden_ref, pooled_ref, pool, weights, tops, meta, *, total, padded
):
    step = pl.program_id(0)
    chunk, width, voxels = fine_ref.shape
    depth = w_ref.shape[1]
    group = hidden_ref.shape[2] // depth
    cells = voxels // SUBS

    @pl.when(step == 0)
    def _():
        hit = hidden_voxel(iota((voxels, cells), 0)) == iota((voxels, cells), 1)
        pool[...] = jnp.where(hit, 1.0 / SUBS, 0.0).astype(BF16)
        weights[...] = jnp.zeros_like(weights)
        for s in range(group):
            weights[s * width : (s + 1) * width, s * depth : (s + 1) * depth] = w_ref[...]
        meta[...] = jnp.full_like(meta, -1.0)
        meta[0:1, 0:total] = (child_ref[...] >> 3).astype(F32)
        meta[1:2, 0:total] = (child_ref[...] & 7).astype(F32)
        meta[2:3, 0 : block_ref.shape[1]] = block_ref[...].astype(F32)
        pooled_ref[SUBS * padded : SUBS * padded + META, :] = meta[...].astype(BF16)

    for j in range(chunk // group):
        cube = fine_ref[j * group : (j + 1) * group].reshape(group * width, voxels)
        octants = dot(cube, pool[...]).astype(BF16)
        hidden = jnp.maximum(dot(octants.T, weights[...]), 0.0).astype(BF16)
        hidden_ref[j] = hidden
        top = jnp.sum(hidden.astype(F32).reshape(SUBS, SUBS, group * depth), axis=0) * (1.0 / SUBS)
        for s in range(group):
            at = (j * group + s) * SUBS
            tops[at : at + SUBS, :] = top[:, s * depth : (s + 1) * depth]
    if padded != total:
        slot = step * chunk + iota(tops.shape, 0) // SUBS
        tops[...] = jnp.where(slot < total, tops[...], 0.0)
    for v in range(SUBS):
        at = pl.multiple_of(v * padded + step * chunk, chunk)
        pooled_ref[pl.ds(at, chunk), :] = tops[pl.ds(v, chunk, stride=SUBS), :].astype(BF16)


def fine_in(fine_feats, fine_child, parent_block, w_parent, chunk, padded):
    total, width, voxels = fine_feats.shape
    depth = w_parent.shape[1]
    group = 256 // width
    cells = voxels // SUBS
    return pl.pallas_call(
        functools.partial(fine_in_kernel, total=total, padded=padded),
        grid=(padded // chunk,),
        in_specs=[
            pl.BlockSpec((1, total), lambda i: (0, 0)),
            pl.BlockSpec((1, parent_block.shape[0]), lambda i: (0, 0)),
            pl.BlockSpec((chunk, width, voxels), lambda i: (i, 0, 0)),
            pl.BlockSpec((width, depth), lambda i: (0, 0)),
        ],
        out_specs=[
            pl.BlockSpec((chunk // group, cells, group * depth), lambda i: (i, 0, 0)),
            pl.BlockSpec((SUBS * padded + META, depth), lambda i: (0, 0)),
        ],
        out_shape=[
            jax.ShapeDtypeStruct((padded // group, cells, group * depth), BF16),
            jax.ShapeDtypeStruct((SUBS * padded + META, depth), BF16),
        ],
        scratch_shapes=[
            pltpu.VMEM((voxels, cells), BF16),
            pltpu.VMEM((group * width, group * depth), BF16),
            pltpu.VMEM((chunk * SUBS, depth), F32),
            pltpu.VMEM((META, 128), F32),
        ],
        compiler_params=params(24),
        cost_estimate=cost(total * width * voxels * 256, 2 * total * width * voxels),
        name="fine_in",
    )(fine_child[None], parent_block[None], fine_feats, w_parent)


def fold_kernel(w_ref, in_ref, out_ref):
    share = w_ref.shape[3]
    depth = in_ref.shape[0]
    nothing = jnp.zeros((share, w_ref.shape[4]), BF16)
    out_ref[:, 0, :, 2 * share :] = jnp.zeros((3, 4 * depth, 2 * share), BF16)
    out_ref[:, 3, :, 0 : 2 * share] = jnp.zeros((3, 4 * depth, 2 * share), BF16)
    for a in range(3):
        for b in range(3):
            for j in range(4):
                first = w_ref[a, b, j] if j < 3 else nothing
                second = w_ref[a, b, j - 1] if j > 0 else nothing
                pair = jnp.concatenate([first, second], axis=0)
                folded = dot_nt(in_ref[...], pair).astype(BF16)
                rows = slice(j * depth, (j + 1) * depth)
                out_ref[a, b, rows, 0 : 2 * share] = folded
                out_ref[a, b + 1, rows, 2 * share : 4 * share] = folded


def fold(w_root, w_root_in):
    share = w_root.shape[0]
    depth = w_root_in.shape[0]
    return pl.pallas_call(
        fold_kernel,
        in_specs=[VMEM, VMEM],
        out_specs=VMEM,
        out_shape=jax.ShapeDtypeStruct((3, 4, 4 * depth, 4 * share), BF16),
        compiler_params=params(16),
        cost_estimate=cost(36 * depth * 256 * 128, 6 << 20),
        name="fold",
    )(w_root.transpose(2, 3, 4, 0, 1), w_root_in)


def y_window(j):
    return ((1, 0), (0, OCT), (1, OCT), (0, 2 * OCT))[j]


def place_kernel(offsets, padded, pairs, *refs):
    groups = len(offsets)
    pooled_refs, w_ref = refs[:groups], refs[groups]
    grid_ref, place_ref, pair_ref, step_ref = refs[groups + 1 : groups + 5]
    table = refs[groups + 5]
    depth = pooled_refs[0].shape[1]
    lane_count = groups * 128
    me = lax.axis_index("ga")
    row = lax.axis_index("row")

    metas = [r[SUBS * padded : SUBS * padded + META, :] for r in pooled_refs]
    parent = jnp.concatenate([m[0:1].astype(F32) for m in metas], axis=1).astype(jnp.int32)
    octant = jnp.concatenate([m[1:2].astype(F32) for m in metas], axis=1).astype(jnp.int32)
    found = jnp.zeros((META, lane_count), F32)
    for k, offset in enumerate(offsets):
        at = iota((128, lane_count), 0)
        hot = (at < pairs) & (parent == at + (me ^ offset) * pairs)
        found += dot(metas[k], jnp.where(hot, 1.0, 0.0).astype(BF16))
    block = found[2:3].astype(jnp.int32)
    side = RXY // HALF
    z = block // (side * side) * 2 + (octant >> 2)
    y = block // side % side * 2 + (octant >> 1) % 2
    x = block % side * 2 + octant % 2
    live = parent >= 0
    place = jnp.where(live, (z * OCT + y) * OCT + x, -1)
    place_ref[...] = jnp.broadcast_to(place, place_ref.shape)

    for k, pooled_ref in enumerate(pooled_refs):
        for v in range(SUBS):
            vz, vy, vx = v >> 2, v >> 1 & 1, v & 1
            lanes = slice((vx * 4 + vz * 2 + vy) * depth, (vx * 4 + vz * 2 + vy + 1) * depth)
            table[k * 128 : k * 128 + padded, lanes] = pooled_ref[v * padded : (v + 1) * padded, :]
            if padded < 128:
                table[k * 128 + padded : (k + 1) * 128, lanes] = jnp.zeros((128 - padded, depth), BF16)

    grid_ref[:, :, 0:OCT, :] = jnp.zeros((2, RZ_REG, OCT, 4 * depth), BF16)
    grid_ref[:, :, OCT + PLANE :, :] = jnp.zeros((2, RZ_REG, OCT, 4 * depth), BF16)
    shifted = (
        (0, 1, jnp.where(live & (x < OCT - 1), place + 1, -1)),
        (1, 0, place),
        (2, 1, place),
        (3, 0, jnp.where(live & (x > 0), place - 1, -1)),
    )
    for j, vx, at in shifted:
        hot = jnp.where(iota((LAYERS * PLANE, lane_count), 0) == at, 1.0, 0.0).astype(BF16)
        for vz in range(2):
            first = (vx * 4 + vz * 2) * depth
            both = dot(hot, table[:, first : first + 2 * depth]).astype(BF16)
            for vy in range(2):
                for layer in range(LAYERS):
                    grid_ref[vy, layer * 2 + vz, OCT : OCT + PLANE, j * depth : (j + 1) * depth] = both[
                        layer * PLANE : (layer + 1) * PLANE, vy * depth : (vy + 1) * depth
                    ]

    even = row % 2 == 0
    for out_ref, up in ((pair_ref, even), (step_ref, jnp.logical_not(even))):
        plane = jnp.where(up, RZ_REG - 1, 0)
        dz = jnp.where(up, 0, 2)
        total = None
        for j in range(4):
            vy, first = y_window(j)
            part = dot(grid_ref[vy, plane, first : first + PLANE, :], w_ref[dz, j])
            total = part if total is None else total + part
        out_ref[...] = total.astype(BF16)


def place(pooled, offsets, folded, padded, pairs):
    groups = len(offsets)
    depth = pooled[0].shape[1]
    wide = folded.shape[3]
    return pl.pallas_call(
        functools.partial(place_kernel, offsets, padded, pairs),
        in_specs=[VMEM] * (groups + 1),
        out_specs=[VMEM] * 4,
        out_shape=[
            jax.ShapeDtypeStruct((2, RZ_REG, BORDERED, 4 * depth), BF16),
            jax.ShapeDtypeStruct((8, groups * 128), jnp.int32),
            jax.ShapeDtypeStruct((PLANE, wide), BF16),
            jax.ShapeDtypeStruct((PLANE, wide), BF16),
        ],
        scratch_shapes=[pltpu.VMEM((groups * 128, SUBS * depth), BF16)],
        compiler_params=params(24),
        cost_estimate=cost(2 << 28, 6 << 20),
        name="place",
    )(*pooled, folded)


def conv_kernel(grid_ref, w_ref, out_ref):
    for z in range(RZ_REG):
        total = None
        for a in range(3):
            if not 0 <= z + a - 1 < RZ_REG:
                continue
            for j in range(4):
                vy, first = y_window(j)
                part = dot(grid_ref[vy, z + a - 1, first : first + PLANE, :], w_ref[a, j])
                total = part if total is None else total + part
        out_ref[z] = total


def conv(grid, folded):
    wide = folded.shape[3]
    return pl.pallas_call(
        conv_kernel,
        in_specs=[VMEM, VMEM],
        out_specs=VMEM,
        out_shape=jax.ShapeDtypeStruct((RZ_REG, PLANE, wide), F32),
        compiler_params=params(16),
        cost_estimate=cost(10 * 4 * PLANE * 512 * 256, 6 << 20),
        name="conv",
    )(grid, folded)


def finish_kernel(padded, place_ref, sums_ref, pair_ref, step_ref, bias_ref, *refs):
    groups = len(refs) - 1
    root_ref, send_refs = refs[0], refs[1:]
    lane_count = place_ref.shape[1]
    row = lax.axis_index("row")
    even = row % 2 == 0
    has_pair_up = even
    last = lax.axis_size("row") - 1
    bias = jnp.concatenate([bias_ref[...]] * 4, axis=1)
    pair = pair_ref[...].astype(F32)
    step = step_ref[...].astype(F32)
    above = jnp.where(even, pair, step)
    below = jnp.where(even, step, pair)
    above = jnp.where(row < last, above, 0.0)
    below = jnp.where(row > 0, below, 0.0)
    del has_pair_up
    column = place_ref[...].astype(F32).T[:, 0:1].astype(jnp.int32)
    hot = jnp.where(column == iota((lane_count, LAYERS * PLANE), 1), 1.0, 0.0).astype(BF16)
    for z in range(RZ_REG):
        total = sums_ref[z] + bias
        if z == 0:
            total += below
        if z == RZ_REG - 1:
            total += above
        root_ref[z % 2, z // 2 * PLANE : (z // 2 + 1) * PLANE, :] = jnp.maximum(total, 0.0).astype(BF16)
    wide = root_ref.shape[2]
    for vz in range(2):
        picked = dot(hot, root_ref[vz]).astype(BF16)
        for k in range(groups):
            send_refs[k][:, vz * wide : (vz + 1) * wide] = picked[k * 128 : k * 128 + padded]


def finish(places, sums, pair, step, root_bias, groups, padded):
    wide = sums.shape[2]
    return pl.pallas_call(
        functools.partial(finish_kernel, padded),
        in_specs=[VMEM] * 5,
        out_specs=[VMEM] * (groups + 1),
        out_shape=[jax.ShapeDtypeStruct((2, LAYERS * PLANE, wide), BF16)]
        + [jax.ShapeDtypeStruct((padded, 2 * wide), BF16)] * groups,
        compiler_params=params(24),
        cost_estimate=cost(1 << 27, 3 << 20),
        name="finish",
    )(places, sums, pair, step, root_bias[None])


def unravel_kernel(root_ref, out_ref):
    share = root_ref.shape[2] // 4
    rows, half = 2 * PLANE // 2, PLANE // 2
    x, y = iota((rows, half), 0), iota((rows, half), 1)
    same = x // RXY == y // OCT
    spread = [
        jnp.where(same & (x % RXY == 2 * (y % OCT) + vx), 1.0, 0.0).astype(BF16) for vx in range(2)
    ]
    lines = half // OCT
    for z in range(RZ_REG):
        for part in range(2):
            first = z // 2 * PLANE + part * half
            for vy in range(2):
                at = vy * 2 * share
                even = root_ref[z % 2, first : first + half, at : at + share]
                odd = root_ref[z % 2, first : first + half, at + share : at + 2 * share]
                line = (dot(spread[0], even) + dot(spread[1], odd)).astype(BF16)
                out_ref[z, part * lines : (part + 1) * lines, vy] = line.reshape(lines, RXY, share)


def unravel(root):
    share = root.shape[2] // 4
    out = pl.pallas_call(
        unravel_kernel,
        in_specs=[VMEM],
        out_specs=VMEM,
        out_shape=jax.ShapeDtypeStruct((RZ_REG, OCT, 2, RXY, share), BF16),
        compiler_params=params(16),
        cost_estimate=cost(1 << 28, 2 << 20),
        name="unravel",
    )(root)
    return out.reshape(RZ_REG, RXY, RXY, share).transpose(3, 0, 1, 2)


def fine_out_kernel(offsets, *refs):
    groups = len(offsets)
    child_ref, fine_ref, hidden_ref, down_ref, skip_ref = refs[:5]
    come_refs = refs[5 : 5 + groups]
    out_ref = refs[5 + groups]
    spread, weights, down, lifted = refs[6 + groups :]
    step = pl.program_id(0)
    chunk, width, voxels = fine_ref.shape
    depth = down_ref.shape[1]
    group = hidden_ref.shape[2] // depth
    cells = voxels // SUBS
    total = child_ref.shape[0]
    share = come_refs[0].shape[1] // SUBS
    me = lax.axis_index("ga")

    @pl.when(step == 0)
    def _():
        hit = hidden_voxel(iota((cells, voxels), 1)) == iota((cells, voxels), 0)
        spread[...] = jnp.where(hit, 1.0, 0.0).astype(BF16)
        weights[...] = jnp.zeros_like(weights)
        turned = skip_ref[...].T
        for s in range(group):
            weights[s * depth : (s + 1) * depth, s * width : (s + 1) * width] = turned
        down[...] = jnp.zeros_like(down)
        for k, offset in enumerate(offsets):
            rows = down_ref[pl.ds(pl.multiple_of((me ^ offset) * share, share), share), :]
            for vx in range(2):
                first = (k * 2 + vx) * share
                down[first : first + share, vx * depth : (vx + 1) * depth] = rows
        for zy in range(4):
            lanes = slice(zy * 2 * share, (zy + 1) * 2 * share)
            both = dot(jnp.concatenate([r[:, lanes] for r in come_refs], axis=1), down[...])
            slots = both.shape[0]
            for vx in range(2):
                lifted[pl.ds(zy * 2 + vx, slots, stride=SUBS), :] = both[:, vx * depth : (vx + 1) * depth]

    for j in range(chunk // group):
        parts = []
        for s in range(group):
            slot = step * chunk + j * group + s
            hidden = hidden_ref[j, :, s * depth : (s + 1) * depth].astype(F32)
            top = lifted[pl.ds(pl.multiple_of(slot * SUBS, SUBS), SUBS), :]
            both = jnp.maximum(hidden.reshape(SUBS, SUBS, depth) + top[None], 0.0)
            live = child_ref[jnp.minimum(slot, total - 1)] >= 0
            parts.append(jnp.where(live, both, 0.0).reshape(cells, depth).astype(BF16))
        skip = dot(jnp.concatenate(parts, axis=1), weights[...]).astype(BF16)
        up = dot(skip.T, spread[...])
        cube = fine_ref[j * group : (j + 1) * group].reshape(group * width, voxels)
        out = (cube.astype(F32) + up).astype(BF16)
        out_ref[j * group : (j + 1) * group] = out.reshape(group, width, voxels)


def fine_out(fine_feats, fine_child, hidden, w_down, w_skip, come, offsets, chunk, padded):
    total, width, voxels = fine_feats.shape
    depth = w_down.shape[1]
    group = 256 // width
    cells = voxels // SUBS
    groups = len(offsets)
    share = come[0].shape[1] // SUBS

    def whole(array):
        return pl.BlockSpec(array.shape, lambda i: (0,) * array.ndim)

    turned = w_skip.T
    return pl.pallas_call(
        functools.partial(fine_out_kernel, offsets),
        grid=(padded // chunk,),
        in_specs=[
            SMEM,
            pl.BlockSpec((chunk, width, voxels), lambda i: (i, 0, 0)),
            pl.BlockSpec((chunk // group, cells, group * depth), lambda i: (i, 0, 0)),
            whole(w_down),
            whole(turned),
        ]
        + [whole(c) for c in come],
        out_specs=pl.BlockSpec((chunk, width, voxels), lambda i: (i, 0, 0)),
        out_shape=jax.ShapeDtypeStruct(fine_feats.shape, BF16),
        scratch_shapes=[
            pltpu.VMEM((cells, voxels), BF16),
            pltpu.VMEM((group * depth, group * width), BF16),
            pltpu.VMEM((groups * 2 * share, 2 * depth), BF16),
            pltpu.VMEM((padded * SUBS, depth), F32),
        ],
        compiler_params=params(24),
        cost_estimate=cost(total * width * voxels * 256, 4 * total * width * voxels),
        name="fine_out",
    )(fine_child, fine_feats, hidden, w_down, turned, *come)


def shards(
    fine_feats, fine_child, parent_block, w_parent, w_root_in, w_root, root_bias, w_down, w_skip
):
    groups = lax.axis_size("ga")
    rows = lax.axis_size("row")
    slots = fine_feats.shape[0]
    chunk = 16
    padded = -(-slots // chunk) * chunk
    pairs = parent_block.shape[0]

    hidden, pooled = fine_in(fine_feats, fine_child, parent_block, w_parent, chunk, padded)

    gathered, offsets = [pooled], [0]
    bit = groups // 2
    while bit:
        swap = [(i, i ^ bit) for i in range(groups)]
        gathered += [lax.ppermute(part, "ga", swap) for part in gathered]
        offsets += [offset ^ bit for offset in offsets]
        bit //= 2
    offsets = tuple(offsets)

    folded = fold(w_root, w_root_in)
    grid, places, pair, step = place(gathered, offsets, folded, padded, pairs)
    pair_swap = [(i, i ^ 1) for i in range(rows) if i ^ 1 < rows]
    step_swap = [(i, (i - 1 ^ 1) + 1) for i in range(1, rows) if (i - 1 ^ 1) + 1 < rows]
    pair = lax.ppermute(pair, "row", pair_swap)
    step = lax.ppermute(step, "row", step_swap)
    sums = conv(grid, folded)
    root, *sends = finish(places, sums, pair, step, root_bias, groups, padded)
    come = [sends[0]]
    for offset, send in zip(offsets[1:], sends[1:]):
        come.append(lax.ppermute(send, "ga", [(i, i ^ offset) for i in range(groups)]))
    root_out = unravel(root)
    fine = fine_out(fine_feats, fine_child, hidden, w_down, w_skip, come, offsets, chunk, padded)
    return (fine, root_out)


def solution(mesh):
    return jax.shard_map(
        shards,
        mesh=mesh,
        in_specs=(
            P(("row", "ga"), None, None),
            P(("row", "ga")),
            P(("row", "ga")),
            P(),
            P(),
            P("ga", None, None, None, None),
            P("ga"),
            P(),
            P(),
        ),
        out_specs=(P(("row", "ga"), None, None), P("ga", "row", None, None)),
        check_vma=False,
    )
```

time: 292 us -> 54.1 us (0.19); the launches traced: 287 us -> 53.8 us
  local copies, waits for them, and re-layouts: 151 us -> 5.15 us
  other arithmetic: 30.7 us -> 0.01 us
  waiting for transfers between devices: 37.7 us -> 10.1 us
  Pallas kernels: 0 us -> 27.5 us
  matrix products: 23.8 us -> 0 us
  blocking collectives: 19.5 us -> 0 us
  starting transfers between devices: 22.5 us -> 10.3 us
    another operation x1 -> x0, local copies, waits for them, and re-layouts: 37.2 us -> none  [join_octants(): octants.reshape(parent_count, 2, 2, 2, channel_count, half_edge, half_edg...]
    pallas_call x0 -> x7, Pallas kernels: none -> 27.5 us  [the longest x1 10.4 us: fine_out(): pl.pallas_call(functools.partial(fine_out_kernel, offsets), grid=(padded...]
    unnamed x33 -> x24, local copies, waits for them, and re-layouts: 32.1 us -> 5.15 us
    transpose x2 -> x0, local copies, waits for them, and re-layouts: 26 us -> none  [the longest x1 25.4 us: join_octants(): cube = cube.transpose(0, 4, 1, 5, 2, 6, 3, 7)]
    scatter x4 -> x0, local copies, waits for them, and re-layouts: 21 us -> none  [the longest x1 12.7 us: shards(): jnp.zeros((child_count + 1, octant_width), jnp.bfloat16).at[landing]]
    conv_general_dilated x1 -> x0, matrix products: 20.2 us -> none  [shards(): lax.conv_general_dilated(padded[None], w_root, (1, 1, 1), ((0, 0), (1, 1)...]
    all_to_all x4 -> x0, waiting for transfers between devices: 17.2 us -> none  [the longest x1 12 us: shards(): lax.all_to_all(returning, 'ga', split_axis=0, concat_axis=0, tiled=True)]
    all_to_all x4 -> x0, starting transfers between devices: 16.3 us -> none  [the longest x1 5.08 us: shards(): lax.all_to_all(returning, 'ga', split_axis=0, concat_axis=0, tiled=True)]
  transfers between devices with their start and end apart: 6 -> 8, of which waited for: 4 -> 4; matrix products, arithmetic and copies ran while one was open for 10% -> 0% of each run, Pallas kernels for 0% -> 10%
where the time goes in v1:
time: 54.1 us; the launch traced here: 53.8 us
  Pallas kernels  27.5 us (51%)
  starting transfers between devices  10.3 us (19%)
  waiting for transfers between devices  10.1 us (19%)
  local copies, waits for them, and re-layouts  5.15 us (10%)
  between operations  0.79 us (1%)
    pallas_call x1, Pallas kernels, fine_out(): pl.pallas_call(functools.partial(fine_out_kernel, offsets), grid=(padded...  10.4 us
    pallas_call x1, Pallas kernels, fine_in(): pl.pallas_call(functools.partial(fine_in_kernel, total=total, padded=padd...  8.91 us
    unnamed x24, local copies, waits for them, and re-layouts  5.15 us
    ppermute x3, waiting for transfers between devices, shards(): gathered += [lax.ppermute(part, 'ga', swap) for part in gathered]  4.73 us
    ppermute x3, starting transfers between devices, shards(): gathered += [lax.ppermute(part, 'ga', swap) for part in gathered]  3.77 us
    ppermute x3, starting transfers between devices, shards(): lax.ppermute(send, 'ga', [(i, i ^ offset) for i in range(groups)])  3.21 us
    ppermute x3, waiting for transfers between devices, shards(): lax.ppermute(send, 'ga', [(i, i ^ offset) for i in range(groups)])  3.18 us
    pallas_call x1, Pallas kernels, conv(): pl.pallas_call(conv_kernel, in_specs=[VMEM, VMEM], out_specs=VMEM, out_sh...  2.86 us
  transfers between devices with their start and end apart: 8, of which 4 were waited for; matrix products, arithmetic and copies ran while one was open for 0% of the time, Pallas kernels for 10%

profile of v1, /device:TPU:25, one launch (start us, length us, event | category | flops | bytes accessed | tf_op | source)
XLA Modules:
  0.0 53.8 jit_solution(13638245414271600269)
XLA Ops:
  0.6 0.0 copy-start
  0.6 3.1 %copy-done = bf16[112,64,512]{2,1,0:T(8,128)(2,1)S(1)} copy-done((bf16[112,64,512]{2,1,0:T(8,128)(2,1)S(1)}, bf16[112,64,512]{2,1,0:T(8,128)(2,1)}, u32[]{:S(2)}) %copy-start) | copy-done | bytes 7340056
  3.7 0.0 copy-start.4
  3.7 0.7 %copy-done.4 = bf16[64,128]{1,0:T(8,128)(2,1)S(1)} copy-done((bf16[64,128]{1,0:T(8,128)(2,1)S(1)}, bf16[64,128]{1,0:T(8,128)(2,1)}, u32[]{:S(2)}) %copy-start.4) | copy-done | bytes 16408
  4.4 0.0 copy-start.6
  4.4 0.7 %copy-done.6 = s32[112]{0:T(128)S(1)} copy-done((s32[112]{0:T(128)S(1)}, s32[112]{0:T(128)}, u32[]{:S(2)}) %copy-start.6) | copy-done | bytes 472
  5.1 0.0 copy-start.9
  5.1 0.7 %copy-done.9 = s32[8]{0:T(128)S(1)} copy-done((s32[8]{0:T(128)S(1)}, s32[8]{0:T(128)}, u32[]{:S(2)}) %copy-start.9) | copy-done | bytes 56
  5.7 0.0 copy-start.1
  5.7 0.0 copy-start.2
  5.8 8.9 %fine_in.1 = (bf16[28,64,512]{2,1,0:T(8,128)(2,1)S(1)}, bf16[912,128]{1,0:T(8,128)(2,1)S(1)}) custom-call(s32[1,112]{1,0:T(1,128)S(1)} %bitcast.12, s32[1,8]{1,0:T(1,128)S(1)} %bitcast.14, bf16[112,64,512]{2,1,0:T(8,128)(2,1)S(1)} %copy-done, bf16[64,128]{1,0:T(8,128)(2,1)S(1)} %copy-done.4), custom_call_target="tpu_custom_call" | custom-call | flops 1879048192 | bytes 7340032 | tf_op jit(solution)/shard_map/fine_in/pallas_call | solution.py:98
  14.7 1.3 %collective-permute-start = (bf16[912,128]{1,0:T(8,128)(2,1)S(1)}, bf16[912,128]{1,0:T(8,128)(2,1)S(1)}, u32[]{:S(2)}, u32[]{:S(2)}) collective-permute-start(bf16[912,128]{1,0:T(8,128)(2,1)S(1)} %get-tuple-element.14.refs_0_), channel_id=1, source_target_pairs={{0,2},{1,3},{2,0},{3,1},{4,6},{5,7},{6,4},{7,5},{8,10},{9,11},{10,... | collective-permute-start | bytes 700424 | tf_op jit(solution)/shard_map/ppermute | solution.py:461
  15.9 1.0 %collective-permute-start.1 = (bf16[912,128]{1,0:T(8,128)(2,1)S(1)}, bf16[912,128]{1,0:T(8,128)(2,1)S(1)}, u32[]{:S(2)}, u32[]{:S(2)}) collective-permute-start(bf16[912,128]{1,0:T(8,128)(2,1)S(1)} %get-tuple-element.14.refs_0_), channel_id=1, source_target_pairs={{0,1},{1,0},{2,3},{3,2},{4,5},{5,4},{6,7},{7,6},{8,9},{9,8},{10,11... | collective-permute-start | bytes 700424 | tf_op jit(solution)/shard_map/ppermute | solution.py:461
  16.9 4.4 %collective-permute-done.refs_1_ = bf16[912,128]{1,0:T(8,128)(2,1)S(1)} collective-permute-done((bf16[912,128]{1,0:T(8,128)(2,1)S(1)}, bf16[912,128]{1,0:T(8,128)(2,1)S(1)}, u32[]{:S(2)}, u32[]{:S(2)}) %collective-permute-start) | collective-permute-done | bytes 233504 | tf_op jit(solution)/shard_map/ppermute | solution.py:461
  21.3 1.5 %collective-permute-start.2 = (bf16[912,128]{1,0:T(8,128)(2,1)S(1)}, bf16[912,128]{1,0:T(8,128)(2,1)S(1)}, u32[]{:S(2)}, u32[]{:S(2)}) collective-permute-start(bf16[912,128]{1,0:T(8,128)(2,1)S(1)} %collective-permute-done.refs_1_), channel_id=1, source_target_pairs={{0,1},{1,0},{2,3},{3,2},{4,5},{5,4},{6,7},{7,6},{8,9},{9,8},{10,11... | collective-permute-start | bytes 700424 | tf_op jit(solution)/shard_map/ppermute | solution.py:461
  22.8 0.0 copy-done.1
  22.8 0.0 copy-done.2
  22.8 0.8 %fold.1.refs_4_.w_ref = bf16[3,4,512,256]{3,2,1,0:T(8,128)(2,1)S(1)} custom-call(bf16[3,3,3,64,256]{4,3,2,1,0:T(8,128)(2,1)S(1)} %bitcast.10, bf16[128,256]{1,0:T(8,128)(2,1)S(1)} %copy-done.2), custom_call_target="tpu_custom_call" | custom-call | flops 301989888 | bytes 6291456 | tf_op jit(solution)/shard_map/fold/pallas_call | solution.py:148
  23.6 0.0 collective-permute-done.1.refs_2_
  23.6 0.3 collective-permute-done.2.refs_3_
  24.0 2.1 %place.1 = (bf16[2,4,288,512]{3,2,1,0:T(8,128)(2,1)S(1)}, s32[8,512]{1,0:T(8,128)S(1)}, bf16[256,256]{1,0:T(8,128)(2,1)S(1)}, bf16[256,256]{1,0:T(8,128)(2,1)S(1)}) custom-call(bf16[912,128]{1,0:T(8,128)(2,1)S(1)} %get-tuple-element.14.refs_0_, bf16[912,128]{1,0:T(8,128)(2,1)S(1)} %collective-permute-done.refs_1_, ...), custom_call_target="tpu_custom_call" | custom-call | flops 1073741824 | bytes 6291456 | tf_op jit(solution)/shard_map/place/pallas_call | solution.py:233
  26.1 1.3 %collective-permute-start.3 = (bf16[256,256]{1,0:T(8,128)(2,1)S(1)}, bf16[256,256]{1,0:T(8,128)(2,1)S(1)}, u32[]{:S(2)}, u32[]{:S(2)}) collective-permute-start(bf16[256,256]{1,0:T(8,128)(2,1)S(1)} %get-tuple-element.17), channel_id=1, source_target_pairs={{0,4},{4,0},{8,12},{12,8},{16,20},{20,16},{24,28},{28,24},{1,5},{5... | collective-permute-start | bytes 393224 | tf_op jit(solution)/shard_map/ppermute | solution.py:470
  27.4 2.0 %collective-permute-start.4 = (bf16[256,256]{1,0:T(8,128)(2,1)S(1)}, bf16[256,256]{1,0:T(8,128)(2,1)S(1)}, u32[]{:S(2)}, u32[]{:S(2)}) collective-permute-start(bf16[256,256]{1,0:T(8,128)(2,1)S(1)} %get-tuple-element.18), channel_id=1, source_target_pairs={{4,8},{8,4},{12,16},{16,12},{20,24},{24,20},{5,9},{9,5},{13,17},{1... | collective-permute-start | bytes 393224 | tf_op jit(solution)/shard_map/ppermute | solution.py:471
  29.4 0.0 slice-start
  29.4 0.0 copy-start.8
  29.4 0.0 slice-start.1
  29.4 2.9 %conv.1.sums_ref = f32[4,256,256]{2,1,0:T(8,128)S(1)} custom-call(bf16[2,4,288,512]{3,2,1,0:T(8,128)(2,1)S(1)} %get-tuple-element.16.grid_ref, bf16[3,4,512,256]{3,2,1,0:T(8,128)(2,1)S(1)} %fold.1.refs_4_.w_ref), custom_call_target="tpu_custom_call" | custom-call | flops 2684354560 | bytes 6291456 | tf_op jit(solution)/shard_map/conv/pallas_call | solution.py:265
  32.3 0.0 copy-start.3
  32.3 0.0 copy-start.5
  32.3 0.0 copy-start.7
  32.3 0.0 collective-permute-done.3.pair_ref
  32.4 2.2 %collective-permute-done.4.step_ref = bf16[256,256]{1,0:T(8,128)(2,1)S(1)} collective-permute-done((bf16[256,256]{1,0:T(8,128)(2,1)S(1)}, bf16[256,256]{1,0:T(8,128)(2,1)S(1)}, u32[]{:S(2)}, u32[]{:S(2)}) %collective-permute-start.4) | collective-permute-done | bytes 131104 | tf_op jit(solution)/shard_map/ppermute | solution.py:471
  34.6 0.0 copy-done.8
  34.6 0.7 %finish.1 = (bf16[2,512,256]{2,1,0:T(8,128)(2,1)S(1)}, bf16[112,512]{1,0:T(8,128)(2,1)S(1)}, bf16[112,512]{1,0:T(8,128)(2,1)S(1)}, bf16[112,512]{1,0:T(8,128)(2,1)S(1)}, bf16[112,512]{1,0:T(8,128)(2,1)S(1)}) custom-call(s32[8,512]{1,0:T(8,128)S(1)} %get-tuple-element.15.place_ref, f32[4,256,256]{2,1,0:T(8,128)S(1)} %conv.1.sums_ref, ...), custom_call_target="tpu_custom_call" | custom-call | flops 268435456 | bytes 3145728 | tf_op jit(solution)/shard_map/finish/pallas_call | solution.py:310
  35.3 1.3 %collective-permute-start.5 = (bf16[112,512]{1,0:T(8,128)(2,1)S(1)}, bf16[112,512]{1,0:T(8,128)(2,1)S(1)}, u32[]{:S(2)}, u32[]{:S(2)}) collective-permute-start(bf16[112,512]{1,0:T(8,128)(2,1)S(1)} %get-tuple-element.20), channel_id=1, source_target_pairs={{0,2},{1,3},{2,0},{3,1},{4,6},{5,7},{6,4},{7,5},{8,10},{9,11},{10,... | collective-permute-start | bytes 344072 | tf_op jit(solution)/shard_map/ppermute | solution.py:476
  36.6 1.8 %collective-permute-start.6 = (bf16[112,512]{1,0:T(8,128)(2,1)S(1)}, bf16[112,512]{1,0:T(8,128)(2,1)S(1)}, u32[]{:S(2)}, u32[]{:S(2)}) collective-permute-start(bf16[112,512]{1,0:T(8,128)(2,1)S(1)} %get-tuple-element.21), channel_id=1, source_target_pairs={{0,1},{1,0},{2,3},{3,2},{4,5},{5,4},{6,7},{7,6},{8,9},{9,8},{10,11... | collective-permute-start | bytes 344072 | tf_op jit(solution)/shard_map/ppermute | solution.py:476
  38.4 0.1 collective-permute-start.7
  38.5 1.7 %unravel.1 = bf16[4,16,2,32,64]{4,3,2,1,0:T(8,128)(2,1)} custom-call(bf16[2,512,256]{2,1,0:T(8,128)(2,1)S(1)} %get-tuple-element.23.root_ref), custom_call_target="tpu_custom_call" | custom-call | flops 536870912 | bytes 2097152 | tf_op jit(solution)/shard_map/unravel/pallas_call | solution.py:344
  40.2 0.0 collective-permute-done.5.refs_6_
  40.3 0.0 collective-permute-done.6.refs_7_
  40.3 3.2 %collective-permute-done.7.refs_8_ = bf16[112,512]{1,0:T(8,128)(2,1)S(1)} collective-permute-done((bf16[112,512]{1,0:T(8,128)(2,1)S(1)}, bf16[112,512]{1,0:T(8,128)(2,1)S(1)}, u32[]{:S(2)}, u32[]{:S(2)}) %collective-permute-start.7) | collective-permute-done | bytes 114720 | tf_op jit(solution)/shard_map/ppermute | solution.py:476
  43.4 0.0 slice-done
  43.4 0.0 slice-done.1
  43.4 0.0 copy-done.3
  43.4 0.0 copy-done.5
  43.5 0.0 copy-done.7
  43.5 10.4 %fine_out.1 = bf16[112,64,512]{2,1,0:T(8,128)(2,1)} custom-call(s32[112]{0:T(128)S(1)} %copy-done.7, bf16[112,64,512]{2,1,0:T(8,128)(2,1)S(1)} %bitcast.9, bf16[28,64,512]{2,1,0:T(8,128)(2,1)S(1)} %get-tuple-element.13.refs_2_, bf16[256,128]{1,0:T(8,128)(2,1)S(1)} %copy-done.3, bf16[64,128]{1,0:T(8,128)(2,1)S(1)} %bitcast.11, ...), custom_call_target="tpu_custom_call" | custom-call | flops 1879048192 | bytes 14680064 | tf_op jit(solution)/shard_map/fine_out/pallas_call | solution.py:420
  (1 shorter events, 0.0 us)
Async XLA Ops:
  0.6 3.1 %copy-start = (bf16[112,64,512]{2,1,0:T(8,128)(2,1)S(1)}, bf16[112,64,512]{2,1,0:T(8,128)(2,1)}, u32[]{:S(2)}) copy-start(bf16[112,64,512]{2,1,0:T(8,128)(2,1)} %refs_1_.1) | copy-start | bytes 22020100
  3.7 0.7 %copy-start.4 = (bf16[64,128]{1,0:T(8,128)(2,1)S(1)}, bf16[64,128]{1,0:T(8,128)(2,1)}, u32[]{:S(2)}) copy-start(bf16[64,128]{1,0:T(8,128)(2,1)} %w_ref.1) | copy-start | bytes 49156
  4.4 0.7 %copy-start.6 = (s32[112]{0:T(128)S(1)}, s32[112]{0:T(128)}, u32[]{:S(2)}) copy-start(s32[112]{0:T(128)} %refs_0_.1) | copy-start | bytes 1348
  5.1 0.7 %copy-start.9 = (s32[8]{0:T(128)S(1)}, s32[8]{0:T(128)}, u32[]{:S(2)}) copy-start(s32[8]{0:T(128)} %param.11) | copy-start | bytes 100
  5.7 17.1 %copy-start.1 = (bf16[64,256,3,3,3]{1,0,4,3,2:T(8,128)(2,1)S(1)}, bf16[64,256,3,3,3]{1,0,4,3,2:T(8,128)(2,1)}, u32[]{:S(2)}) copy-start(bf16[64,256,3,3,3]{1,0,4,3,2:T(8,128)(2,1)} %param.14) | copy-start | bytes 2654212
  5.7 17.1 %copy-start.2 = (bf16[128,256]{1,0:T(8,128)(2,1)S(1)}, bf16[128,256]{1,0:T(8,128)(2,1)}, u32[]{:S(2)}) copy-start(bf16[128,256]{1,0:T(8,128)(2,1)} %in_ref.1) | copy-start | bytes 196612
  14.7 6.6 %collective-permute-start = (bf16[912,128]{1,0:T(8,128)(2,1)S(1)}, bf16[912,128]{1,0:T(8,128)(2,1)S(1)}, u32[]{:S(2)}, u32[]{:S(2)}) collective-permute-start(bf16[912,128]{1,0:T(8,128)(2,1)S(1)} %get-tuple-element.14.refs_0_), channel_id=1, source_target_pairs={{0,2},{1,3},{2,0},{3,1},{4,6},{5,7},{6,4},{7,5},{8,10},{9,11},{10,... | collective-permute-start | bytes 700424 | tf_op jit(solution)/shard_map/ppermute | solution.py:461
  15.9 7.7 %collective-permute-start.1 = (bf16[912,128]{1,0:T(8,128)(2,1)S(1)}, bf16[912,128]{1,0:T(8,128)(2,1)S(1)}, u32[]{:S(2)}, u32[]{:S(2)}) collective-permute-start(bf16[912,128]{1,0:T(8,128)(2,1)S(1)} %get-tuple-element.14.refs_0_), channel_id=1, source_target_pairs={{0,1},{1,0},{2,3},{3,2},{4,5},{5,4},{6,7},{7,6},{8,9},{9,8},{10,11... | collective-permute-start | bytes 700424 | tf_op jit(solution)/shard_map/ppermute | solution.py:461
  21.3 2.7 %collective-permute-start.2 = (bf16[912,128]{1,0:T(8,128)(2,1)S(1)}, bf16[912,128]{1,0:T(8,128)(2,1)S(1)}, u32[]{:S(2)}, u32[]{:S(2)}) collective-permute-start(bf16[912,128]{1,0:T(8,128)(2,1)S(1)} %collective-permute-done.refs_1_), channel_id=1, source_target_pairs={{0,1},{1,0},{2,3},{3,2},{4,5},{5,4},{6,7},{7,6},{8,9},{9,8},{10,11... | collective-permute-start | bytes 700424 | tf_op jit(solution)/shard_map/ppermute | solution.py:461
  26.1 6.3 %collective-permute-start.3 = (bf16[256,256]{1,0:T(8,128)(2,1)S(1)}, bf16[256,256]{1,0:T(8,128)(2,1)S(1)}, u32[]{:S(2)}, u32[]{:S(2)}) collective-permute-start(bf16[256,256]{1,0:T(8,128)(2,1)S(1)} %get-tuple-element.17), channel_id=1, source_target_pairs={{0,4},{4,0},{8,12},{12,8},{16,20},{20,16},{24,28},{28,24},{1,5},{5... | collective-permute-start | bytes 393224 | tf_op jit(solution)/shard_map/ppermute | solution.py:470
  27.4 7.2 %collective-permute-start.4 = (bf16[256,256]{1,0:T(8,128)(2,1)S(1)}, bf16[256,256]{1,0:T(8,128)(2,1)S(1)}, u32[]{:S(2)}, u32[]{:S(2)}) collective-permute-start(bf16[256,256]{1,0:T(8,128)(2,1)S(1)} %get-tuple-element.18), channel_id=1, source_target_pairs={{4,8},{8,4},{12,16},{16,12},{20,24},{24,20},{5,9},{9,5},{13,17},{1... | collective-permute-start | bytes 393224 | tf_op jit(solution)/shard_map/ppermute | solution.py:471
  29.4 14.0 %slice-start = ((s8[7340032]{0:T(1024)(128)(4,1)}), s8[4194304]{0:T(1024)(128)(4,1)S(1)}, s32[]{:S(2)}) async-start(s8[7340032]{0:T(1024)(128)(4,1)} %bitcast.8), calls=%async_computation | async-start | bytes 8388608
  29.4 5.1 %copy-start.8 = (f32[64]{0:T(128)S(1)}, f32[64]{0:T(128)}, u32[]{:S(2)}) copy-start(f32[64]{0:T(128)} %param.15) | copy-start | bytes 772
  29.4 14.0 %slice-start.1 = ((s8[7340032]{0:T(1024)(128)(4,1)}), s8[3145728]{0:T(1024)(128)(4,1)S(1)}, s32[]{:S(2)}) async-start(s8[7340032]{0:T(1024)(128)(4,1)} %bitcast.8), calls=%async_computation.1 | async-start | bytes 6291456
  32.3 11.1 %copy-start.3 = (bf16[256,128]{1,0:T(8,128)(2,1)S(1)}, bf16[256,128]{1,0:T(8,128)(2,1)}, u32[]{:S(2)}) copy-start(bf16[256,128]{1,0:T(8,128)(2,1)} %refs_3_.1) | copy-start | bytes 196612
  32.3 11.1 %copy-start.5 = (bf16[128,64]{0,1:T(8,128)(2,1)S(1)}, bf16[128,64]{0,1:T(8,128)(2,1)}, u32[]{:S(2)}) copy-start(bf16[128,64]{0,1:T(8,128)(2,1)} %param.17) | copy-start | bytes 49156
  32.3 11.1 %copy-start.7 = (s32[112]{0:T(128)S(1)}, s32[112]{0:T(128)}, u32[]{:S(2)}) copy-start(s32[112]{0:T(128)} %refs_0_.1) | copy-start | bytes 1348
  35.3 5.0 %collective-permute-start.5 = (bf16[112,512]{1,0:T(8,128)(2,1)S(1)}, bf16[112,512]{1,0:T(8,128)(2,1)S(1)}, u32[]{:S(2)}, u32[]{:S(2)}) collective-permute-start(bf16[112,512]{1,0:T(8,128)(2,1)S(1)} %get-tuple-element.20), channel_id=1, source_target_pairs={{0,2},{1,3},{2,0},{3,1},{4,6},{5,7},{6,4},{7,5},{8,10},{9,11},{10,... | collective-permute-start | bytes 344072 | tf_op jit(solution)/shard_map/ppermute | solution.py:476
  36.6 3.7 %collective-permute-start.6 = (bf16[112,512]{1,0:T(8,128)(2,1)S(1)}, bf16[112,512]{1,0:T(8,128)(2,1)S(1)}, u32[]{:S(2)}, u32[]{:S(2)}) collective-permute-start(bf16[112,512]{1,0:T(8,128)(2,1)S(1)} %get-tuple-element.21), channel_id=1, source_target_pairs={{0,1},{1,0},{2,3},{3,2},{4,5},{5,4},{6,7},{7,6},{8,9},{9,8},{10,11... | collective-permute-start | bytes 344072 | tf_op jit(solution)/shard_map/ppermute | solution.py:476
  38.4 5.1 %collective-permute-start.7 = (bf16[112,512]{1,0:T(8,128)(2,1)S(1)}, bf16[112,512]{1,0:T(8,128)(2,1)S(1)}, u32[]{:S(2)}, u32[]{:S(2)}) collective-permute-start(bf16[112,512]{1,0:T(8,128)(2,1)S(1)} %get-tuple-element.22), channel_id=1, source_target_pairs={{0,3},{1,2},{2,1},{3,0},{4,7},{5,6},{6,5},{7,4},{8,11},{9,10},{10,... | collective-permute-start | bytes 344072 | tf_op jit(solution)/shard_map/ppermute | solution.py:476

commit v2 on v1

--- a/solution.py
+++ b/solution.py
@@ -17,11 +17,12 @@
 PLANE = OCT * OCT
 BORDERED = PLANE + 2 * OCT
 SUBS = 8
+AHEAD = 2
 META = 16
 BF16 = jnp.bfloat16
 F32 = jnp.float32
 VMEM = pl.BlockSpec(memory_space=pltpu.VMEM)
-SMEM = pl.BlockSpec(memory_space=pltpu.SMEM)
+ANY = pl.BlockSpec(memory_space=pl.ANY)
 
 
 def params(mib):
@@ -45,80 +46,120 @@
 
 
 def hidden_voxel(fine):
-    z, y, x = fine // (B * B), fine // B % B, fine % B
-    low = z // 2 % 2 * 4 + y // 2 % 2 * 2 + x // 2 % 2
-    high = z // HALF * 4 + y // HALF * 2 + x // HALF
+    edge = B.bit_length() - 1
+    z, y, x = fine >> 2 * edge, fine >> edge & B - 1, fine & B - 1
+    low = (z >> 1 & 1) * 4 + (y >> 1 & 1) * 2 + (x >> 1 & 1)
+    high = (z >> edge - 1) * 4 + (y >> edge - 1) * 2 + (x >> edge - 1)
     return low * SUBS + high
 
 
+def parts_of(total, group, most):
+    return max(n for n in range(group, most + 1, group) if total % n == 0)
+
+
 def fine_in_kernel(
-    child_ref, block_ref, fine_ref, w_ref, hidden_ref, pooled_ref, pool, weights, tops, meta, *, total, padded
+    child_hbm, block_hbm, fine_hbm, w_hbm, hidden_hbm, pooled_ref, fine_ref, hidden_ref,
+    child_ref, block_ref, w_ref, pool, weights, turned, tops, meta, fine_sems, hidden_sems, sems, *, total, padded
 ):
-    step = pl.program_id(0)
-    chunk, width, voxels = fine_ref.shape
+    _, width, voxels = fine_ref.shape
     depth = w_ref.shape[1]
     group = hidden_ref.shape[2] // depth
     cells = voxels // SUBS
-
-    @pl.when(step == 0)
-    def _():
-        hit = hidden_voxel(iota((voxels, cells), 0)) == iota((voxels, cells), 1)
-        pool[...] = jnp.where(hit, 1.0 / SUBS, 0.0).astype(BF16)
-        weights[...] = jnp.zeros_like(weights)
-        for s in range(group):
-            weights[s * width : (s + 1) * width, s * depth : (s + 1) * depth] = w_ref[...]
-        meta[...] = jnp.full_like(meta, -1.0)
-        meta[0:1, 0:total] = (child_ref[...] >> 3).astype(F32)
-        meta[1:2, 0:total] = (child_ref[...] & 7).astype(F32)
-        meta[2:3, 0 : block_ref.shape[1]] = block_ref[...].astype(F32)
-        pooled_ref[SUBS * padded : SUBS * padded + META, :] = meta[...].astype(BF16)
-
-    for j in range(chunk // group):
-        cube = fine_ref[j * group : (j + 1) * group].reshape(group * width, voxels)
+    chunk = total // fine_sems.shape[0]
+    sets = chunk // group
+
+    def fetch(i):
+        part = pl.ds(i * chunk, chunk)
+        return pltpu.make_async_copy(fine_hbm.at[part], fine_ref.at[part], fine_sems.at[i])
+
+    def store(i):
+        part = pl.ds(i * sets, sets)
+        return pltpu.make_async_copy(hidden_ref.at[part], hidden_hbm.at[part], hidden_sems.at[i])
+
+    fetch(0).start()
+    small = [
+        pltpu.make_async_copy(source, target, sems.at[i])
+        for i, (source, target) in enumerate(
+            ((w_hbm, w_ref), (child_hbm, child_ref), (block_hbm, block_ref))
+        )
+    ]
+    for copy in small:
+        copy.start()
+    for i in range(1, min(AHEAD, total // chunk)):
+        fetch(i).start()
+
+    hit = hidden_voxel(iota((voxels, cells), 0)) == iota((voxels, cells), 1)
+    pool[...] = jnp.where(hit, 1.0 / SUBS, 0.0).astype(BF16)
+    weights[...] = jnp.zeros_like(weights)
+    for copy in small:
+        copy.wait()
+    for s in range(group):
+        weights[s * width : (s + 1) * width, s * depth : (s + 1) * depth] = w_ref[...]
+    meta[...] = jnp.full_like(meta, -1.0)
+    meta[0:1, 0:total] = (child_ref[...] >> 3).astype(F32)
+    meta[1:2, 0:total] = (child_ref[...] & 7).astype(F32)
+    meta[2:3, 0 : block_ref.shape[1]] = block_ref[...].astype(F32)
+    pooled_ref[SUBS * padded : SUBS * padded + META, :] = meta[...].astype(BF16)
+
+    for i in range(total // chunk):
+        fetch(i).wait()
+        if i + AHEAD < total // chunk:
+            fetch(i + AHEAD).start()
+        cube = fine_ref[i * chunk : (i + 1) * chunk].reshape(chunk * width, voxels)
         octants = dot(cube, pool[...]).astype(BF16)
-        hidden = jnp.maximum(dot(octants.T, weights[...]), 0.0).astype(BF16)
-        hidden_ref[j] = hidden
-        top = jnp.sum(hidden.astype(F32).reshape(SUBS, SUBS, group * depth), axis=0) * (1.0 / SUBS)
-        for s in range(group):
-            at = (j * group + s) * SUBS
-            tops[at : at + SUBS, :] = top[:, s * depth : (s + 1) * depth]
+        for g in range(sets):
+            at = (i * sets + g) * cells
+            turned[at : at + cells, :] = octants[g * group * width : (g + 1) * group * width].T
+    for i in range(total // chunk):
+        rows = turned[i * sets * cells : (i + 1) * sets * cells, :]
+        hidden = jnp.maximum(dot(rows, weights[...]), 0.0).astype(BF16)
+        hidden_ref[i * sets : (i + 1) * sets] = hidden.reshape(sets, cells, group * depth)
+        store(i).start()
+        cubes = hidden.astype(F32).reshape(sets, SUBS, SUBS, group * depth)
+        top = jnp.sum(cubes, axis=1) * (1.0 / SUBS)
+        for g in range(sets):
+            for s in range(group):
+                at = (i * chunk + g * group + s) * SUBS
+                tops[at : at + SUBS, :] = top[g, :, s * depth : (s + 1) * depth]
     if padded != total:
-        slot = step * chunk + iota(tops.shape, 0) // SUBS
-        tops[...] = jnp.where(slot < total, tops[...], 0.0)
+        tops[total * SUBS :, :] = jnp.zeros(((padded - total) * SUBS, depth), F32)
     for v in range(SUBS):
-        at = pl.multiple_of(v * padded + step * chunk, chunk)
-        pooled_ref[pl.ds(at, chunk), :] = tops[pl.ds(v, chunk, stride=SUBS), :].astype(BF16)
-
-
-def fine_in(fine_feats, fine_child, parent_block, w_parent, chunk, padded):
+        pooled_ref[v * padded : (v + 1) * padded, :] = tops[pl.ds(v, padded, stride=SUBS), :].astype(BF16)
+    for i in range(total // chunk):
+        store(i).wait()
+
+
+def fine_in(fine_feats, fine_child, parent_block, w_parent, padded):
     total, width, voxels = fine_feats.shape
     depth = w_parent.shape[1]
+    pairs = parent_block.shape[0]
     group = 256 // width
     cells = voxels // SUBS
+    chunk = parts_of(total, group, 16)
     return pl.pallas_call(
         functools.partial(fine_in_kernel, total=total, padded=padded),
-        grid=(padded // chunk,),
-        in_specs=[
-            pl.BlockSpec((1, total), lambda i: (0, 0)),
-            pl.BlockSpec((1, parent_block.shape[0]), lambda i: (0, 0)),
-            pl.BlockSpec((chunk, width, voxels), lambda i: (i, 0, 0)),
-            pl.BlockSpec((width, depth), lambda i: (0, 0)),
-        ],
-        out_specs=[
-            pl.BlockSpec((chunk // group, cells, group * depth), lambda i: (i, 0, 0)),
-            pl.BlockSpec((SUBS * padded + META, depth), lambda i: (0, 0)),
-        ],
+        in_specs=[ANY] * 4,
+        out_specs=[ANY, VMEM],
         out_shape=[
-            jax.ShapeDtypeStruct((padded // group, cells, group * depth), BF16),
+            jax.ShapeDtypeStruct((total // group, cells, group * depth), BF16),
             jax.ShapeDtypeStruct((SUBS * padded + META, depth), BF16),
         ],
         scratch_shapes=[
+            pltpu.VMEM(fine_feats.shape, BF16),
+            pltpu.VMEM((total // group, cells, group * depth), BF16),
+            pltpu.VMEM((1, total), jnp.int32),
+            pltpu.VMEM((1, pairs), jnp.int32),
+            pltpu.VMEM(w_parent.shape, BF16),
             pltpu.VMEM((voxels, cells), BF16),
             pltpu.VMEM((group * width, group * depth), BF16),
-            pltpu.VMEM((chunk * SUBS, depth), F32),
+            pltpu.VMEM((total // group * cells, group * width), BF16),
+            pltpu.VMEM((padded * SUBS, depth), F32),
             pltpu.VMEM((META, 128), F32),
+            pltpu.SemaphoreType.DMA((total // chunk,)),
+            pltpu.SemaphoreType.DMA((total // chunk,)),
+            pltpu.SemaphoreType.DMA((3,)),
         ],
-        compiler_params=params(24),
+        compiler_params=params(58),
         cost_estimate=cost(total * width * voxels * 256, 2 * total * width * voxels),
         name="fine_in",
     )(fine_child[None], parent_block[None], fine_feats, w_parent)
@@ -274,12 +315,11 @@
 
 
 def finish_kernel(padded, place_ref, sums_ref, pair_ref, step_ref, bias_ref, *refs):
-    groups = len(refs) - 1
-    root_ref, send_refs = refs[0], refs[1:]
+    groups = len(refs) - 2
+    root_ref, empty_ref, send_refs = refs[0], refs[1], refs[2:]
     lane_count = place_ref.shape[1]
     row = lax.axis_index("row")
     even = row % 2 == 0
-    has_pair_up = even
     last = lax.axis_size("row") - 1
     bias = jnp.concatenate([bias_ref[...]] * 4, axis=1)
     pair = pair_ref[...].astype(F32)
@@ -288,8 +328,8 @@
     below = jnp.where(even, step, pair)
     above = jnp.where(row < last, above, 0.0)
     below = jnp.where(row > 0, below, 0.0)
-    del has_pair_up
     column = place_ref[...].astype(F32).T[:, 0:1].astype(jnp.int32)
+    empty_ref[...] = jnp.broadcast_to(jnp.where(column[0:padded] < 0, -1e30, 0.0), empty_ref.shape)
     hot = jnp.where(column == iota((lane_count, LAYERS * PLANE), 1), 1.0, 0.0).astype(BF16)
     for z in range(RZ_REG):
         total = sums_ref[z] + bias
@@ -310,8 +350,11 @@
     return pl.pallas_call(
         functools.partial(finish_kernel, padded),
         in_specs=[VMEM] * 5,
-        out_specs=[VMEM] * (groups + 1),
-        out_shape=[jax.ShapeDtypeStruct((2, LAYERS * PLANE, wide), BF16)]
+        out_specs=[VMEM] * (groups + 2),
+        out_shape=[
+            jax.ShapeDtypeStruct((2, LAYERS * PLANE, wide), BF16),
+            jax.ShapeDtypeStruct((padded, 128), F32),
+        ]
         + [jax.ShapeDtypeStruct((padded, 2 * wide), BF16)] * groups,
         compiler_params=params(24),
         cost_estimate=cost(1 << 27, 3 << 20),
@@ -319,9 +362,9 @@
     )(places, sums, pair, step, root_bias[None])
 
 
-def unravel_kernel(root_ref, out_ref):
+def unravel_kernel(offsets, root_ref, down_ref, skip_ref, out_ref, lift_ref, weights_ref, spread_ref):
     share = root_ref.shape[2] // 4
-    rows, half = 2 * PLANE // 2, PLANE // 2
+    rows, half = PLANE, PLANE // 2
     x, y = iota((rows, half), 0), iota((rows, half), 1)
     same = x // RXY == y // OCT
     spread = [
@@ -338,108 +381,114 @@
                 line = (dot(spread[0], even) + dot(spread[1], odd)).astype(BF16)
                 out_ref[z, part * lines : (part + 1) * lines, vy] = line.reshape(lines, RXY, share)
 
-
-def unravel(root):
+    me = lax.axis_index("ga")
+    width, depth = skip_ref.shape
+    lift_ref[...] = jnp.zeros_like(lift_ref)
+    for k, offset in enumerate(offsets):
+        own = down_ref[pl.ds(pl.multiple_of((me ^ offset) * share, share), share), :]
+        for vx in range(2):
+            first = (k * 2 + vx) * share
+            lift_ref[first : first + share, vx * depth : (vx + 1) * depth] = own
+    weights_ref[...] = jnp.zeros_like(weights_ref)
+    turned = skip_ref[...].T
+    for s in range(weights_ref.shape[0] // depth):
+        weights_ref[s * depth : (s + 1) * depth, s * width : (s + 1) * width] = turned
+    hit = hidden_voxel(iota(spread_ref.shape, 1)) == iota(spread_ref.shape, 0)
+    spread_ref[...] = jnp.where(hit, 1.0, 0.0).astype(BF16)
+
+
+def unravel(root, w_down, w_skip, offsets, voxels):
     share = root.shape[2] // 4
-    out = pl.pallas_call(
-        unravel_kernel,
-        in_specs=[VMEM],
-        out_specs=VMEM,
-        out_shape=jax.ShapeDtypeStruct((RZ_REG, OCT, 2, RXY, share), BF16),
-        compiler_params=params(16),
+    depth, width = w_skip.shape
+    group = 256 // width
+    out, lift, weights, spread = pl.pallas_call(
+        functools.partial(unravel_kernel, offsets),
+        in_specs=[VMEM] * 3,
+        out_specs=[VMEM] * 4,
+        out_shape=[
+            jax.ShapeDtypeStruct((RZ_REG, OCT, 2, RXY, share), BF16),
+            jax.ShapeDtypeStruct((len(offsets) * 2 * share, 2 * depth), BF16),
+            jax.ShapeDtypeStruct((group * depth, group * width), BF16),
+            jax.ShapeDtypeStruct((voxels // SUBS, voxels), BF16),
+        ],
+        compiler_params=params(12),
         cost_estimate=cost(1 << 28, 2 << 20),
         name="unravel",
-    )(root)
-    return out.reshape(RZ_REG, RXY, RXY, share).transpose(3, 0, 1, 2)
-
-
-def fine_out_kernel(offsets, *refs):
-    groups = len(offsets)
-    child_ref, fine_ref, hidden_ref, down_ref, skip_ref = refs[:5]
-    come_refs = refs[5 : 5 + groups]
-    out_ref = refs[5 + groups]
-    spread, weights, down, lifted = refs[6 + groups :]
-    step = pl.program_id(0)
-    chunk, width, voxels = fine_ref.shape
-    depth = down_ref.shape[1]
+    )(root, w_down, w_skip.T)
+    return out.reshape(RZ_REG, RXY, RXY, share).transpose(3, 0, 1, 2), lift, weights, spread
+
+
+def fine_out_kernel(groups, *refs):
+    fine_ref, hidden_ref, empty_ref, lift_ref, weights_ref, spread_ref = refs[:6]
+    come_refs = refs[6 : 6 + groups]
+    out_hbm, out_ref, lifted, skips, sems = refs[6 + groups :]
+    total, width, voxels = fine_ref.shape
+    depth = lift_ref.shape[1] // 2
     group = hidden_ref.shape[2] // depth
     cells = voxels // SUBS
-    total = child_ref.shape[0]
     share = come_refs[0].shape[1] // SUBS
-    me = lax.axis_index("ga")
-
-    @pl.when(step == 0)
-    def _():
-        hit = hidden_voxel(iota((cells, voxels), 1)) == iota((cells, voxels), 0)
-        spread[...] = jnp.where(hit, 1.0, 0.0).astype(BF16)
-        weights[...] = jnp.zeros_like(weights)
-        turned = skip_ref[...].T
-        for s in range(group):
-            weights[s * depth : (s + 1) * depth, s * width : (s + 1) * width] = turned
-        down[...] = jnp.zeros_like(down)
-        for k, offset in enumerate(offsets):
-            rows = down_ref[pl.ds(pl.multiple_of((me ^ offset) * share, share), share), :]
-            for vx in range(2):
-                first = (k * 2 + vx) * share
-                down[first : first + share, vx * depth : (vx + 1) * depth] = rows
-        for zy in range(4):
-            lanes = slice(zy * 2 * share, (zy + 1) * 2 * share)
-            both = dot(jnp.concatenate([r[:, lanes] for r in come_refs], axis=1), down[...])
-            slots = both.shape[0]
-            for vx in range(2):
-                lifted[pl.ds(zy * 2 + vx, slots, stride=SUBS), :] = both[:, vx * depth : (vx + 1) * depth]
-
-    for j in range(chunk // group):
-        parts = []
-        for s in range(group):
-            slot = step * chunk + j * group + s
-            hidden = hidden_ref[j, :, s * depth : (s + 1) * depth].astype(F32)
-            top = lifted[pl.ds(pl.multiple_of(slot * SUBS, SUBS), SUBS), :]
-            both = jnp.maximum(hidden.reshape(SUBS, SUBS, depth) + top[None], 0.0)
-            live = child_ref[jnp.minimum(slot, total - 1)] >= 0
-            parts.append(jnp.where(live, both, 0.0).reshape(cells, depth).astype(BF16))
-        skip = dot(jnp.concatenate(parts, axis=1), weights[...]).astype(BF16)
-        up = dot(skip.T, spread[...])
-        cube = fine_ref[j * group : (j + 1) * group].reshape(group * width, voxels)
-        out = (cube.astype(F32) + up).astype(BF16)
-        out_ref[j * group : (j + 1) * group] = out.reshape(group, width, voxels)
-
-
-def fine_out(fine_feats, fine_child, hidden, w_down, w_skip, come, offsets, chunk, padded):
+    chunk = total // sems.shape[0]
+    sets = chunk // group
+
+    for zy in range(4):
+        lanes = slice(zy * 2 * share, (zy + 1) * 2 * share)
+        both = dot(jnp.concatenate([r[:, lanes] for r in come_refs], axis=1), lift_ref[...])
+        slots = both.shape[0]
+        for vx in range(2):
+            top = both[:, vx * depth : (vx + 1) * depth] + empty_ref[...]
+            lifted[pl.ds(zy * 2 + vx, slots, stride=SUBS), :] = top
+
+    for i in range(total // chunk):
+        rows = []
+        for g in range(sets):
+            at = i * sets + g
+            tops = [
+                lifted[(at * group + s) * SUBS : (at * group + s + 1) * SUBS, :] for s in range(group)
+            ]
+            hidden = hidden_ref[at].astype(F32).reshape(SUBS, SUBS, group * depth)
+            decoded = jnp.maximum(hidden + jnp.concatenate(tops, axis=1)[None], 0.0)
+            rows.append(decoded.reshape(cells, group * depth).astype(BF16))
+        skip = dot(jnp.concatenate(rows, axis=0), weights_ref[...]).astype(BF16)
+        for g in range(sets):
+            at = (i * sets + g) * group * width
+            skips[at : at + group * width, :] = skip[g * cells : (g + 1) * cells].T
+
+    def send(i):
+        part = pl.ds(i * chunk, chunk)
+        return pltpu.make_async_copy(out_ref.at[part], out_hbm.at[part], sems.at[i])
+
+    for i in range(total // chunk):
+        part = slice(i * chunk, (i + 1) * chunk)
+        up = dot(skips[i * chunk * width : (i + 1) * chunk * width, :], spread_ref[...])
+        cube = fine_ref[part].reshape(chunk * width, voxels)
+        out_ref[part] = (cube.astype(F32) + up).astype(BF16).reshape(chunk, width, voxels)
+        send(i).start()
+    for i in range(total // chunk):
+        send(i).wait()
+
+
+def fine_out(fine_feats, hidden, empty, lift, weights, spread, come):
     total, width, voxels = fine_feats.shape
-    depth = w_down.shape[1]
+    padded = empty.shape[0]
+    depth = lift.shape[1] // 2
     group = 256 // width
-    cells = voxels // SUBS
-    groups = len(offsets)
-    share = come[0].shape[1] // SUBS
-
-    def whole(array):
-        return pl.BlockSpec(array.shape, lambda i: (0,) * array.ndim)
-
-    turned = w_skip.T
+    groups = len(come)
+    chunk = parts_of(total, group, 16)
     return pl.pallas_call(
-        functools.partial(fine_out_kernel, offsets),
-        grid=(padded // chunk,),
-        in_specs=[
-            SMEM,
-            pl.BlockSpec((chunk, width, voxels), lambda i: (i, 0, 0)),
-            pl.BlockSpec((chunk // group, cells, group * depth), lambda i: (i, 0, 0)),
-            whole(w_down),
-            whole(turned),
-        ]
-        + [whole(c) for c in come],
-        out_specs=pl.BlockSpec((chunk, width, voxels), lambda i: (i, 0, 0)),
+        functools.partial(fine_out_kernel, groups),
+        in_specs=[VMEM] * (6 + groups),
+        out_specs=ANY,
         out_shape=jax.ShapeDtypeStruct(fine_feats.shape, BF16),
         scratch_shapes=[
-            pltpu.VMEM((cells, voxels), BF16),
-            pltpu.VMEM((group * depth, group * width), BF16),
-            pltpu.VMEM((groups * 2 * share, 2 * depth), BF16),
+            pltpu.VMEM(fine_feats.shape, BF16),
             pltpu.VMEM((padded * SUBS, depth), F32),
+            pltpu.VMEM((total * width, voxels // SUBS), BF16),
+            pltpu.SemaphoreType.DMA((total // chunk,)),
         ],
-        compiler_params=params(24),
+        compiler_params=params(28),
         cost_estimate=cost(total * width * voxels * 256, 4 * total * width * voxels),
         name="fine_out",
-    )(fine_child, fine_feats, hidden, w_down, turned, *come)
+    )(fine_feats, hidden, empty, lift, weights, spread, *come)
 
 
 def shards(
@@ -448,11 +497,10 @@
     groups = lax.axis_size("ga")
     rows = lax.axis_size("row")
     slots = fine_feats.shape[0]
-    chunk = 16
-    padded = -(-slots // chunk) * chunk
+    padded = -(-slots // META) * META
     pairs = parent_block.shape[0]
 
-    hidden, pooled = fine_in(fine_feats, fine_child, parent_block, w_parent, chunk, padded)
+    hidden, pooled = fine_in(fine_feats, fine_child, parent_block, w_parent, padded)
 
     gathered, offsets = [pooled], [0]
     bit = groups // 2
@@ -470,12 +518,12 @@
     pair = lax.ppermute(pair, "row", pair_swap)
     step = lax.ppermute(step, "row", step_swap)
     sums = conv(grid, folded)
-    root, *sends = finish(places, sums, pair, step, root_bias, groups, padded)
+    root, empty, *sends = finish(places, sums, pair, step, root_bias, groups, padded)
     come = [sends[0]]
     for offset, send in zip(offsets[1:], sends[1:]):
         come.append(lax.ppermute(send, "ga", [(i, i ^ offset) for i in range(groups)]))
-    root_out = unravel(root)
-    fine = fine_out(fine_feats, fine_child, hidden, w_down, w_skip, come, offsets, chunk, padded)
+    root_out, lift, weights, spread = unravel(root, w_down, w_skip, offsets, fine_feats.shape[2])
+    fine = fine_out(fine_feats, hidden, empty, lift, weights, spread, come)
     return (fine, root_out)
 
 

time: 54.1 us -> 42.6 us (0.79)
  Pallas kernels: 27.5 us -> 20.9 us
  local copies, waits for them, and re-layouts: 5.15 us -> 0.05 us
    pallas_call x2, Pallas kernels: 12.1 us -> 6.14 us  [the longest x1 4.35 us: fine_out(): pl.pallas_call(functools.partial(fine_out_kernel, groups), in_specs=[VMEM...]
    unnamed x24 -> x18, local copies, waits for them, and re-layouts: 5.15 us -> 0.05 us
    pallas_call x1, Pallas kernels: 8.91 us -> 8.25 us  [fine_in(): pl.pallas_call(functools.partial(fine_in_kernel, total=total, padded=padd...]
  transfers between devices with their start and end apart: 8 -> 8, of which waited for: 4 -> 4; matrix products, arithmetic and copies ran while one was open for 0% -> 0% of each run, Pallas kernels for 10% -> 13%
where the time goes in v2:
time: 42.6 us; the launch traced here: 42.4 us
  Pallas kernels  20.9 us (49%)
  starting transfers between devices  10.5 us (25%)
  waiting for transfers between devices  10.1 us (24%)
  between operations  0.95 us (2%)
    pallas_call x1, Pallas kernels, fine_in(): pl.pallas_call(functools.partial(fine_in_kernel, total=total, padded=padd...  8.25 us
    ppermute x3, waiting for transfers between devices, shards(): gathered += [lax.ppermute(part, 'ga', swap) for part in gathered]  4.94 us
    pallas_call x1, Pallas kernels, fine_out(): pl.pallas_call(functools.partial(fine_out_kernel, groups), in_specs=[VMEM...  4.35 us
    ppermute x3, starting transfers between devices, shards(): gathered += [lax.ppermute(part, 'ga', swap) for part in gathered]  3.77 us
    ppermute x3, starting transfers between devices, shards(): lax.ppermute(send, 'ga', [(i, i ^ offset) for i in range(groups)])  3.24 us
    ppermute x3, waiting for transfers between devices, shards(): lax.ppermute(send, 'ga', [(i, i ^ offset) for i in range(groups)])  3.12 us
    pallas_call x1, Pallas kernels, conv(): pl.pallas_call(conv_kernel, in_specs=[VMEM, VMEM], out_specs=VMEM, out_sh...  2.86 us
    ppermute x1, starting transfers between devices, shards(): step = lax.ppermute(step, 'row', step_swap)  2.19 us
  transfers between devices with their start and end apart: 8, of which 4 were waited for; matrix products, arithmetic and copies ran while one was open for 0% of the time, Pallas kernels for 13%

profile of v2, /device:TPU:25, one launch (start us, length us, event | category | flops | bytes accessed | tf_op | source)
XLA Modules:
  0.0 42.4 jit_solution(8518059949880441738)
XLA Ops:
  0.6 0.0 copy-start.1
  0.6 0.0 copy-start.3
  0.7 8.3 %fine_in.1 = (bf16[28,64,512]{2,1,0:T(8,128)(2,1)}, bf16[912,128]{1,0:T(8,128)(2,1)}) custom-call(s32[1,112]{1,0:T(1,128)} %bitcast.13, s32[1,8]{1,0:T(1,128)} %bitcast.14, bf16[112,64,512]{2,1,0:T(8,128)(2,1)} %refs_0_.1, bf16[64,128]{1,0:T(8,128)(2,1)} %w_hbm.1), custom_call_target="tpu_custom_call" | custom-call | flops 1879048192 | bytes 7340032 | tf_op jit(solution)/shard_map/fine_in/pallas_call | solution.py:139
  8.9 0.0 copy-start.2
  8.9 1.3 %collective-permute-start = (bf16[912,128]{1,0:T(8,128)(2,1)}, bf16[912,128]{1,0:T(8,128)(2,1)S(1)}, u32[]{:S(2)}, u32[]{:S(2)}) collective-permute-start(bf16[912,128]{1,0:T(8,128)(2,1)} %get-tuple-element.19.refs_0_), channel_id=1, source_target_pairs={{0,2},{1,3},{2,0},{3,1},{4,6},{5,7},{6,4},{7,5},{8,10},{9,11},{10,... | collective-permute-start | bytes 700424 | tf_op jit(solution)/shard_map/ppermute | solution.py:509
  10.2 1.0 %collective-permute-start.1 = (bf16[912,128]{1,0:T(8,128)(2,1)}, bf16[912,128]{1,0:T(8,128)(2,1)S(1)}, u32[]{:S(2)}, u32[]{:S(2)}) collective-permute-start(bf16[912,128]{1,0:T(8,128)(2,1)} %get-tuple-element.19.refs_0_), channel_id=1, source_target_pairs={{0,1},{1,0},{2,3},{3,2},{4,5},{5,4},{6,7},{7,6},{8,9},{9,8},{10,11... | collective-permute-start | bytes 700424 | tf_op jit(solution)/shard_map/ppermute | solution.py:509
  11.2 4.6 %collective-permute-done.refs_1_ = bf16[912,128]{1,0:T(8,128)(2,1)S(1)} collective-permute-done((bf16[912,128]{1,0:T(8,128)(2,1)}, bf16[912,128]{1,0:T(8,128)(2,1)S(1)}, u32[]{:S(2)}, u32[]{:S(2)}) %collective-permute-start) | collective-permute-done | bytes 233504 | tf_op jit(solution)/shard_map/ppermute | solution.py:509
  15.8 1.5 %collective-permute-start.2 = (bf16[912,128]{1,0:T(8,128)(2,1)S(1)}, bf16[912,128]{1,0:T(8,128)(2,1)S(1)}, u32[]{:S(2)}, u32[]{:S(2)}) collective-permute-start(bf16[912,128]{1,0:T(8,128)(2,1)S(1)} %collective-permute-done.refs_1_), channel_id=1, source_target_pairs={{0,1},{1,0},{2,3},{3,2},{4,5},{5,4},{6,7},{7,6},{8,9},{9,8},{10,11... | collective-permute-start | bytes 700424 | tf_op jit(solution)/shard_map/ppermute | solution.py:509
  17.3 0.0 copy-done.1
  17.3 0.0 copy-done.3
  17.3 0.8 %fold.1.refs_4_.w_ref = bf16[3,4,512,256]{3,2,1,0:T(8,128)(2,1)S(1)} custom-call(bf16[3,3,3,64,256]{4,3,2,1,0:T(8,128)(2,1)S(1)} %bitcast.10, bf16[128,256]{1,0:T(8,128)(2,1)S(1)} %copy-done.3), custom_call_target="tpu_custom_call" | custom-call | flops 301989888 | bytes 6291456 | tf_op jit(solution)/shard_map/fold/pallas_call | solution.py:189
  18.1 0.0 collective-permute-done.1.refs_2_
  18.1 0.3 collective-permute-done.2.refs_3_
  18.4 0.0 copy-done.2
  18.4 2.1 %place.1 = (bf16[2,4,288,512]{3,2,1,0:T(8,128)(2,1)S(1)}, s32[8,512]{1,0:T(8,128)S(1)}, bf16[256,256]{1,0:T(8,128)(2,1)S(1)}, bf16[256,256]{1,0:T(8,128)(2,1)S(1)}) custom-call(bf16[912,128]{1,0:T(8,128)(2,1)S(1)} %copy-done.2, bf16[912,128]{1,0:T(8,128)(2,1)S(1)} %collective-permute-done.refs_1_, bf16[912,128]{1,0:T(8,128)(2,1)S(1)} %collective-permute-done.1.refs_2_, ...), custom_call_target="tpu_custom_call" | custom-call | flops 1073741824 | bytes 6291456 | tf_op jit(solution)/shard_map/place/pallas_call | solution.py:274
  20.6 1.3 %collective-permute-start.3 = (bf16[256,256]{1,0:T(8,128)(2,1)S(1)}, bf16[256,256]{1,0:T(8,128)(2,1)S(1)}, u32[]{:S(2)}, u32[]{:S(2)}) collective-permute-start(bf16[256,256]{1,0:T(8,128)(2,1)S(1)} %get-tuple-element.22), channel_id=1, source_target_pairs={{0,4},{4,0},{8,12},{12,8},{16,20},{20,16},{24,28},{28,24},{1,5},{5... | collective-permute-start | bytes 393224 | tf_op jit(solution)/shard_map/ppermute | solution.py:518
  21.9 2.2 %collective-permute-start.4 = (bf16[256,256]{1,0:T(8,128)(2,1)S(1)}, bf16[256,256]{1,0:T(8,128)(2,1)S(1)}, u32[]{:S(2)}, u32[]{:S(2)}) collective-permute-start(bf16[256,256]{1,0:T(8,128)(2,1)S(1)} %get-tuple-element.23), channel_id=1, source_target_pairs={{4,8},{8,4},{12,16},{16,12},{20,24},{24,20},{5,9},{9,5},{13,17},{1... | collective-permute-start | bytes 393224 | tf_op jit(solution)/shard_map/ppermute | solution.py:519
  24.1 0.0 slice-start
  24.1 0.0 copy-start.4
  24.1 0.0 copy-start.5
  24.1 0.0 copy-start.6
  24.1 0.0 slice-start.1
  24.1 2.9 %conv.1.sums_ref = f32[4,256,256]{2,1,0:T(8,128)S(1)} custom-call(bf16[2,4,288,512]{3,2,1,0:T(8,128)(2,1)S(1)} %get-tuple-element.21.grid_ref, bf16[3,4,512,256]{3,2,1,0:T(8,128)(2,1)S(1)} %fold.1.refs_4_.w_ref), custom_call_target="tpu_custom_call" | custom-call | flops 2684354560 | bytes 6291456 | tf_op jit(solution)/shard_map/conv/pallas_call | solution.py:306
  27.0 0.0 copy-start
  27.0 0.0 collective-permute-done.3.pair_ref
  27.0 2.0 %collective-permute-done.4.step_ref = bf16[256,256]{1,0:T(8,128)(2,1)S(1)} collective-permute-done((bf16[256,256]{1,0:T(8,128)(2,1)S(1)}, bf16[256,256]{1,0:T(8,128)(2,1)S(1)}, u32[]{:S(2)}, u32[]{:S(2)}) %collective-permute-start.4) | collective-permute-done | bytes 131104 | tf_op jit(solution)/shard_map/ppermute | solution.py:519
  29.0 0.0 copy-done.4
  29.0 0.7 %finish.1 = (bf16[2,512,256]{2,1,0:T(8,128)(2,1)S(1)}, f32[112,128]{1,0:T(8,128)S(1)}, bf16[112,512]{1,0:T(8,128)(2,1)S(1)}, bf16[112,512]{1,0:T(8,128)(2,1)S(1)...) custom-call(s32[8,512]{1,0:T(8,128)S(1)} %get-tuple-element.20.place_ref, f32[4,256,256]{2,1,0:T(8,128)S(1)} %conv.1.sums_ref, ...), custom_call_target="tpu_custom_call" | custom-call | flops 268435456 | bytes 3145728 | tf_op jit(solution)/shard_map/finish/pallas_call | solution.py:350
  29.7 1.3 %collective-permute-start.5 = (bf16[112,512]{1,0:T(8,128)(2,1)S(1)}, bf16[112,512]{1,0:T(8,128)(2,1)S(1)}, u32[]{:S(2)}, u32[]{:S(2)}) collective-permute-start(bf16[112,512]{1,0:T(8,128)(2,1)S(1)} %get-tuple-element.30), channel_id=1, source_target_pairs={{0,2},{1,3},{2,0},{3,1},{4,6},{5,7},{6,4},{7,5},{8,10},{9,11},{10,... | collective-permute-start | bytes 344072 | tf_op jit(solution)/shard_map/ppermute | solution.py:524
  31.0 1.8 %collective-permute-start.6 = (bf16[112,512]{1,0:T(8,128)(2,1)S(1)}, bf16[112,512]{1,0:T(8,128)(2,1)S(1)}, u32[]{:S(2)}, u32[]{:S(2)}) collective-permute-start(bf16[112,512]{1,0:T(8,128)(2,1)S(1)} %get-tuple-element.31), channel_id=1, source_target_pairs={{0,1},{1,0},{2,3},{3,2},{4,5},{5,4},{6,7},{7,6},{8,9},{9,8},{10,11... | collective-permute-start | bytes 344072 | tf_op jit(solution)/shard_map/ppermute | solution.py:524
  32.8 0.1 collective-permute-start.7
  33.0 0.0 copy-done.5
  33.0 0.0 copy-done.6
  33.0 1.8 %unravel.1 = (bf16[4,16,2,32,64]{4,3,2,1,0:T(8,128)(2,1)}, bf16[512,256]{1,0:T(8,128)(2,1)S(1)}, bf16[512,256]{1,0:T(8,128)(2,1)S(1)}, bf16[64,512]{1,0:T(8,128)(2,1)S(1)}) custom-call(bf16[2,512,256]{2,1,0:T(8,128)(2,1)S(1)} %get-tuple-element.25.root_ref, bf16[256,128]{1,0:T(8,128)(2,1)S(1)} %copy-done.5, bf16[64,128]{1,0:T(8,128)(2,1)S(1)} %bitcast.12), custom_call_target="tpu_custom_call" | custom-call | flops 536870912 | bytes 2097152 | tf_op jit(solution)/shard_map/unravel/pallas_call | solution.py:404
  34.8 0.0 collective-permute-done.5.refs_7_
  34.8 0.0 collective-permute-done.6.refs_8_
  34.8 3.1 %collective-permute-done.7.refs_9_ = bf16[112,512]{1,0:T(8,128)(2,1)S(1)} collective-permute-done((bf16[112,512]{1,0:T(8,128)(2,1)S(1)}, bf16[112,512]{1,0:T(8,128)(2,1)S(1)}, u32[]{:S(2)}, u32[]{:S(2)}) %collective-permute-start.7) | collective-permute-done | bytes 114720 | tf_op jit(solution)/shard_map/ppermute | solution.py:524
  37.9 0.0 slice-done
  37.9 0.0 slice-done.1
  37.9 0.0 copy-done
  37.9 4.4 %fine_out.1 = bf16[112,64,512]{2,1,0:T(8,128)(2,1)} custom-call(bf16[112,64,512]{2,1,0:T(8,128)(2,1)S(1)} %bitcast.9, bf16[28,64,512]{2,1,0:T(8,128)(2,1)S(1)} %copy-done, f32[112,128]{1,0:T(8,128)S(1)} %get-tuple-element.24.refs_2_, bf16[512,256]{1,0:T(8,128)(2,1)S(1)} %get-tuple-element.26.refs_3_, bf16[512,256]{1,0:T(8,128)(2,1)S(1)} %get-tuple-element.27.refs_4_, ...), custom_call_target="tpu_custom_call" | custom-call | flops 1879048192 | bytes 14680064 | tf_op jit(solution)/shard_map/fine_out/pallas_call | solution.py:477
  (1 shorter events, 0.0 us)
Async XLA Ops:
  0.6 16.7 %copy-start.1 = (bf16[64,256,3,3,3]{1,0,4,3,2:T(8,128)(2,1)S(1)}, bf16[64,256,3,3,3]{1,0,4,3,2:T(8,128)(2,1)}, u32[]{:S(2)}) copy-start(bf16[64,256,3,3,3]{1,0,4,3,2:T(8,128)(2,1)} %param.14) | copy-start | bytes 2654212
  0.6 16.7 %copy-start.3 = (bf16[128,256]{1,0:T(8,128)(2,1)S(1)}, bf16[128,256]{1,0:T(8,128)(2,1)}, u32[]{:S(2)}) copy-start(bf16[128,256]{1,0:T(8,128)(2,1)} %in_ref.1) | copy-start | bytes 196612
  8.9 9.5 %copy-start.2 = (bf16[912,128]{1,0:T(8,128)(2,1)S(1)}, bf16[912,128]{1,0:T(8,128)(2,1)}, u32[]{:S(2)}) copy-start(bf16[912,128]{1,0:T(8,128)(2,1)} %get-tuple-element.19.refs_0_) | copy-start | bytes 700420
  8.9 6.8 %collective-permute-start = (bf16[912,128]{1,0:T(8,128)(2,1)}, bf16[912,128]{1,0:T(8,128)(2,1)S(1)}, u32[]{:S(2)}, u32[]{:S(2)}) collective-permute-start(bf16[912,128]{1,0:T(8,128)(2,1)} %get-tuple-element.19.refs_0_), channel_id=1, source_target_pairs={{0,2},{1,3},{2,0},{3,1},{4,6},{5,7},{6,4},{7,5},{8,10},{9,11},{10,... | collective-permute-start | bytes 700424 | tf_op jit(solution)/shard_map/ppermute | solution.py:509
  10.2 7.9 %collective-permute-start.1 = (bf16[912,128]{1,0:T(8,128)(2,1)}, bf16[912,128]{1,0:T(8,128)(2,1)S(1)}, u32[]{:S(2)}, u32[]{:S(2)}) collective-permute-start(bf16[912,128]{1,0:T(8,128)(2,1)} %get-tuple-element.19.refs_0_), channel_id=1, source_target_pairs={{0,1},{1,0},{2,3},{3,2},{4,5},{5,4},{6,7},{7,6},{8,9},{9,8},{10,11... | collective-permute-start | bytes 700424 | tf_op jit(solution)/shard_map/ppermute | solution.py:509
  15.8 2.7 %collective-permute-start.2 = (bf16[912,128]{1,0:T(8,128)(2,1)S(1)}, bf16[912,128]{1,0:T(8,128)(2,1)S(1)}, u32[]{:S(2)}, u32[]{:S(2)}) collective-permute-start(bf16[912,128]{1,0:T(8,128)(2,1)S(1)} %collective-permute-done.refs_1_), channel_id=1, source_target_pairs={{0,1},{1,0},{2,3},{3,2},{4,5},{5,4},{6,7},{7,6},{8,9},{9,8},{10,11... | collective-permute-start | bytes 700424 | tf_op jit(solution)/shard_map/ppermute | solution.py:509
  20.6 6.4 %collective-permute-start.3 = (bf16[256,256]{1,0:T(8,128)(2,1)S(1)}, bf16[256,256]{1,0:T(8,128)(2,1)S(1)}, u32[]{:S(2)}, u32[]{:S(2)}) collective-permute-start(bf16[256,256]{1,0:T(8,128)(2,1)S(1)} %get-tuple-element.22), channel_id=1, source_target_pairs={{0,4},{4,0},{8,12},{12,8},{16,20},{20,16},{24,28},{28,24},{1,5},{5... | collective-permute-start | bytes 393224 | tf_op jit(solution)/shard_map/ppermute | solution.py:518
  21.9 7.2 %collective-permute-start.4 = (bf16[256,256]{1,0:T(8,128)(2,1)S(1)}, bf16[256,256]{1,0:T(8,128)(2,1)S(1)}, u32[]{:S(2)}, u32[]{:S(2)}) collective-permute-start(bf16[256,256]{1,0:T(8,128)(2,1)S(1)} %get-tuple-element.23), channel_id=1, source_target_pairs={{4,8},{8,4},{12,16},{16,12},{20,24},{24,20},{5,9},{9,5},{13,17},{1... | collective-permute-start | bytes 393224 | tf_op jit(solution)/shard_map/ppermute | solution.py:519
  24.1 13.9 %slice-start = ((s8[7340032]{0:T(1024)(128)(4,1)}), s8[4194304]{0:T(1024)(128)(4,1)S(1)}, s32[]{:S(2)}) async-start(s8[7340032]{0:T(1024)(128)(4,1)} %bitcast.8), calls=%async_computation | async-start | bytes 8388608
  24.1 5.0 %copy-start.4 = (f32[64]{0:T(128)S(1)}, f32[64]{0:T(128)}, u32[]{:S(2)}) copy-start(f32[64]{0:T(128)} %param.15) | copy-start | bytes 772
  24.1 8.9 %copy-start.5 = (bf16[256,128]{1,0:T(8,128)(2,1)S(1)}, bf16[256,128]{1,0:T(8,128)(2,1)}, u32[]{:S(2)}) copy-start(bf16[256,128]{1,0:T(8,128)(2,1)} %down_ref.1) | copy-start | bytes 196612
  24.1 8.9 %copy-start.6 = (bf16[128,64]{0,1:T(8,128)(2,1)S(1)}, bf16[128,64]{0,1:T(8,128)(2,1)}, u32[]{:S(2)}) copy-start(bf16[128,64]{0,1:T(8,128)(2,1)} %param.17) | copy-start | bytes 49156
  24.1 13.8 %slice-start.1 = ((s8[7340032]{0:T(1024)(128)(4,1)}), s8[3145728]{0:T(1024)(128)(4,1)S(1)}, s32[]{:S(2)}) async-start(s8[7340032]{0:T(1024)(128)(4,1)} %bitcast.8), calls=%async_computation.1 | async-start | bytes 6291456
  27.0 10.9 %copy-start = (bf16[28,64,512]{2,1,0:T(8,128)(2,1)S(1)}, bf16[28,64,512]{2,1,0:T(8,128)(2,1)}, u32[]{:S(2)}) copy-start(bf16[28,64,512]{2,1,0:T(8,128)(2,1)} %get-tuple-element.18.refs_1_) | copy-start | bytes 5505028
  29.7 5.0 %collective-permute-start.5 = (bf16[112,512]{1,0:T(8,128)(2,1)S(1)}, bf16[112,512]{1,0:T(8,128)(2,1)S(1)}, u32[]{:S(2)}, u32[]{:S(2)}) collective-permute-start(bf16[112,512]{1,0:T(8,128)(2,1)S(1)} %get-tuple-element.30), channel_id=1, source_target_pairs={{0,2},{1,3},{2,0},{3,1},{4,6},{5,7},{6,4},{7,5},{8,10},{9,11},{10,... | collective-permute-start | bytes 344072 | tf_op jit(solution)/shard_map/ppermute | solution.py:524
  31.0 3.8 %collective-permute-start.6 = (bf16[112,512]{1,0:T(8,128)(2,1)S(1)}, bf16[112,512]{1,0:T(8,128)(2,1)S(1)}, u32[]{:S(2)}, u32[]{:S(2)}) collective-permute-start(bf16[112,512]{1,0:T(8,128)(2,1)S(1)} %get-tuple-element.31), channel_id=1, source_target_pairs={{0,1},{1,0},{2,3},{3,2},{4,5},{5,4},{6,7},{7,6},{8,9},{9,8},{10,11... | collective-permute-start | bytes 344072 | tf_op jit(solution)/shard_map/ppermute | solution.py:524
  32.8 5.1 %collective-permute-start.7 = (bf16[112,512]{1,0:T(8,128)(2,1)S(1)}, bf16[112,512]{1,0:T(8,128)(2,1)S(1)}, u32[]{:S(2)}, u32[]{:S(2)}) collective-permute-start(bf16[112,512]{1,0:T(8,128)(2,1)S(1)} %get-tuple-element.32), channel_id=1, source_target_pairs={{0,3},{1,2},{2,1},{3,0},{4,7},{5,6},{6,5},{7,4},{8,11},{9,10},{10,... | collective-permute-start | bytes 344072 | tf_op jit(solution)/shard_map/ppermute | solution.py:524

commit v3 on v2

--- a/solution.py
+++ b/solution.py
@@ -17,7 +17,6 @@
 PLANE = OCT * OCT
 BORDERED = PLANE + 2 * OCT
 SUBS = 8
-AHEAD = 2
 META = 16
 BF16 = jnp.bfloat16
 F32 = jnp.float32
@@ -53,17 +52,31 @@
     return low * SUBS + high
 
 
+def run_bounds(count):
+    cuts = [0]
+    while cuts[-1] < count:
+        cuts.append(min(2 * cuts[-1] + 1, count))
+    return list(zip(cuts, cuts[1:]))
+
+
+def repeat_blocks(ref, block):
+    rows, columns = block.shape
+    ref[...] = jnp.zeros_like(ref)
+    for s in range(ref.shape[0] // rows):
+        ref[s * rows : (s + 1) * rows, s * columns : (s + 1) * columns] = block
+
+
 def parts_of(total, group, most):
     return max(n for n in range(group, most + 1, group) if total % n == 0)
 
 
 def fine_in_kernel(
-    child_hbm, block_hbm, fine_hbm, w_hbm, hidden_hbm, pooled_ref, fine_ref, hidden_ref,
-    child_ref, block_ref, w_ref, pool, weights, turned, tops, meta, fine_sems, hidden_sems, sems, *, total, padded
+    child_hbm, block_hbm, fine_hbm, w_hbm, turned_hbm, pooled_ref,
+    fine_ref, child_ref, block_ref, w_ref, pool, weights, turned, tops, meta, fine_sems, turned_sems, sems, *, total, padded
 ):
     _, width, voxels = fine_ref.shape
     depth = w_ref.shape[1]
-    group = hidden_ref.shape[2] // depth
+    group = turned.shape[1] // width
     cells = voxels // SUBS
     chunk = total // fine_sems.shape[0]
     sets = chunk // group
@@ -72,11 +85,11 @@
         part = pl.ds(i * chunk, chunk)
         return pltpu.make_async_copy(fine_hbm.at[part], fine_ref.at[part], fine_sems.at[i])
 
-    def store(i):
-        part = pl.ds(i * sets, sets)
-        return pltpu.make_async_copy(hidden_ref.at[part], hidden_hbm.at[part], hidden_sems.at[i])
-
-    fetch(0).start()
+    def store(low, high):
+        part = pl.ds(low * sets * cells, (high - low) * sets * cells)
+        return pltpu.make_async_copy(turned.at[part], turned_hbm.at[part], turned_sems.at[low])
+
+    fetch(0).start(priority=1)
     small = [
         pltpu.make_async_copy(source, target, sems.at[i])
         for i, (source, target) in enumerate(
@@ -85,48 +98,45 @@
     ]
     for copy in small:
         copy.start()
-    for i in range(1, min(AHEAD, total // chunk)):
-        fetch(i).start()
+    for i in range(1, total // chunk):
+        fetch(i).start(priority=1)
 
     hit = hidden_voxel(iota((voxels, cells), 0)) == iota((voxels, cells), 1)
     pool[...] = jnp.where(hit, 1.0 / SUBS, 0.0).astype(BF16)
-    weights[...] = jnp.zeros_like(weights)
     for copy in small:
         copy.wait()
-    for s in range(group):
-        weights[s * width : (s + 1) * width, s * depth : (s + 1) * depth] = w_ref[...]
+    repeat_blocks(weights, w_ref[...])
     meta[...] = jnp.full_like(meta, -1.0)
     meta[0:1, 0:total] = (child_ref[...] >> 3).astype(F32)
     meta[1:2, 0:total] = (child_ref[...] & 7).astype(F32)
     meta[2:3, 0 : block_ref.shape[1]] = block_ref[...].astype(F32)
     pooled_ref[SUBS * padded : SUBS * padded + META, :] = meta[...].astype(BF16)
 
-    for i in range(total // chunk):
-        fetch(i).wait()
-        if i + AHEAD < total // chunk:
-            fetch(i + AHEAD).start()
-        cube = fine_ref[i * chunk : (i + 1) * chunk].reshape(chunk * width, voxels)
+    runs = run_bounds(total // chunk)
+    for low, high in runs:
+        for i in range(low, high):
+            fetch(i).wait()
+        cube = fine_ref[low * chunk : high * chunk].reshape((high - low) * chunk * width, voxels)
         octants = dot(cube, pool[...]).astype(BF16)
-        for g in range(sets):
-            at = (i * sets + g) * cells
+        for g in range((high - low) * sets):
+            at = (low * sets + g) * cells
             turned[at : at + cells, :] = octants[g * group * width : (g + 1) * group * width].T
-    for i in range(total // chunk):
-        rows = turned[i * sets * cells : (i + 1) * sets * cells, :]
+        store(low, high).start()
+    for low, high in runs:
+        rows = turned[low * sets * cells : high * sets * cells, :]
         hidden = jnp.maximum(dot(rows, weights[...]), 0.0).astype(BF16)
-        hidden_ref[i * sets : (i + 1) * sets] = hidden.reshape(sets, cells, group * depth)
-        store(i).start()
-        cubes = hidden.astype(F32).reshape(sets, SUBS, SUBS, group * depth)
+        cubes = hidden.astype(F32).reshape((high - low) * sets, SUBS, SUBS, group * depth)
         top = jnp.sum(cubes, axis=1) * (1.0 / SUBS)
-        for g in range(sets):
+        for g in range((high - low) * sets):
             for s in range(group):
-                at = (i * chunk + g * group + s) * SUBS
+                at = (low * chunk + g * group + s) * SUBS
                 tops[at : at + SUBS, :] = top[g, :, s * depth : (s + 1) * depth]
     if padded != total:
         tops[total * SUBS :, :] = jnp.zeros(((padded - total) * SUBS, depth), F32)
     for v in range(SUBS):
         pooled_ref[v * padded : (v + 1) * padded, :] = tops[pl.ds(v, padded, stride=SUBS), :].astype(BF16)
-    for i in range(total // chunk):
-        store(i).wait()
+    for low, high in runs:
+        store(low, high).wait()
 
 
 def fine_in(fine_feats, fine_child, parent_block, w_parent, padded):
@@ -141,12 +151,11 @@
         in_specs=[ANY] * 4,
         out_specs=[ANY, VMEM],
         out_shape=[
-            jax.ShapeDtypeStruct((total // group, cells, group * depth), BF16),
+            jax.ShapeDtypeStruct((total // group * cells, group * width), BF16),
             jax.ShapeDtypeStruct((SUBS * padded + META, depth), BF16),
         ],
         scratch_shapes=[
             pltpu.VMEM(fine_feats.shape, BF16),
-            pltpu.VMEM((total // group, cells, group * depth), BF16),
             pltpu.VMEM((1, total), jnp.int32),
             pltpu.VMEM((1, pairs), jnp.int32),
             pltpu.VMEM(w_parent.shape, BF16),
@@ -163,6 +172,26 @@
         cost_estimate=cost(total * width * voxels * 256, 2 * total * width * voxels),
         name="fine_in",
     )(fine_child[None], parent_block[None], fine_feats, w_parent)
+
+
+def hide_kernel(turned_ref, w_ref, hidden_ref, weights):
+    repeat_blocks(weights, w_ref[...])
+    hidden_ref[...] = jnp.maximum(dot(turned_ref[...], weights[...]), 0.0).astype(BF16)
+
+
+def hide(turned, w_parent):
+    width, depth = w_parent.shape
+    rows, wide = turned.shape
+    return pl.pallas_call(
+        hide_kernel,
+        in_specs=[VMEM] * 2,
+        out_specs=VMEM,
+        out_shape=jax.ShapeDtypeStruct((rows, wide // width * depth), BF16),
+        scratch_shapes=[pltpu.VMEM((wide, wide // width * depth), BF16)],
+        compiler_params=params(12),
+        cost_estimate=cost(rows * wide * 512, rows * wide * 6),
+        name="hide",
+    )(turned, w_parent)
 
 
 def fold_kernel(w_ref, in_ref, out_ref):
@@ -314,8 +343,7 @@
     )(grid, folded)
 
 
-def finish_kernel(padded, place_ref, sums_ref, pair_ref, step_ref, bias_ref, *refs):
-    groups = len(refs) - 2
+def finish_kernel(padded, order, place_ref, sums_ref, pair_ref, step_ref, bias_ref, *refs):
     root_ref, empty_ref, send_refs = refs[0], refs[1], refs[2:]
     lane_count = place_ref.shape[1]
     row = lax.axis_index("row")
@@ -341,14 +369,15 @@
     wide = root_ref.shape[2]
     for vz in range(2):
         picked = dot(hot, root_ref[vz]).astype(BF16)
-        for k in range(groups):
-            send_refs[k][:, vz * wide : (vz + 1) * wide] = picked[k * 128 : k * 128 + padded]
-
-
-def finish(places, sums, pair, step, root_bias, groups, padded):
+        for send_ref, k in zip(send_refs, order):
+            send_ref[:, vz * wide : (vz + 1) * wide] = picked[k * 128 : k * 128 + padded]
+
+
+def finish(places, sums, pair, step, root_bias, order, padded):
     wide = sums.shape[2]
-    return pl.pallas_call(
-        functools.partial(finish_kernel, padded),
+    groups = len(order)
+    return pl.pallas_call(
+        functools.partial(finish_kernel, padded, order),
         in_specs=[VMEM] * 5,
         out_specs=[VMEM] * (groups + 2),
         out_shape=[
@@ -389,10 +418,7 @@
         for vx in range(2):
             first = (k * 2 + vx) * share
             lift_ref[first : first + share, vx * depth : (vx + 1) * depth] = own
-    weights_ref[...] = jnp.zeros_like(weights_ref)
-    turned = skip_ref[...].T
-    for s in range(weights_ref.shape[0] // depth):
-        weights_ref[s * depth : (s + 1) * depth, s * width : (s + 1) * width] = turned
+    repeat_blocks(weights_ref, skip_ref[...].T)
     hit = hidden_voxel(iota(spread_ref.shape, 1)) == iota(spread_ref.shape, 0)
     spread_ref[...] = jnp.where(hit, 1.0, 0.0).astype(BF16)
 
@@ -424,7 +450,7 @@
     out_hbm, out_ref, lifted, skips, sems = refs[6 + groups :]
     total, width, voxels = fine_ref.shape
     depth = lift_ref.shape[1] // 2
-    group = hidden_ref.shape[2] // depth
+    group = hidden_ref.shape[1] // depth
     cells = voxels // SUBS
     share = come_refs[0].shape[1] // SUBS
     chunk = total // sems.shape[0]
@@ -445,7 +471,7 @@
             tops = [
                 lifted[(at * group + s) * SUBS : (at * group + s + 1) * SUBS, :] for s in range(group)
             ]
-            hidden = hidden_ref[at].astype(F32).reshape(SUBS, SUBS, group * depth)
+            hidden = hidden_ref[at * cells : (at + 1) * cells, :].astype(F32).reshape(SUBS, SUBS, group * depth)
             decoded = jnp.maximum(hidden + jnp.concatenate(tops, axis=1)[None], 0.0)
             rows.append(decoded.reshape(cells, group * depth).astype(BF16))
         skip = dot(jnp.concatenate(rows, axis=0), weights_ref[...]).astype(BF16)
@@ -500,7 +526,10 @@
     padded = -(-slots // META) * META
     pairs = parent_block.shape[0]
 
-    hidden, pooled = fine_in(fine_feats, fine_child, parent_block, w_parent, padded)
+    turned, pooled = fine_in(fine_feats, fine_child, parent_block, w_parent, padded)
+
+    hidden = hide(turned, w_parent)
+    folded = fold(w_root, w_root_in)
 
     gathered, offsets = [pooled], [0]
     bit = groups // 2
@@ -508,21 +537,25 @@
         swap = [(i, i ^ bit) for i in range(groups)]
         gathered += [lax.ppermute(part, "ga", swap) for part in gathered]
         offsets += [offset ^ bit for offset in offsets]
+        if bit == groups // 2:
+            gathered[1], folded, hidden = lax.optimization_barrier((gathered[1], folded, hidden))
         bit //= 2
     offsets = tuple(offsets)
 
-    folded = fold(w_root, w_root_in)
     grid, places, pair, step = place(gathered, offsets, folded, padded, pairs)
     pair_swap = [(i, i ^ 1) for i in range(rows) if i ^ 1 < rows]
     step_swap = [(i, (i - 1 ^ 1) + 1) for i in range(1, rows) if (i - 1 ^ 1) + 1 < rows]
     pair = lax.ppermute(pair, "row", pair_swap)
     step = lax.ppermute(step, "row", step_swap)
     sums = conv(grid, folded)
-    root, empty, *sends = finish(places, sums, pair, step, root_bias, groups, padded)
-    come = [sends[0]]
-    for offset, send in zip(offsets[1:], sends[1:]):
-        come.append(lax.ppermute(send, "ga", [(i, i ^ offset) for i in range(groups)]))
-    root_out, lift, weights, spread = unravel(root, w_down, w_skip, offsets, fine_feats.shape[2])
+    order = sorted(range(groups), key=lambda k: (offsets[k] > 0, offsets[k] < groups // 2, offsets[k]))
+    root, empty, *sends = finish(places, sums, pair, step, root_bias, order, padded)
+    come = sends[:1]
+    for k, send in zip(order[1:], sends[1:]):
+        come.append(lax.ppermute(send, "ga", [(i, i ^ offsets[k]) for i in range(groups)]))
+    root_out, lift, weights, spread = unravel(
+        root, w_down, w_skip, [offsets[k] for k in order], fine_feats.shape[2]
+    )
     fine = fine_out(fine_feats, hidden, empty, lift, weights, spread, come)
     return (fine, root_out)
 

time: 42.6 us -> 41.4 us (0.972)
  waiting for transfers between devices: 10.1 us -> 9.42 us
  Pallas kernels: 20.9 us -> 20.3 us
    pallas_call x1, Pallas kernels: 8.25 us -> 7.04 us  [fine_in(): pl.pallas_call(functools.partial(fine_in_kernel, total=total, padded=padd...]
    ppermute x3, waiting for transfers between devices: 4.94 us -> 4.26 us  [shards(): gathered += [lax.ppermute(part, 'ga', swap) for part in gathered]]
    pallas_call x1 -> x2, Pallas kernels: 0.71 us -> 1.36 us  [the longest x1 0.71 us: finish(): pl.pallas_call(functools.partial(finish_kernel, padded, order), in_specs=...]
  transfers between devices with their start and end apart: 8 -> 8, of which waited for: 4 -> 4; matrix products, arithmetic and copies ran while one was open for 0% -> 0% of each run, Pallas kernels for 13% -> 15%
where the time goes in v3:
time: 41.4 us; the launch traced here: 41.2 us
  Pallas kernels  20.3 us (49%)
  starting transfers between devices  10.5 us (25%)
  waiting for transfers between devices  9.42 us (23%)
  between operations  0.96 us (2%)
    pallas_call x1, Pallas kernels, fine_in(): pl.pallas_call(functools.partial(fine_in_kernel, total=total, padded=padd...  7.04 us
    pallas_call x1, Pallas kernels, fine_out(): pl.pallas_call(functools.partial(fine_out_kernel, groups), in_specs=[VMEM...  4.35 us
    ppermute x3, waiting for transfers between devices, shards(): gathered += [lax.ppermute(part, 'ga', swap) for part in gathered]  4.26 us
    ppermute x3, starting transfers between devices, shards(): gathered += [lax.ppermute(part, 'ga', swap) for part in gathered]  3.78 us
    ppermute x3, starting transfers between devices, shards(): lax.ppermute(send, 'ga', [(i, i ^ offsets[k]) for i in range(groups)])  3.24 us
    ppermute x3, waiting for transfers between devices, shards(): lax.ppermute(send, 'ga', [(i, i ^ offsets[k]) for i in range(groups)])  3.12 us
    pallas_call x1, Pallas kernels, conv(): pl.pallas_call(conv_kernel, in_specs=[VMEM, VMEM], out_specs=VMEM, out_sh...  2.86 us
    ppermute x1, starting transfers between devices, shards(): step = lax.ppermute(step, 'row', step_swap)  2.19 us
  transfers between devices with their start and end apart: 8, of which 4 were waited for; matrix products, arithmetic and copies ran while one was open for 0% of the time, Pallas kernels for 15%

profile of v3, /device:TPU:25, one launch (start us, length us, event | category | flops | bytes accessed | tf_op | source)
XLA Modules:
  0.0 41.2 jit_solution(10234951234686205636)
XLA Ops:
  0.6 0.0 copy-start.1
  0.6 0.0 copy-start.3
  0.7 7.0 %fine_in.1 = (bf16[1792,256]{1,0:T(8,128)(2,1)}, bf16[912,128]{1,0:T(8,128)(2,1)}) custom-call(s32[1,112]{1,0:T(1,128)} %bitcast.13, s32[1,8]{1,0:T(1,128)} %bitcast.14, bf16[112,64,512]{2,1,0:T(8,128)(2,1)} %refs_0_.1, bf16[64,128]{1,0:T(8,128)(2,1)} %w_ref.1), custom_call_target="tpu_custom_call" | custom-call | flops 1879048192 | bytes 7340032 | tf_op jit(solution)/shard_map/fine_in/pallas_call | solution.py:149
  7.7 0.0 copy-start
  7.7 0.0 copy-start.4
  7.7 1.3 %collective-permute-start = (bf16[912,128]{1,0:T(8,128)(2,1)}, bf16[912,128]{1,0:T(8,128)(2,1)S(1)}, u32[]{:S(2)}, u32[]{:S(2)}) collective-permute-start(bf16[912,128]{1,0:T(8,128)(2,1)} %get-tuple-element.21.refs_0_), channel_id=1, source_target_pairs={{0,2},{1,3},{2,0},{3,1},{4,6},{5,7},{6,4},{7,5},{8,10},{9,11},{10,... | collective-permute-start | bytes 700424 | tf_op jit(solution)/shard_map/ppermute | solution.py:538
  9.0 1.0 %collective-permute-start.1 = (bf16[912,128]{1,0:T(8,128)(2,1)}, bf16[912,128]{1,0:T(8,128)(2,1)S(1)}, u32[]{:S(2)}, u32[]{:S(2)}) collective-permute-start(bf16[912,128]{1,0:T(8,128)(2,1)} %get-tuple-element.21.refs_0_), channel_id=1, source_target_pairs={{0,1},{1,0},{2,3},{3,2},{4,5},{5,4},{6,7},{7,6},{8,9},{9,8},{10,11... | collective-permute-start | bytes 700424 | tf_op jit(solution)/shard_map/ppermute | solution.py:538
  10.0 0.0 copy-done.1
  10.0 0.0 copy-done.3
  10.0 0.0 copy-start.2
  10.0 0.8 %fold.1.refs_4_.w_ref = bf16[3,4,512,256]{3,2,1,0:T(8,128)(2,1)S(1)} custom-call(bf16[3,3,3,64,256]{4,3,2,1,0:T(8,128)(2,1)S(1)} %bitcast.10, bf16[128,256]{1,0:T(8,128)(2,1)S(1)} %copy-done.3), custom_call_target="tpu_custom_call" | custom-call | flops 301989888 | bytes 6291456 | tf_op jit(solution)/shard_map/fold/pallas_call | solution.py:218
  10.7 0.0 copy-done
  10.7 0.0 copy-done.4
  10.8 0.7 %hide.1.refs_1_ = bf16[1792,512]{1,0:T(8,128)(2,1)S(1)} custom-call(bf16[1792,256]{1,0:T(8,128)(2,1)S(1)} %copy-done, bf16[64,128]{1,0:T(8,128)(2,1)S(1)} %copy-done.4), custom_call_target="tpu_custom_call" | custom-call | flops 469762048 | bytes 2752512 | tf_op jit(solution)/shard_map/hide/pallas_call | solution.py:185
  11.4 3.1 %collective-permute-done.refs_1_ = bf16[912,128]{1,0:T(8,128)(2,1)S(1)} collective-permute-done((bf16[912,128]{1,0:T(8,128)(2,1)}, bf16[912,128]{1,0:T(8,128)(2,1)S(1)}, u32[]{:S(2)}, u32[]{:S(2)}) %collective-permute-start) | collective-permute-done | bytes 233504 | tf_op jit(solution)/shard_map/ppermute | solution.py:538
  14.6 1.5 %collective-permute-start.2 = (bf16[912,128]{1,0:T(8,128)(2,1)S(1)}, bf16[912,128]{1,0:T(8,128)(2,1)S(1)}, u32[]{:S(2)}, u32[]{:S(2)}) collective-permute-start(bf16[912,128]{1,0:T(8,128)(2,1)S(1)} %collective-permute-done.refs_1_), channel_id=1, source_target_pairs={{0,1},{1,0},{2,3},{3,2},{4,5},{5,4},{6,7},{7,6},{8,9},{9,8},{10,11... | collective-permute-start | bytes 700424 | tf_op jit(solution)/shard_map/ppermute | solution.py:538
  16.1 0.0 collective-permute-done.1.refs_2_
  16.1 1.1 %collective-permute-done.2.refs_3_ = bf16[912,128]{1,0:T(8,128)(2,1)S(1)} collective-permute-done((bf16[912,128]{1,0:T(8,128)(2,1)S(1)}, bf16[912,128]{1,0:T(8,128)(2,1)S(1)}, u32[]{:S(2)}, u32[]{:S(2)}) %collective-permute-start.2) | collective-permute-done | bytes 233504 | tf_op jit(solution)/shard_map/ppermute | solution.py:538
  17.2 0.0 copy-done.2
  17.2 2.1 %place.1 = (bf16[2,4,288,512]{3,2,1,0:T(8,128)(2,1)S(1)}, s32[8,512]{1,0:T(8,128)S(1)}, bf16[256,256]{1,0:T(8,128)(2,1)S(1)}, bf16[256,256]{1,0:T(8,128)(2,1)S(1)}) custom-call(bf16[912,128]{1,0:T(8,128)(2,1)S(1)} %copy-done.2, bf16[912,128]{1,0:T(8,128)(2,1)S(1)} %collective-permute-done.refs_1_, bf16[912,128]{1,0:T(8,128)(2,1)S(1)} %collective-permute-done.1.refs_2_, ...), custom_call_target="tpu_custom_call" | custom-call | flops 1073741824 | bytes 6291456 | tf_op jit(solution)/shard_map/place/pallas_call | solution.py:303
  19.3 1.3 %collective-permute-start.3 = (bf16[256,256]{1,0:T(8,128)(2,1)S(1)}, bf16[256,256]{1,0:T(8,128)(2,1)S(1)}, u32[]{:S(2)}, u32[]{:S(2)}) collective-permute-start(bf16[256,256]{1,0:T(8,128)(2,1)S(1)} %get-tuple-element.28), channel_id=1, source_target_pairs={{0,4},{4,0},{8,12},{12,8},{16,20},{20,16},{24,28},{28,24},{1,5},{5... | collective-permute-start | bytes 393224 | tf_op jit(solution)/shard_map/ppermute | solution.py:548
  20.6 2.2 %collective-permute-start.4 = (bf16[256,256]{1,0:T(8,128)(2,1)S(1)}, bf16[256,256]{1,0:T(8,128)(2,1)S(1)}, u32[]{:S(2)}, u32[]{:S(2)}) collective-permute-start(bf16[256,256]{1,0:T(8,128)(2,1)S(1)} %get-tuple-element.29), channel_id=1, source_target_pairs={{4,8},{8,4},{12,16},{16,12},{20,24},{24,20},{5,9},{9,5},{13,17},{1... | collective-permute-start | bytes 393224 | tf_op jit(solution)/shard_map/ppermute | solution.py:549
  22.8 0.0 slice-start
  22.9 0.0 copy-start.5
  22.9 0.0 copy-start.6
  22.9 0.0 copy-start.7
  22.9 0.0 slice-start.1
  22.9 2.9 %conv.1.sums_ref = f32[4,256,256]{2,1,0:T(8,128)S(1)} custom-call(bf16[2,4,288,512]{3,2,1,0:T(8,128)(2,1)S(1)} %get-tuple-element.27.grid_ref, bf16[3,4,512,256]{3,2,1,0:T(8,128)(2,1)S(1)} %fold.1.refs_4_.w_ref), custom_call_target="tpu_custom_call" | custom-call | flops 2684354560 | bytes 6291456 | tf_op jit(solution)/shard_map/conv/pallas_call | solution.py:335
  25.8 0.0 collective-permute-done.3.pair_ref
  25.8 2.0 %collective-permute-done.4.step_ref = bf16[256,256]{1,0:T(8,128)(2,1)S(1)} collective-permute-done((bf16[256,256]{1,0:T(8,128)(2,1)S(1)}, bf16[256,256]{1,0:T(8,128)(2,1)S(1)}, u32[]{:S(2)}, u32[]{:S(2)}) %collective-permute-start.4) | collective-permute-done | bytes 131104 | tf_op jit(solution)/shard_map/ppermute | solution.py:549
  27.8 0.0 copy-done.5
  27.8 0.7 %finish.1 = (bf16[2,512,256]{2,1,0:T(8,128)(2,1)S(1)}, f32[112,128]{1,0:T(8,128)S(1)}, bf16[112,512]{1,0:T(8,128)(2,1)S(1)}, bf16[112,512]{1,0:T(8,128)(2,1)S(1)...) custom-call(s32[8,512]{1,0:T(8,128)S(1)} %get-tuple-element.26.place_ref, f32[4,256,256]{2,1,0:T(8,128)S(1)} %conv.1.sums_ref, ...), custom_call_target="tpu_custom_call" | custom-call | flops 268435456 | bytes 3145728 | tf_op jit(solution)/shard_map/finish/pallas_call | solution.py:379
  28.5 1.3 %collective-permute-start.5 = (bf16[112,512]{1,0:T(8,128)(2,1)S(1)}, bf16[112,512]{1,0:T(8,128)(2,1)S(1)}, u32[]{:S(2)}, u32[]{:S(2)}) collective-permute-start(bf16[112,512]{1,0:T(8,128)(2,1)S(1)} %get-tuple-element.36), channel_id=1, source_target_pairs={{0,2},{1,3},{2,0},{3,1},{4,6},{5,7},{6,4},{7,5},{8,10},{9,11},{10,... | collective-permute-start | bytes 344072 | tf_op jit(solution)/shard_map/ppermute | solution.py:555
  29.8 2.0 %collective-permute-start.6 = (bf16[112,512]{1,0:T(8,128)(2,1)S(1)}, bf16[112,512]{1,0:T(8,128)(2,1)S(1)}, u32[]{:S(2)}, u32[]{:S(2)}) collective-permute-start(bf16[112,512]{1,0:T(8,128)(2,1)S(1)} %get-tuple-element.37), channel_id=1, source_target_pairs={{0,3},{1,2},{2,1},{3,0},{4,7},{5,6},{6,5},{7,4},{8,11},{9,10},{10,... | collective-permute-start | bytes 344072 | tf_op jit(solution)/shard_map/ppermute | solution.py:555
  31.8 0.0 collective-permute-start.7
  31.8 0.0 copy-done.6
  31.8 0.0 copy-done.7
  31.8 1.8 %unravel.1 = (bf16[4,16,2,32,64]{4,3,2,1,0:T(8,128)(2,1)}, bf16[512,256]{1,0:T(8,128)(2,1)S(1)}, bf16[512,256]{1,0:T(8,128)(2,1)S(1)}, bf16[64,512]{1,0:T(8,128)(2,1)S(1)}) custom-call(bf16[2,512,256]{2,1,0:T(8,128)(2,1)S(1)} %get-tuple-element.31.root_ref, bf16[256,128]{1,0:T(8,128)(2,1)S(1)} %copy-done.6, bf16[64,128]{1,0:T(8,128)(2,1)S(1)} %bitcast.12), custom_call_target="tpu_custom_call" | custom-call | flops 536870912 | bytes 2097152 | tf_op jit(solution)/shard_map/unravel/pallas_call | solution.py:430
  33.6 0.0 collective-permute-done.5.refs_7_
  33.6 3.1 %collective-permute-done.6.refs_8_ = bf16[112,512]{1,0:T(8,128)(2,1)S(1)} collective-permute-done((bf16[112,512]{1,0:T(8,128)(2,1)S(1)}, bf16[112,512]{1,0:T(8,128)(2,1)S(1)}, u32[]{:S(2)}, u32[]{:S(2)}) %collective-permute-start.6) | collective-permute-done | bytes 114720 | tf_op jit(solution)/shard_map/ppermute | solution.py:555
  36.7 0.0 collective-permute-done.7.refs_9_
  36.7 0.0 slice-done
  36.7 0.0 slice-done.1
  36.7 4.4 %fine_out.1 = bf16[112,64,512]{2,1,0:T(8,128)(2,1)} custom-call(bf16[112,64,512]{2,1,0:T(8,128)(2,1)S(1)} %bitcast.9, bf16[1792,512]{1,0:T(8,128)(2,1)S(1)} %hide.1.refs_1_, f32[112,128]{1,0:T(8,128)S(1)} %get-tuple-element.30.refs_2_, bf16[512,256]{1,0:T(8,128)(2,1)S(1)} %get-tuple-element.32.refs_3_, bf16[512,256]{1,0:T(8,128)(2,1)S(1)} %get-tuple-element.33.refs_4_, ...), custom_call_target="tpu_custom_call" | custom-call | flops 1879048192 | bytes 14680064 | tf_op jit(solution)/shard_map/fine_out/pallas_call | solution.py:503
  (1 shorter events, 0.0 us)
Async XLA Ops:
  0.6 9.3 %copy-start.1 = (bf16[64,256,3,3,3]{1,0,4,3,2:T(8,128)(2,1)S(1)}, bf16[64,256,3,3,3]{1,0,4,3,2:T(8,128)(2,1)}, u32[]{:S(2)}) copy-start(bf16[64,256,3,3,3]{1,0,4,3,2:T(8,128)(2,1)} %param.14) | copy-start | bytes 2654212
  0.6 9.3 %copy-start.3 = (bf16[128,256]{1,0:T(8,128)(2,1)S(1)}, bf16[128,256]{1,0:T(8,128)(2,1)}, u32[]{:S(2)}) copy-start(bf16[128,256]{1,0:T(8,128)(2,1)} %in_ref.1) | copy-start | bytes 196612
  7.7 3.0 %copy-start = (bf16[1792,256]{1,0:T(8,128)(2,1)S(1)}, bf16[1792,256]{1,0:T(8,128)(2,1)}, u32[]{:S(2)}) copy-start(bf16[1792,256]{1,0:T(8,128)(2,1)} %get-tuple-element.22.turned_ref) | copy-start | bytes 2752516
  7.7 3.0 %copy-start.4 = (bf16[64,128]{1,0:T(8,128)(2,1)S(1)}, bf16[64,128]{1,0:T(8,128)(2,1)}, u32[]{:S(2)}) copy-start(bf16[64,128]{1,0:T(8,128)(2,1)} %w_ref.1) | copy-start | bytes 49156
  7.7 6.8 %collective-permute-start = (bf16[912,128]{1,0:T(8,128)(2,1)}, bf16[912,128]{1,0:T(8,128)(2,1)S(1)}, u32[]{:S(2)}, u32[]{:S(2)}) collective-permute-start(bf16[912,128]{1,0:T(8,128)(2,1)} %get-tuple-element.21.refs_0_), channel_id=1, source_target_pairs={{0,2},{1,3},{2,0},{3,1},{4,6},{5,7},{6,4},{7,5},{8,10},{9,11},{10,... | collective-permute-start | bytes 700424 | tf_op jit(solution)/shard_map/ppermute | solution.py:538
  9.0 7.1 %collective-permute-start.1 = (bf16[912,128]{1,0:T(8,128)(2,1)}, bf16[912,128]{1,0:T(8,128)(2,1)S(1)}, u32[]{:S(2)}, u32[]{:S(2)}) collective-permute-start(bf16[912,128]{1,0:T(8,128)(2,1)} %get-tuple-element.21.refs_0_), channel_id=1, source_target_pairs={{0,1},{1,0},{2,3},{3,2},{4,5},{5,4},{6,7},{7,6},{8,9},{9,8},{10,11... | collective-permute-start | bytes 700424 | tf_op jit(solution)/shard_map/ppermute | solution.py:538
  10.0 7.3 %copy-start.2 = (bf16[912,128]{1,0:T(8,128)(2,1)S(1)}, bf16[912,128]{1,0:T(8,128)(2,1)}, u32[]{:S(2)}) copy-start(bf16[912,128]{1,0:T(8,128)(2,1)} %get-tuple-element.21.refs_0_) | copy-start | bytes 700420
  14.6 2.7 %collective-permute-start.2 = (bf16[912,128]{1,0:T(8,128)(2,1)S(1)}, bf16[912,128]{1,0:T(8,128)(2,1)S(1)}, u32[]{:S(2)}, u32[]{:S(2)}) collective-permute-start(bf16[912,128]{1,0:T(8,128)(2,1)S(1)} %collective-permute-done.refs_1_), channel_id=1, source_target_pairs={{0,1},{1,0},{2,3},{3,2},{4,5},{5,4},{6,7},{7,6},{8,9},{9,8},{10,11... | collective-permute-start | bytes 700424 | tf_op jit(solution)/shard_map/ppermute | solution.py:538
  19.3 6.4 %collective-permute-start.3 = (bf16[256,256]{1,0:T(8,128)(2,1)S(1)}, bf16[256,256]{1,0:T(8,128)(2,1)S(1)}, u32[]{:S(2)}, u32[]{:S(2)}) collective-permute-start(bf16[256,256]{1,0:T(8,128)(2,1)S(1)} %get-tuple-element.28), channel_id=1, source_target_pairs={{0,4},{4,0},{8,12},{12,8},{16,20},{20,16},{24,28},{28,24},{1,5},{5... | collective-permute-start | bytes 393224 | tf_op jit(solution)/shard_map/ppermute | solution.py:548
  20.6 7.2 %collective-permute-start.4 = (bf16[256,256]{1,0:T(8,128)(2,1)S(1)}, bf16[256,256]{1,0:T(8,128)(2,1)S(1)}, u32[]{:S(2)}, u32[]{:S(2)}) collective-permute-start(bf16[256,256]{1,0:T(8,128)(2,1)S(1)} %get-tuple-element.29), channel_id=1, source_target_pairs={{4,8},{8,4},{12,16},{16,12},{20,24},{24,20},{5,9},{9,5},{13,17},{1... | collective-permute-start | bytes 393224 | tf_op jit(solution)/shard_map/ppermute | solution.py:549
  22.8 13.9 %slice-start = ((s8[7340032]{0:T(1024)(128)(4,1)}), s8[4194304]{0:T(1024)(128)(4,1)S(1)}, s32[]{:S(2)}) async-start(s8[7340032]{0:T(1024)(128)(4,1)} %bitcast.8), calls=%async_computation | async-start | bytes 8388608
  22.9 5.0 %copy-start.5 = (f32[64]{0:T(128)S(1)}, f32[64]{0:T(128)}, u32[]{:S(2)}) copy-start(f32[64]{0:T(128)} %param.15) | copy-start | bytes 772
  22.9 8.9 %copy-start.6 = (bf16[256,128]{1,0:T(8,128)(2,1)S(1)}, bf16[256,128]{1,0:T(8,128)(2,1)}, u32[]{:S(2)}) copy-start(bf16[256,128]{1,0:T(8,128)(2,1)} %down_ref.1) | copy-start | bytes 196612
  22.9 8.9 %copy-start.7 = (bf16[128,64]{0,1:T(8,128)(2,1)S(1)}, bf16[128,64]{0,1:T(8,128)(2,1)}, u32[]{:S(2)}) copy-start(bf16[128,64]{0,1:T(8,128)(2,1)} %param.17) | copy-start | bytes 49156
  22.9 13.8 %slice-start.1 = ((s8[7340032]{0:T(1024)(128)(4,1)}), s8[3145728]{0:T(1024)(128)(4,1)S(1)}, s32[]{:S(2)}) async-start(s8[7340032]{0:T(1024)(128)(4,1)} %bitcast.8), calls=%async_computation.1 | async-start | bytes 6291456
  28.5 5.0 %collective-permute-start.5 = (bf16[112,512]{1,0:T(8,128)(2,1)S(1)}, bf16[112,512]{1,0:T(8,128)(2,1)S(1)}, u32[]{:S(2)}, u32[]{:S(2)}) collective-permute-start(bf16[112,512]{1,0:T(8,128)(2,1)S(1)} %get-tuple-element.36), channel_id=1, source_target_pairs={{0,2},{1,3},{2,0},{3,1},{4,6},{5,7},{6,4},{7,5},{8,10},{9,11},{10,... | collective-permute-start | bytes 344072 | tf_op jit(solution)/shard_map/ppermute | solution.py:555
  29.8 6.9 %collective-permute-start.6 = (bf16[112,512]{1,0:T(8,128)(2,1)S(1)}, bf16[112,512]{1,0:T(8,128)(2,1)S(1)}, u32[]{:S(2)}, u32[]{:S(2)}) collective-permute-start(bf16[112,512]{1,0:T(8,128)(2,1)S(1)} %get-tuple-element.37), channel_id=1, source_target_pairs={{0,3},{1,2},{2,1},{3,0},{4,7},{5,6},{6,5},{7,4},{8,11},{9,10},{10,... | collective-permute-start | bytes 344072 | tf_op jit(solution)/shard_map/ppermute | solution.py:555
  31.8 4.9 %collective-permute-start.7 = (bf16[112,512]{1,0:T(8,128)(2,1)S(1)}, bf16[112,512]{1,0:T(8,128)(2,1)S(1)}, u32[]{:S(2)}, u32[]{:S(2)}) collective-permute-start(bf16[112,512]{1,0:T(8,128)(2,1)S(1)} %get-tuple-element.38), channel_id=1, source_target_pairs={{0,1},{1,0},{2,3},{3,2},{4,5},{5,4},{6,7},{7,6},{8,9},{9,8},{10,11... | collective-permute-start | bytes 344072 | tf_op jit(solution)/shard_map/ppermute | solution.py:555

commit v4 on v3

--- a/solution.py
+++ b/solution.py
@@ -544,9 +544,14 @@
 
     grid, places, pair, step = place(gathered, offsets, folded, padded, pairs)
     pair_swap = [(i, i ^ 1) for i in range(rows) if i ^ 1 < rows]
-    step_swap = [(i, (i - 1 ^ 1) + 1) for i in range(1, rows) if (i - 1 ^ 1) + 1 < rows]
+    step_swap = []
+    for i in range(rows):
+        inner = 0 < i < rows - 1
+        for j in range(groups):
+            target = ((i - 1 ^ 1) + 1) * groups + j if inner else i * groups + (j ^ 1)
+            step_swap.append((i * groups + j, target))
     pair = lax.ppermute(pair, "row", pair_swap)
-    step = lax.ppermute(step, "row", step_swap)
+    step = lax.ppermute(step, ("row", "ga"), step_swap)
     sums = conv(grid, folded)
     order = sorted(range(groups), key=lambda k: (offsets[k] > 0, offsets[k] < groups // 2, offsets[k]))
     root, empty, *sends = finish(places, sums, pair, step, root_bias, order, padded)

time: 41.4 us -> 40.2 us (0.971)
  starting transfers between devices: 10.5 us -> 9 us
    ppermute x1, starting transfers between devices: 2.19 us -> 0.11 us  [shards(): step = lax.ppermute(step, ('row', 'ga'), step_swap)]
    ppermute x3, starting transfers between devices: 3.24 us -> 3.8 us  [shards(): lax.ppermute(send, 'ga', [(i, i ^ offsets[k]) for i in range(groups)])]
    ppermute x1, waiting for transfers between devices: 0.01 us -> 0.47 us  [shards(): pair = lax.ppermute(pair, 'row', pair_swap)]
  transfers between devices with their start and end apart: 8 -> 8, of which waited for: 4 -> 5; matrix products, arithmetic and copies ran while one was open for 0% -> 0% of each run, Pallas kernels for 15% -> 15%
where the time goes in v4:
time: 40.2 us; the launch traced here: 39.9 us
  Pallas kernels  20.3 us (50%)
  waiting for transfers between devices  9.77 us (24%)
  starting transfers between devices  9 us (22%)
  between operations  0.76 us (2%)
    pallas_call x1, Pallas kernels, fine_in(): pl.pallas_call(functools.partial(fine_in_kernel, total=total, padded=padd...  7.03 us
    pallas_call x1, Pallas kernels, fine_out(): pl.pallas_call(functools.partial(fine_out_kernel, groups), in_specs=[VMEM...  4.35 us
    ppermute x3, waiting for transfers between devices, shards(): gathered += [lax.ppermute(part, 'ga', swap) for part in gathered]  4.27 us
    ppermute x3, starting transfers between devices, shards(): lax.ppermute(send, 'ga', [(i, i ^ offsets[k]) for i in range(groups)])  3.8 us
    ppermute x3, starting transfers between devices, shards(): gathered += [lax.ppermute(part, 'ga', swap) for part in gathered]  3.78 us
    ppermute x3, waiting for transfers between devices, shards(): lax.ppermute(send, 'ga', [(i, i ^ offsets[k]) for i in range(groups)])  3.12 us
    pallas_call x1, Pallas kernels, conv(): pl.pallas_call(conv_kernel, in_specs=[VMEM, VMEM], out_specs=VMEM, out_sh...  2.86 us
    pallas_call x1, Pallas kernels, place(): pl.pallas_call(functools.partial(place_kernel, offsets, padded, pairs), i...  2.11 us
  transfers between devices with their start and end apart: 8, of which 5 were waited for; matrix products, arithmetic and copies ran while one was open for 0% of the time, Pallas kernels for 15%

profile of v4, /device:TPU:25, one launch (start us, length us, event | category | flops | bytes accessed | tf_op | source)
XLA Modules:
  0.0 39.9 jit_solution(8884467951107960357)
XLA Ops:
  0.6 0.0 copy-start.1
  0.6 0.0 copy-start.3
  0.7 7.0 %fine_in.1 = (bf16[1792,256]{1,0:T(8,128)(2,1)}, bf16[912,128]{1,0:T(8,128)(2,1)}) custom-call(s32[1,112]{1,0:T(1,128)} %bitcast.13, s32[1,8]{1,0:T(1,128)} %bitcast.14, bf16[112,64,512]{2,1,0:T(8,128)(2,1)} %refs_0_.1, bf16[64,128]{1,0:T(8,128)(2,1)} %w_ref.1), custom_call_target="tpu_custom_call" | custom-call | flops 1879048192 | bytes 7340032 | tf_op jit(solution)/shard_map/fine_in/pallas_call | solution.py:149
  7.7 0.0 copy-start
  7.7 0.0 copy-start.4
  7.7 1.3 %collective-permute-start = (bf16[912,128]{1,0:T(8,128)(2,1)}, bf16[912,128]{1,0:T(8,128)(2,1)S(1)}, u32[]{:S(2)}, u32[]{:S(2)}) collective-permute-start(bf16[912,128]{1,0:T(8,128)(2,1)} %get-tuple-element.21.refs_0_), channel_id=1, source_target_pairs={{0,2},{1,3},{2,0},{3,1},{4,6},{5,7},{6,4},{7,5},{8,10},{9,11},{10,... | collective-permute-start | bytes 700424 | tf_op jit(solution)/shard_map/ppermute | solution.py:538
  9.0 1.0 %collective-permute-start.1 = (bf16[912,128]{1,0:T(8,128)(2,1)}, bf16[912,128]{1,0:T(8,128)(2,1)S(1)}, u32[]{:S(2)}, u32[]{:S(2)}) collective-permute-start(bf16[912,128]{1,0:T(8,128)(2,1)} %get-tuple-element.21.refs_0_), channel_id=1, source_target_pairs={{0,1},{1,0},{2,3},{3,2},{4,5},{5,4},{6,7},{7,6},{8,9},{9,8},{10,11... | collective-permute-start | bytes 700424 | tf_op jit(solution)/shard_map/ppermute | solution.py:538
  10.0 0.0 copy-done.1
  10.0 0.0 copy-done.3
  10.0 0.0 copy-start.2
  10.0 0.8 %fold.1.refs_4_.w_ref = bf16[3,4,512,256]{3,2,1,0:T(8,128)(2,1)S(1)} custom-call(bf16[3,3,3,64,256]{4,3,2,1,0:T(8,128)(2,1)S(1)} %bitcast.10, bf16[128,256]{1,0:T(8,128)(2,1)S(1)} %copy-done.3), custom_call_target="tpu_custom_call" | custom-call | flops 301989888 | bytes 6291456 | tf_op jit(solution)/shard_map/fold/pallas_call | solution.py:218
  10.7 0.0 copy-done
  10.7 0.0 copy-done.4
  10.8 0.7 %hide.1.refs_1_ = bf16[1792,512]{1,0:T(8,128)(2,1)S(1)} custom-call(bf16[1792,256]{1,0:T(8,128)(2,1)S(1)} %copy-done, bf16[64,128]{1,0:T(8,128)(2,1)S(1)} %copy-done.4), custom_call_target="tpu_custom_call" | custom-call | flops 469762048 | bytes 2752512 | tf_op jit(solution)/shard_map/hide/pallas_call | solution.py:185
  11.4 3.1 %collective-permute-done.refs_1_ = bf16[912,128]{1,0:T(8,128)(2,1)S(1)} collective-permute-done((bf16[912,128]{1,0:T(8,128)(2,1)}, bf16[912,128]{1,0:T(8,128)(2,1)S(1)}, u32[]{:S(2)}, u32[]{:S(2)}) %collective-permute-start) | collective-permute-done | bytes 233504 | tf_op jit(solution)/shard_map/ppermute | solution.py:538
  14.6 1.5 %collective-permute-start.2 = (bf16[912,128]{1,0:T(8,128)(2,1)S(1)}, bf16[912,128]{1,0:T(8,128)(2,1)S(1)}, u32[]{:S(2)}, u32[]{:S(2)}) collective-permute-start(bf16[912,128]{1,0:T(8,128)(2,1)S(1)} %collective-permute-done.refs_1_), channel_id=1, source_target_pairs={{0,1},{1,0},{2,3},{3,2},{4,5},{5,4},{6,7},{7,6},{8,9},{9,8},{10,11... | collective-permute-start | bytes 700424 | tf_op jit(solution)/shard_map/ppermute | solution.py:538
  16.1 0.0 collective-permute-done.1.refs_2_
  16.1 1.1 %collective-permute-done.2.refs_3_ = bf16[912,128]{1,0:T(8,128)(2,1)S(1)} collective-permute-done((bf16[912,128]{1,0:T(8,128)(2,1)S(1)}, bf16[912,128]{1,0:T(8,128)(2,1)S(1)}, u32[]{:S(2)}, u32[]{:S(2)}) %collective-permute-start.2) | collective-permute-done | bytes 233504 | tf_op jit(solution)/shard_map/ppermute | solution.py:538
  17.2 0.0 copy-done.2
  17.2 2.1 %place.1 = (bf16[2,4,288,512]{3,2,1,0:T(8,128)(2,1)S(1)}, s32[8,512]{1,0:T(8,128)S(1)}, bf16[256,256]{1,0:T(8,128)(2,1)S(1)}, bf16[256,256]{1,0:T(8,128)(2,1)S(1)}) custom-call(bf16[912,128]{1,0:T(8,128)(2,1)S(1)} %copy-done.2, bf16[912,128]{1,0:T(8,128)(2,1)S(1)} %collective-permute-done.refs_1_, bf16[912,128]{1,0:T(8,128)(2,1)S(1)} %collective-permute-done.1.refs_2_, ...), custom_call_target="tpu_custom_call" | custom-call | flops 1073741824 | bytes 6291456 | tf_op jit(solution)/shard_map/place/pallas_call | solution.py:303
  19.3 1.3 %collective-permute-start.3 = (bf16[256,256]{1,0:T(8,128)(2,1)S(1)}, bf16[256,256]{1,0:T(8,128)(2,1)S(1)}, u32[]{:S(2)}, u32[]{:S(2)}) collective-permute-start(bf16[256,256]{1,0:T(8,128)(2,1)S(1)} %get-tuple-element.28), channel_id=1, source_target_pairs={{0,4},{4,0},{8,12},{12,8},{16,20},{20,16},{24,28},{28,24},{1,5},{5... | collective-permute-start | bytes 393224 | tf_op jit(solution)/shard_map/ppermute | solution.py:553
  20.6 0.1 collective-permute-start.4
  20.8 0.0 slice-start
  20.8 0.0 copy-start.5
  20.8 0.0 copy-start.6
  20.8 0.0 copy-start.7
  20.8 0.0 slice-start.1
  20.8 2.9 %conv.1.sums_ref = f32[4,256,256]{2,1,0:T(8,128)S(1)} custom-call(bf16[2,4,288,512]{3,2,1,0:T(8,128)(2,1)S(1)} %get-tuple-element.27.grid_ref, bf16[3,4,512,256]{3,2,1,0:T(8,128)(2,1)S(1)} %fold.1.refs_4_.w_ref), custom_call_target="tpu_custom_call" | custom-call | flops 2684354560 | bytes 6291456 | tf_op jit(solution)/shard_map/conv/pallas_call | solution.py:335
  23.7 0.5 %collective-permute-done.3.pair_ref = bf16[256,256]{1,0:T(8,128)(2,1)S(1)} collective-permute-done((bf16[256,256]{1,0:T(8,128)(2,1)S(1)}, bf16[256,256]{1,0:T(8,128)(2,1)S(1)}, u32[]{:S(2)}, u32[]{:S(2)}) %collective-permute-start.3) | collective-permute-done | bytes 131104 | tf_op jit(solution)/shard_map/ppermute | solution.py:553
  24.1 1.9 %collective-permute-done.4.step_ref = bf16[256,256]{1,0:T(8,128)(2,1)S(1)} collective-permute-done((bf16[256,256]{1,0:T(8,128)(2,1)S(1)}, bf16[256,256]{1,0:T(8,128)(2,1)S(1)}, u32[]{:S(2)}, u32[]{:S(2)}) %collective-permute-start.4) | collective-permute-done | bytes 131104 | tf_op jit(solution)/shard_map/ppermute | solution.py:554
  26.0 0.0 copy-done.5
  26.0 0.7 %finish.1 = (bf16[2,512,256]{2,1,0:T(8,128)(2,1)S(1)}, f32[112,128]{1,0:T(8,128)S(1)}, bf16[112,512]{1,0:T(8,128)(2,1)S(1)}, bf16[112,512]{1,0:T(8,128)(2,1)S(1)...) custom-call(s32[8,512]{1,0:T(8,128)S(1)} %get-tuple-element.26.place_ref, f32[4,256,256]{2,1,0:T(8,128)S(1)} %conv.1.sums_ref, ...), custom_call_target="tpu_custom_call" | custom-call | flops 268435456 | bytes 3145728 | tf_op jit(solution)/shard_map/finish/pallas_call | solution.py:379
  26.8 1.3 %collective-permute-start.5 = (bf16[112,512]{1,0:T(8,128)(2,1)S(1)}, bf16[112,512]{1,0:T(8,128)(2,1)S(1)}, u32[]{:S(2)}, u32[]{:S(2)}) collective-permute-start(bf16[112,512]{1,0:T(8,128)(2,1)S(1)} %get-tuple-element.36), channel_id=1, source_target_pairs={{0,2},{1,3},{2,0},{3,1},{4,6},{5,7},{6,4},{7,5},{8,10},{9,11},{10,... | collective-permute-start | bytes 344072 | tf_op jit(solution)/shard_map/ppermute | solution.py:560
  28.0 2.5 %collective-permute-start.6 = (bf16[112,512]{1,0:T(8,128)(2,1)S(1)}, bf16[112,512]{1,0:T(8,128)(2,1)S(1)}, u32[]{:S(2)}, u32[]{:S(2)}) collective-permute-start(bf16[112,512]{1,0:T(8,128)(2,1)S(1)} %get-tuple-element.37), channel_id=1, source_target_pairs={{0,3},{1,2},{2,1},{3,0},{4,7},{5,6},{6,5},{7,4},{8,11},{9,10},{10,... | collective-permute-start | bytes 344072 | tf_op jit(solution)/shard_map/ppermute | solution.py:560
  30.6 0.0 collective-permute-start.7
  30.6 0.0 copy-done.6
  30.6 0.0 copy-done.7
  30.6 1.8 %unravel.1 = (bf16[4,16,2,32,64]{4,3,2,1,0:T(8,128)(2,1)}, bf16[512,256]{1,0:T(8,128)(2,1)S(1)}, bf16[512,256]{1,0:T(8,128)(2,1)S(1)}, bf16[64,512]{1,0:T(8,128)(2,1)S(1)}) custom-call(bf16[2,512,256]{2,1,0:T(8,128)(2,1)S(1)} %get-tuple-element.31.root_ref, bf16[256,128]{1,0:T(8,128)(2,1)S(1)} %copy-done.6, bf16[64,128]{1,0:T(8,128)(2,1)S(1)} %bitcast.12), custom_call_target="tpu_custom_call" | custom-call | flops 536870912 | bytes 2097152 | tf_op jit(solution)/shard_map/unravel/pallas_call | solution.py:430
  32.4 0.0 collective-permute-done.5.refs_7_
  32.4 3.1 %collective-permute-done.6.refs_8_ = bf16[112,512]{1,0:T(8,128)(2,1)S(1)} collective-permute-done((bf16[112,512]{1,0:T(8,128)(2,1)S(1)}, bf16[112,512]{1,0:T(8,128)(2,1)S(1)}, u32[]{:S(2)}, u32[]{:S(2)}) %collective-permute-start.6) | collective-permute-done | bytes 114720 | tf_op jit(solution)/shard_map/ppermute | solution.py:560
  35.5 0.0 collective-permute-done.7.refs_9_
  35.5 0.0 slice-done
  35.5 0.0 slice-done.1
  35.5 4.4 %fine_out.1 = bf16[112,64,512]{2,1,0:T(8,128)(2,1)} custom-call(bf16[112,64,512]{2,1,0:T(8,128)(2,1)S(1)} %bitcast.9, bf16[1792,512]{1,0:T(8,128)(2,1)S(1)} %hide.1.refs_1_, f32[112,128]{1,0:T(8,128)S(1)} %get-tuple-element.30.refs_2_, bf16[512,256]{1,0:T(8,128)(2,1)S(1)} %get-tuple-element.32.refs_3_, bf16[512,256]{1,0:T(8,128)(2,1)S(1)} %get-tuple-element.33.refs_4_, ...), custom_call_target="tpu_custom_call" | custom-call | flops 1879048192 | bytes 14680064 | tf_op jit(solution)/shard_map/fine_out/pallas_call | solution.py:503
  (1 shorter events, 0.0 us)
Async XLA Ops:
  0.6 9.3 %copy-start.1 = (bf16[64,256,3,3,3]{1,0,4,3,2:T(8,128)(2,1)S(1)}, bf16[64,256,3,3,3]{1,0,4,3,2:T(8,128)(2,1)}, u32[]{:S(2)}) copy-start(bf16[64,256,3,3,3]{1,0,4,3,2:T(8,128)(2,1)} %param.14) | copy-start | bytes 2654212
  0.6 9.3 %copy-start.3 = (bf16[128,256]{1,0:T(8,128)(2,1)S(1)}, bf16[128,256]{1,0:T(8,128)(2,1)}, u32[]{:S(2)}) copy-start(bf16[128,256]{1,0:T(8,128)(2,1)} %in_ref.1) | copy-start | bytes 196612
  7.7 3.0 %copy-start = (bf16[1792,256]{1,0:T(8,128)(2,1)S(1)}, bf16[1792,256]{1,0:T(8,128)(2,1)}, u32[]{:S(2)}) copy-start(bf16[1792,256]{1,0:T(8,128)(2,1)} %get-tuple-element.22.turned_ref) | copy-start | bytes 2752516
  7.7 3.0 %copy-start.4 = (bf16[64,128]{1,0:T(8,128)(2,1)S(1)}, bf16[64,128]{1,0:T(8,128)(2,1)}, u32[]{:S(2)}) copy-start(bf16[64,128]{1,0:T(8,128)(2,1)} %w_ref.1) | copy-start | bytes 49156
  7.7 6.8 %collective-permute-start = (bf16[912,128]{1,0:T(8,128)(2,1)}, bf16[912,128]{1,0:T(8,128)(2,1)S(1)}, u32[]{:S(2)}, u32[]{:S(2)}) collective-permute-start(bf16[912,128]{1,0:T(8,128)(2,1)} %get-tuple-element.21.refs_0_), channel_id=1, source_target_pairs={{0,2},{1,3},{2,0},{3,1},{4,6},{5,7},{6,4},{7,5},{8,10},{9,11},{10,... | collective-permute-start | bytes 700424 | tf_op jit(solution)/shard_map/ppermute | solution.py:538
  9.0 7.1 %collective-permute-start.1 = (bf16[912,128]{1,0:T(8,128)(2,1)}, bf16[912,128]{1,0:T(8,128)(2,1)S(1)}, u32[]{:S(2)}, u32[]{:S(2)}) collective-permute-start(bf16[912,128]{1,0:T(8,128)(2,1)} %get-tuple-element.21.refs_0_), channel_id=1, source_target_pairs={{0,1},{1,0},{2,3},{3,2},{4,5},{5,4},{6,7},{7,6},{8,9},{9,8},{10,11... | collective-permute-start | bytes 700424 | tf_op jit(solution)/shard_map/ppermute | solution.py:538
  10.0 7.3 %copy-start.2 = (bf16[912,128]{1,0:T(8,128)(2,1)S(1)}, bf16[912,128]{1,0:T(8,128)(2,1)}, u32[]{:S(2)}) copy-start(bf16[912,128]{1,0:T(8,128)(2,1)} %get-tuple-element.21.refs_0_) | copy-start | bytes 700420
  14.6 2.7 %collective-permute-start.2 = (bf16[912,128]{1,0:T(8,128)(2,1)S(1)}, bf16[912,128]{1,0:T(8,128)(2,1)S(1)}, u32[]{:S(2)}, u32[]{:S(2)}) collective-permute-start(bf16[912,128]{1,0:T(8,128)(2,1)S(1)} %collective-permute-done.refs_1_), channel_id=1, source_target_pairs={{0,1},{1,0},{2,3},{3,2},{4,5},{5,4},{6,7},{7,6},{8,9},{9,8},{10,11... | collective-permute-start | bytes 700424 | tf_op jit(solution)/shard_map/ppermute | solution.py:538
  19.3 4.8 %collective-permute-start.3 = (bf16[256,256]{1,0:T(8,128)(2,1)S(1)}, bf16[256,256]{1,0:T(8,128)(2,1)S(1)}, u32[]{:S(2)}, u32[]{:S(2)}) collective-permute-start(bf16[256,256]{1,0:T(8,128)(2,1)S(1)} %get-tuple-element.28), channel_id=1, source_target_pairs={{0,4},{4,0},{8,12},{12,8},{16,20},{20,16},{24,28},{28,24},{1,5},{5... | collective-permute-start | bytes 393224 | tf_op jit(solution)/shard_map/ppermute | solution.py:553
  20.6 5.4 %collective-permute-start.4 = (bf16[256,256]{1,0:T(8,128)(2,1)S(1)}, bf16[256,256]{1,0:T(8,128)(2,1)S(1)}, u32[]{:S(2)}, u32[]{:S(2)}) collective-permute-start(bf16[256,256]{1,0:T(8,128)(2,1)S(1)} %get-tuple-element.29), channel_id=1, source_target_pairs={{0,1},{1,0},{2,3},{3,2},{4,8},{5,9},{6,10},{7,11},{8,4},{9,5},{10,... | collective-permute-start | bytes 393224 | tf_op jit(solution)/shard_map/ppermute | solution.py:554
  20.8 14.7 %slice-start = ((s8[7340032]{0:T(1024)(128)(4,1)}), s8[4194304]{0:T(1024)(128)(4,1)S(1)}, s32[]{:S(2)}) async-start(s8[7340032]{0:T(1024)(128)(4,1)} %bitcast.8), calls=%async_computation | async-start | bytes 8388608
  20.8 5.3 %copy-start.5 = (f32[64]{0:T(128)S(1)}, f32[64]{0:T(128)}, u32[]{:S(2)}) copy-start(f32[64]{0:T(128)} %param.15) | copy-start | bytes 772
  20.8 9.8 %copy-start.6 = (bf16[256,128]{1,0:T(8,128)(2,1)S(1)}, bf16[256,128]{1,0:T(8,128)(2,1)}, u32[]{:S(2)}) copy-start(bf16[256,128]{1,0:T(8,128)(2,1)} %down_ref.1) | copy-start | bytes 196612
  20.8 9.8 %copy-start.7 = (bf16[128,64]{0,1:T(8,128)(2,1)S(1)}, bf16[128,64]{0,1:T(8,128)(2,1)}, u32[]{:S(2)}) copy-start(bf16[128,64]{0,1:T(8,128)(2,1)} %param.17) | copy-start | bytes 49156
  20.8 14.7 %slice-start.1 = ((s8[7340032]{0:T(1024)(128)(4,1)}), s8[3145728]{0:T(1024)(128)(4,1)S(1)}, s32[]{:S(2)}) async-start(s8[7340032]{0:T(1024)(128)(4,1)} %bitcast.8), calls=%async_computation.1 | async-start | bytes 6291456
  26.8 5.6 %collective-permute-start.5 = (bf16[112,512]{1,0:T(8,128)(2,1)S(1)}, bf16[112,512]{1,0:T(8,128)(2,1)S(1)}, u32[]{:S(2)}, u32[]{:S(2)}) collective-permute-start(bf16[112,512]{1,0:T(8,128)(2,1)S(1)} %get-tuple-element.36), channel_id=1, source_target_pairs={{0,2},{1,3},{2,0},{3,1},{4,6},{5,7},{6,4},{7,5},{8,10},{9,11},{10,... | collective-permute-start | bytes 344072 | tf_op jit(solution)/shard_map/ppermute | solution.py:560
  28.0 7.5 %collective-permute-start.6 = (bf16[112,512]{1,0:T(8,128)(2,1)S(1)}, bf16[112,512]{1,0:T(8,128)(2,1)S(1)}, u32[]{:S(2)}, u32[]{:S(2)}) collective-permute-start(bf16[112,512]{1,0:T(8,128)(2,1)S(1)} %get-tuple-element.37), channel_id=1, source_target_pairs={{0,3},{1,2},{2,1},{3,0},{4,7},{5,6},{6,5},{7,4},{8,11},{9,10},{10,... | collective-permute-start | bytes 344072 | tf_op jit(solution)/shard_map/ppermute | solution.py:560
  30.6 4.9 %collective-permute-start.7 = (bf16[112,512]{1,0:T(8,128)(2,1)S(1)}, bf16[112,512]{1,0:T(8,128)(2,1)S(1)}, u32[]{:S(2)}, u32[]{:S(2)}) collective-permute-start(bf16[112,512]{1,0:T(8,128)(2,1)S(1)} %get-tuple-element.38), channel_id=1, source_target_pairs={{0,1},{1,0},{2,3},{3,2},{4,5},{5,4},{6,7},{7,6},{8,9},{9,8},{10,11... | collective-permute-start | bytes 344072 | tf_op jit(solution)/shard_map/ppermute | solution.py:560

commit v5 on v4

--- a/solution.py
+++ b/solution.py
@@ -15,6 +15,8 @@
 OCT = RXY // 2
 LAYERS = RZ_REG // 2
 PLANE = OCT * OCT
+INNER = (1, 2)
+OUTER = (0, 3)
 BORDERED = PLANE + 2 * OCT
 SUBS = 8
 META = 16
@@ -230,11 +232,33 @@
     return ((1, 0), (0, OCT), (1, OCT), (0, 2 * OCT))[j]
 
 
+def fill_planes(planes_ref, planes, place, table):
+    depth = table.shape[1] // SUBS
+    x = place % OCT
+    planes_ref[:, :, 0:OCT, :] = jnp.zeros((2, LAYERS, OCT, 4 * depth), BF16)
+    planes_ref[:, :, OCT + PLANE :, :] = jnp.zeros((2, LAYERS, OCT, 4 * depth), BF16)
+    live = place >= 0
+    shifted = (
+        (0, 1, jnp.where(live & (x < OCT - 1), place + 1, -1)),
+        (1, 0, place),
+        (2, 1, place),
+        (3, 0, jnp.where(live & (x > 0), place - 1, -1)),
+    )
+    for j, vx, at in shifted:
+        hot = jnp.where(iota((LAYERS * PLANE, place.shape[1]), 0) == at, 1.0, 0.0).astype(BF16)
+        for layer, z in enumerate(planes):
+            first = (vx * 4 + z % 2 * 2) * depth
+            both = dot(hot[layer * PLANE : (layer + 1) * PLANE], table[:, first : first + 2 * depth]).astype(BF16)
+            for vy in range(2):
+                planes_ref[vy, layer, OCT : OCT + PLANE, j * depth : (j + 1) * depth] = both[
+                    :, vy * depth : (vy + 1) * depth
+                ]
+
+
 def place_kernel(offsets, padded, pairs, *refs):
     groups = len(offsets)
     pooled_refs, w_ref = refs[:groups], refs[groups]
-    grid_ref, place_ref, pair_ref, step_ref = refs[groups + 1 : groups + 5]
-    table = refs[groups + 5]
+    faces_ref, table, place_ref, pair_ref, step_ref = refs[groups + 1 : groups + 6]
     depth = pooled_refs[0].shape[1]
     lane_count = groups * 128
     me = lax.axis_index("ga")
@@ -265,33 +289,16 @@
             if padded < 128:
                 table[k * 128 + padded : (k + 1) * 128, lanes] = jnp.zeros((128 - padded, depth), BF16)
 
-    grid_ref[:, :, 0:OCT, :] = jnp.zeros((2, RZ_REG, OCT, 4 * depth), BF16)
-    grid_ref[:, :, OCT + PLANE :, :] = jnp.zeros((2, RZ_REG, OCT, 4 * depth), BF16)
-    shifted = (
-        (0, 1, jnp.where(live & (x < OCT - 1), place + 1, -1)),
-        (1, 0, place),
-        (2, 1, place),
-        (3, 0, jnp.where(live & (x > 0), place - 1, -1)),
-    )
-    for j, vx, at in shifted:
-        hot = jnp.where(iota((LAYERS * PLANE, lane_count), 0) == at, 1.0, 0.0).astype(BF16)
-        for vz in range(2):
-            first = (vx * 4 + vz * 2) * depth
-            both = dot(hot, table[:, first : first + 2 * depth]).astype(BF16)
-            for vy in range(2):
-                for layer in range(LAYERS):
-                    grid_ref[vy, layer * 2 + vz, OCT : OCT + PLANE, j * depth : (j + 1) * depth] = both[
-                        layer * PLANE : (layer + 1) * PLANE, vy * depth : (vy + 1) * depth
-                    ]
+    fill_planes(faces_ref, OUTER, place, table)
 
     even = row % 2 == 0
     for out_ref, up in ((pair_ref, even), (step_ref, jnp.logical_not(even))):
-        plane = jnp.where(up, RZ_REG - 1, 0)
+        plane = jnp.where(up, 1, 0)
         dz = jnp.where(up, 0, 2)
         total = None
         for j in range(4):
             vy, first = y_window(j)
-            part = dot(grid_ref[vy, plane, first : first + PLANE, :], w_ref[dz, j])
+            part = dot(faces_ref[vy, plane, first : first + PLANE, :], w_ref[dz, j])
             total = part if total is None else total + part
         out_ref[...] = total.astype(BF16)
 
@@ -303,44 +310,48 @@
     return pl.pallas_call(
         functools.partial(place_kernel, offsets, padded, pairs),
         in_specs=[VMEM] * (groups + 1),
-        out_specs=[VMEM] * 4,
+        out_specs=[VMEM] * 5,
         out_shape=[
-            jax.ShapeDtypeStruct((2, RZ_REG, BORDERED, 4 * depth), BF16),
+            jax.ShapeDtypeStruct((2, LAYERS, BORDERED, 4 * depth), BF16),
+            jax.ShapeDtypeStruct((groups * 128, SUBS * depth), BF16),
             jax.ShapeDtypeStruct((8, groups * 128), jnp.int32),
             jax.ShapeDtypeStruct((PLANE, wide), BF16),
             jax.ShapeDtypeStruct((PLANE, wide), BF16),
         ],
-        scratch_shapes=[pltpu.VMEM((groups * 128, SUBS * depth), BF16)],
-        compiler_params=params(24),
-        cost_estimate=cost(2 << 28, 6 << 20),
+        compiler_params=params(16),
+        cost_estimate=cost(1 << 28, 6 << 20),
         name="place",
     )(*pooled, folded)
 
 
-def conv_kernel(grid_ref, w_ref, out_ref):
+def conv_kernel(faces_ref, table_ref, place_ref, w_ref, out_ref, inside):
+    fill_planes(inside, INNER, place_ref[0:1, :], table_ref)
     for z in range(RZ_REG):
         total = None
         for a in range(3):
-            if not 0 <= z + a - 1 < RZ_REG:
+            source = z + a - 1
+            if not 0 <= source < RZ_REG:
                 continue
+            planes = inside if source in INNER else faces_ref
             for j in range(4):
                 vy, first = y_window(j)
-                part = dot(grid_ref[vy, z + a - 1, first : first + PLANE, :], w_ref[a, j])
+                part = dot(planes[vy, source // 2, first : first + PLANE, :], w_ref[a, j])
                 total = part if total is None else total + part
         out_ref[z] = total
 
 
-def conv(grid, folded):
+def conv(faces, table, places, folded):
     wide = folded.shape[3]
     return pl.pallas_call(
         conv_kernel,
-        in_specs=[VMEM, VMEM],
+        in_specs=[VMEM] * 4,
         out_specs=VMEM,
         out_shape=jax.ShapeDtypeStruct((RZ_REG, PLANE, wide), F32),
-        compiler_params=params(16),
+        scratch_shapes=[pltpu.VMEM(faces.shape, BF16)],
+        compiler_params=params(20),
         cost_estimate=cost(10 * 4 * PLANE * 512 * 256, 6 << 20),
         name="conv",
-    )(grid, folded)
+    )(faces, table, places, folded)
 
 
 def finish_kernel(padded, order, place_ref, sums_ref, pair_ref, step_ref, bias_ref, *refs):
@@ -542,7 +553,7 @@
         bit //= 2
     offsets = tuple(offsets)
 
-    grid, places, pair, step = place(gathered, offsets, folded, padded, pairs)
+    faces, table, places, pair, step = place(gathered, offsets, folded, padded, pairs)
     pair_swap = [(i, i ^ 1) for i in range(rows) if i ^ 1 < rows]
     step_swap = []
     for i in range(rows):
@@ -552,7 +563,7 @@
             step_swap.append((i * groups + j, target))
     pair = lax.ppermute(pair, "row", pair_swap)
     step = lax.ppermute(step, ("row", "ga"), step_swap)
-    sums = conv(grid, folded)
+    sums = conv(faces, table, places, folded)
     order = sorted(range(groups), key=lambda k: (offsets[k] > 0, offsets[k] < groups // 2, offsets[k]))
     root, empty, *sends = finish(places, sums, pair, step, root_bias, order, padded)
     come = sends[:1]

time: 40.2 us -> 39.7 us (0.988)
  waiting for transfers between devices: 9.77 us -> 9.17 us
    pallas_call x1, Pallas kernels: 2.86 us -> 3.45 us  [conv(): pl.pallas_call(conv_kernel, in_specs=[VMEM] * 4, out_specs=VMEM, out_shap...]
    pallas_call x1, Pallas kernels: 2.11 us -> 1.56 us  [place(): pl.pallas_call(functools.partial(place_kernel, offsets, padded, pairs), i...]
    ppermute x1, waiting for transfers between devices: 0.47 us -> 0.01 us  [shards(): pair = lax.ppermute(pair, 'row', pair_swap)]
  transfers between devices with their start and end apart: 8 -> 8, of which waited for: 5 -> 4; matrix products, arithmetic and copies ran while one was open for 0% -> 0% of each run, Pallas kernels for 15% -> 17%
where the time goes in v5:
time: 39.7 us; the launch traced here: 39.3 us
  Pallas kernels  20.3 us (51%)
  waiting for transfers between devices  9.17 us (23%)
  starting transfers between devices  9.01 us (23%)
  between operations  0.77 us (2%)
    pallas_call x1, Pallas kernels, fine_in(): pl.pallas_call(functools.partial(fine_in_kernel, total=total, padded=padd...  7.03 us
    pallas_call x1, Pallas kernels, fine_out(): pl.pallas_call(functools.partial(fine_out_kernel, groups), in_specs=[VMEM...  4.35 us
    ppermute x3, waiting for transfers between devices, shards(): gathered += [lax.ppermute(part, 'ga', swap) for part in gathered]  4.27 us
    ppermute x3, starting transfers between devices, shards(): lax.ppermute(send, 'ga', [(i, i ^ offsets[k]) for i in range(groups)])  3.82 us
    ppermute x3, starting transfers between devices, shards(): gathered += [lax.ppermute(part, 'ga', swap) for part in gathered]  3.78 us
    pallas_call x1, Pallas kernels, conv(): pl.pallas_call(conv_kernel, in_specs=[VMEM] * 4, out_specs=VMEM, out_shap...  3.45 us
    ppermute x3, waiting for transfers between devices, shards(): lax.ppermute(send, 'ga', [(i, i ^ offsets[k]) for i in range(groups)])  3.12 us
    pallas_call x1, Pallas kernels, unravel(): pl.pallas_call(functools.partial(unravel_kernel, offsets), in_specs=[VMEM...  1.8 us
  transfers between devices with their start and end apart: 8, of which 4 were waited for; matrix products, arithmetic and copies ran while one was open for 0% of the time, Pallas kernels for 17%

profile of v5, /device:TPU:25, one launch (start us, length us, event | category | flops | bytes accessed | tf_op | source)
XLA Modules:
  0.0 39.3 jit_solution(9048662359779696879)
XLA Ops:
  0.6 0.0 copy-start.1
  0.6 0.0 copy-start.3
  0.7 7.0 %fine_in.1 = (bf16[1792,256]{1,0:T(8,128)(2,1)}, bf16[912,128]{1,0:T(8,128)(2,1)}) custom-call(s32[1,112]{1,0:T(1,128)} %bitcast.13, s32[1,8]{1,0:T(1,128)} %bitcast.14, bf16[112,64,512]{2,1,0:T(8,128)(2,1)} %refs_0_.1, bf16[64,128]{1,0:T(8,128)(2,1)} %w_ref.1), custom_call_target="tpu_custom_call" | custom-call | flops 1879048192 | bytes 7340032 | tf_op jit(solution)/shard_map/fine_in/pallas_call | solution.py:151
  7.7 0.0 copy-start
  7.7 0.0 copy-start.4
  7.7 1.3 %collective-permute-start = (bf16[912,128]{1,0:T(8,128)(2,1)}, bf16[912,128]{1,0:T(8,128)(2,1)S(1)}, u32[]{:S(2)}, u32[]{:S(2)}) collective-permute-start(bf16[912,128]{1,0:T(8,128)(2,1)} %get-tuple-element.22.refs_0_), channel_id=1, source_target_pairs={{0,2},{1,3},{2,0},{3,1},{4,6},{5,7},{6,4},{7,5},{8,10},{9,11},{10,... | collective-permute-start | bytes 700424 | tf_op jit(solution)/shard_map/ppermute | solution.py:549
  9.0 1.0 %collective-permute-start.1 = (bf16[912,128]{1,0:T(8,128)(2,1)}, bf16[912,128]{1,0:T(8,128)(2,1)S(1)}, u32[]{:S(2)}, u32[]{:S(2)}) collective-permute-start(bf16[912,128]{1,0:T(8,128)(2,1)} %get-tuple-element.22.refs_0_), channel_id=1, source_target_pairs={{0,1},{1,0},{2,3},{3,2},{4,5},{5,4},{6,7},{7,6},{8,9},{9,8},{10,11... | collective-permute-start | bytes 700424 | tf_op jit(solution)/shard_map/ppermute | solution.py:549
  10.0 0.0 copy-done.1
  10.0 0.0 copy-done.3
  10.0 0.0 copy-start.2
  10.0 0.8 %fold.1.refs_4_.w_ref = bf16[3,4,512,256]{3,2,1,0:T(8,128)(2,1)S(1)} custom-call(bf16[3,3,3,64,256]{4,3,2,1,0:T(8,128)(2,1)S(1)} %bitcast.10, bf16[128,256]{1,0:T(8,128)(2,1)S(1)} %copy-done.3), custom_call_target="tpu_custom_call" | custom-call | flops 301989888 | bytes 6291456 | tf_op jit(solution)/shard_map/fold/pallas_call | solution.py:220
  10.7 0.0 copy-done
  10.7 0.0 copy-done.4
  10.8 0.7 %hide.1.refs_1_ = bf16[1792,512]{1,0:T(8,128)(2,1)S(1)} custom-call(bf16[1792,256]{1,0:T(8,128)(2,1)S(1)} %copy-done, bf16[64,128]{1,0:T(8,128)(2,1)S(1)} %copy-done.4), custom_call_target="tpu_custom_call" | custom-call | flops 469762048 | bytes 2752512 | tf_op jit(solution)/shard_map/hide/pallas_call | solution.py:187
  11.4 3.1 %collective-permute-done.refs_1_ = bf16[912,128]{1,0:T(8,128)(2,1)S(1)} collective-permute-done((bf16[912,128]{1,0:T(8,128)(2,1)}, bf16[912,128]{1,0:T(8,128)(2,1)S(1)}, u32[]{:S(2)}, u32[]{:S(2)}) %collective-permute-start) | collective-permute-done | bytes 233504 | tf_op jit(solution)/shard_map/ppermute | solution.py:549
  14.6 1.5 %collective-permute-start.2 = (bf16[912,128]{1,0:T(8,128)(2,1)S(1)}, bf16[912,128]{1,0:T(8,128)(2,1)S(1)}, u32[]{:S(2)}, u32[]{:S(2)}) collective-permute-start(bf16[912,128]{1,0:T(8,128)(2,1)S(1)} %collective-permute-done.refs_1_), channel_id=1, source_target_pairs={{0,1},{1,0},{2,3},{3,2},{4,5},{5,4},{6,7},{7,6},{8,9},{9,8},{10,11... | collective-permute-start | bytes 700424 | tf_op jit(solution)/shard_map/ppermute | solution.py:549
  16.1 0.0 collective-permute-done.1.refs_2_
  16.1 1.1 %collective-permute-done.2.refs_3_ = bf16[912,128]{1,0:T(8,128)(2,1)S(1)} collective-permute-done((bf16[912,128]{1,0:T(8,128)(2,1)S(1)}, bf16[912,128]{1,0:T(8,128)(2,1)S(1)}, u32[]{:S(2)}, u32[]{:S(2)}) %collective-permute-start.2) | collective-permute-done | bytes 233504 | tf_op jit(solution)/shard_map/ppermute | solution.py:549
  17.2 0.0 copy-done.2
  17.2 1.6 %place.1 = (bf16[2,2,288,512]{3,2,1,0:T(8,128)(2,1)S(1)}, bf16[512,1024]{1,0:T(8,128)(2,1)S(1)}, s32[8,512]{1,0:T(8,128)S(1)}, bf16[256,256]{1,0:T(8,128)(2,1)S(1)}, bf16[256,256]{1,0:T(8,128)(2,1)S(1)}) custom-call(bf16[912,128]{1,0:T(8,128)(2,1)S(1)} %copy-done.2, bf16[912,128]{1,0:T(8,128)(2,1)S(1)} %collective-permute-done.refs_1_, ...), custom_call_target="tpu_custom_call" | custom-call | flops 536870912 | bytes 6291456 | tf_op jit(solution)/shard_map/place/pallas_call | solution.py:310
  18.8 1.3 %collective-permute-start.3 = (bf16[256,256]{1,0:T(8,128)(2,1)S(1)}, bf16[256,256]{1,0:T(8,128)(2,1)S(1)}, u32[]{:S(2)}, u32[]{:S(2)}) collective-permute-start(bf16[256,256]{1,0:T(8,128)(2,1)S(1)} %get-tuple-element.30), channel_id=1, source_target_pairs={{0,4},{4,0},{8,12},{12,8},{16,20},{20,16},{24,28},{28,24},{1,5},{5... | collective-permute-start | bytes 393224 | tf_op jit(solution)/shard_map/ppermute | solution.py:564
  20.1 0.1 collective-permute-start.4
  20.2 0.0 slice-start
  20.2 0.0 copy-start.5
  20.2 0.0 copy-start.6
  20.2 0.0 copy-start.7
  20.2 0.0 slice-start.1
  20.2 3.5 %conv.1.sums_ref = f32[4,256,256]{2,1,0:T(8,128)S(1)} custom-call(bf16[2,2,288,512]{3,2,1,0:T(8,128)(2,1)S(1)} %get-tuple-element.28.faces_ref, bf16[512,1024]{1,0:T(8,128)(2,1)S(1)} %get-tuple-element.29.table_ref, s32[8,512]{1,0:T(8,128)S(1)} %get-tuple-element.27.place_ref, bf16[3,4,512,256]{3,2,1,0:T(8,128)(2,1)S(1)} %fold.1.refs_4_.w_ref), custom_call_target="tpu_custom_call" | custom-call | flops 2684354560 | bytes 6291456 | tf_op jit(solution)/shard_map/conv/pallas_call | solution.py:345
  23.7 0.0 collective-permute-done.3.pair_ref
  23.7 1.8 %collective-permute-done.4.step_ref = bf16[256,256]{1,0:T(8,128)(2,1)S(1)} collective-permute-done((bf16[256,256]{1,0:T(8,128)(2,1)S(1)}, bf16[256,256]{1,0:T(8,128)(2,1)S(1)}, u32[]{:S(2)}, u32[]{:S(2)}) %collective-permute-start.4) | collective-permute-done | bytes 131104 | tf_op jit(solution)/shard_map/ppermute | solution.py:565
  25.5 0.0 copy-done.5
  25.5 0.7 %finish.1 = (bf16[2,512,256]{2,1,0:T(8,128)(2,1)S(1)}, f32[112,128]{1,0:T(8,128)S(1)}, bf16[112,512]{1,0:T(8,128)(2,1)S(1)}, bf16[112,512]{1,0:T(8,128)(2,1)S(1)...) custom-call(s32[8,512]{1,0:T(8,128)S(1)} %get-tuple-element.27.place_ref, f32[4,256,256]{2,1,0:T(8,128)S(1)} %conv.1.sums_ref, ...), custom_call_target="tpu_custom_call" | custom-call | flops 268435456 | bytes 3145728 | tf_op jit(solution)/shard_map/finish/pallas_call | solution.py:390
  26.2 1.3 %collective-permute-start.5 = (bf16[112,512]{1,0:T(8,128)(2,1)S(1)}, bf16[112,512]{1,0:T(8,128)(2,1)S(1)}, u32[]{:S(2)}, u32[]{:S(2)}) collective-permute-start(bf16[112,512]{1,0:T(8,128)(2,1)S(1)} %get-tuple-element.38), channel_id=1, source_target_pairs={{0,2},{1,3},{2,0},{3,1},{4,6},{5,7},{6,4},{7,5},{8,10},{9,11},{10,... | collective-permute-start | bytes 344072 | tf_op jit(solution)/shard_map/ppermute | solution.py:571
  27.5 2.5 %collective-permute-start.6 = (bf16[112,512]{1,0:T(8,128)(2,1)S(1)}, bf16[112,512]{1,0:T(8,128)(2,1)S(1)}, u32[]{:S(2)}, u32[]{:S(2)}) collective-permute-start(bf16[112,512]{1,0:T(8,128)(2,1)S(1)} %get-tuple-element.39), channel_id=1, source_target_pairs={{0,3},{1,2},{2,1},{3,0},{4,7},{5,6},{6,5},{7,4},{8,11},{9,10},{10,... | collective-permute-start | bytes 344072 | tf_op jit(solution)/shard_map/ppermute | solution.py:571
  30.0 0.0 collective-permute-start.7
  30.0 0.0 copy-done.6
  30.0 0.0 copy-done.7
  30.0 1.8 %unravel.1 = (bf16[4,16,2,32,64]{4,3,2,1,0:T(8,128)(2,1)}, bf16[512,256]{1,0:T(8,128)(2,1)S(1)}, bf16[512,256]{1,0:T(8,128)(2,1)S(1)}, bf16[64,512]{1,0:T(8,128)(2,1)S(1)}) custom-call(bf16[2,512,256]{2,1,0:T(8,128)(2,1)S(1)} %get-tuple-element.33.root_ref, bf16[256,128]{1,0:T(8,128)(2,1)S(1)} %copy-done.6, bf16[64,128]{1,0:T(8,128)(2,1)S(1)} %bitcast.12), custom_call_target="tpu_custom_call" | custom-call | flops 536870912 | bytes 2097152 | tf_op jit(solution)/shard_map/unravel/pallas_call | solution.py:441
  31.8 0.0 collective-permute-done.5.refs_7_
  31.8 3.1 %collective-permute-done.6.refs_8_ = bf16[112,512]{1,0:T(8,128)(2,1)S(1)} collective-permute-done((bf16[112,512]{1,0:T(8,128)(2,1)S(1)}, bf16[112,512]{1,0:T(8,128)(2,1)S(1)}, u32[]{:S(2)}, u32[]{:S(2)}) %collective-permute-start.6) | collective-permute-done | bytes 114720 | tf_op jit(solution)/shard_map/ppermute | solution.py:571
  34.9 0.0 collective-permute-done.7.refs_9_
  35.0 0.0 slice-done
  35.0 0.0 slice-done.1
  35.0 4.4 %fine_out.1 = bf16[112,64,512]{2,1,0:T(8,128)(2,1)} custom-call(bf16[112,64,512]{2,1,0:T(8,128)(2,1)S(1)} %bitcast.9, bf16[1792,512]{1,0:T(8,128)(2,1)S(1)} %hide.1.refs_1_, f32[112,128]{1,0:T(8,128)S(1)} %get-tuple-element.32.refs_2_, bf16[512,256]{1,0:T(8,128)(2,1)S(1)} %get-tuple-element.34.refs_3_, bf16[512,256]{1,0:T(8,128)(2,1)S(1)} %get-tuple-element.35.refs_4_, ...), custom_call_target="tpu_custom_call" | custom-call | flops 1879048192 | bytes 14680064 | tf_op jit(solution)/shard_map/fine_out/pallas_call | solution.py:514
  (1 shorter events, 0.0 us)
Async XLA Ops:
  0.6 9.3 %copy-start.1 = (bf16[64,256,3,3,3]{1,0,4,3,2:T(8,128)(2,1)S(1)}, bf16[64,256,3,3,3]{1,0,4,3,2:T(8,128)(2,1)}, u32[]{:S(2)}) copy-start(bf16[64,256,3,3,3]{1,0,4,3,2:T(8,128)(2,1)} %param.14) | copy-start | bytes 2654212
  0.6 9.3 %copy-start.3 = (bf16[128,256]{1,0:T(8,128)(2,1)S(1)}, bf16[128,256]{1,0:T(8,128)(2,1)}, u32[]{:S(2)}) copy-start(bf16[128,256]{1,0:T(8,128)(2,1)} %in_ref.1) | copy-start | bytes 196612
  7.7 3.0 %copy-start = (bf16[1792,256]{1,0:T(8,128)(2,1)S(1)}, bf16[1792,256]{1,0:T(8,128)(2,1)}, u32[]{:S(2)}) copy-start(bf16[1792,256]{1,0:T(8,128)(2,1)} %get-tuple-element.23.turned_ref) | copy-start | bytes 2752516
  7.7 3.0 %copy-start.4 = (bf16[64,128]{1,0:T(8,128)(2,1)S(1)}, bf16[64,128]{1,0:T(8,128)(2,1)}, u32[]{:S(2)}) copy-start(bf16[64,128]{1,0:T(8,128)(2,1)} %w_ref.1) | copy-start | bytes 49156
  7.7 6.8 %collective-permute-start = (bf16[912,128]{1,0:T(8,128)(2,1)}, bf16[912,128]{1,0:T(8,128)(2,1)S(1)}, u32[]{:S(2)}, u32[]{:S(2)}) collective-permute-start(bf16[912,128]{1,0:T(8,128)(2,1)} %get-tuple-element.22.refs_0_), channel_id=1, source_target_pairs={{0,2},{1,3},{2,0},{3,1},{4,6},{5,7},{6,4},{7,5},{8,10},{9,11},{10,... | collective-permute-start | bytes 700424 | tf_op jit(solution)/shard_map/ppermute | solution.py:549
  9.0 7.1 %collective-permute-start.1 = (bf16[912,128]{1,0:T(8,128)(2,1)}, bf16[912,128]{1,0:T(8,128)(2,1)S(1)}, u32[]{:S(2)}, u32[]{:S(2)}) collective-permute-start(bf16[912,128]{1,0:T(8,128)(2,1)} %get-tuple-element.22.refs_0_), channel_id=1, source_target_pairs={{0,1},{1,0},{2,3},{3,2},{4,5},{5,4},{6,7},{7,6},{8,9},{9,8},{10,11... | collective-permute-start | bytes 700424 | tf_op jit(solution)/shard_map/ppermute | solution.py:549
  10.0 7.3 %copy-start.2 = (bf16[912,128]{1,0:T(8,128)(2,1)S(1)}, bf16[912,128]{1,0:T(8,128)(2,1)}, u32[]{:S(2)}) copy-start(bf16[912,128]{1,0:T(8,128)(2,1)} %get-tuple-element.22.refs_0_) | copy-start | bytes 700420
  14.6 2.7 %collective-permute-start.2 = (bf16[912,128]{1,0:T(8,128)(2,1)S(1)}, bf16[912,128]{1,0:T(8,128)(2,1)S(1)}, u32[]{:S(2)}, u32[]{:S(2)}) collective-permute-start(bf16[912,128]{1,0:T(8,128)(2,1)S(1)} %collective-permute-done.refs_1_), channel_id=1, source_target_pairs={{0,1},{1,0},{2,3},{3,2},{4,5},{5,4},{6,7},{7,6},{8,9},{9,8},{10,11... | collective-permute-start | bytes 700424 | tf_op jit(solution)/shard_map/ppermute | solution.py:549
  18.8 4.9 %collective-permute-start.3 = (bf16[256,256]{1,0:T(8,128)(2,1)S(1)}, bf16[256,256]{1,0:T(8,128)(2,1)S(1)}, u32[]{:S(2)}, u32[]{:S(2)}) collective-permute-start(bf16[256,256]{1,0:T(8,128)(2,1)S(1)} %get-tuple-element.30), channel_id=1, source_target_pairs={{0,4},{4,0},{8,12},{12,8},{16,20},{20,16},{24,28},{28,24},{1,5},{5... | collective-permute-start | bytes 393224 | tf_op jit(solution)/shard_map/ppermute | solution.py:564
  20.1 5.4 %collective-permute-start.4 = (bf16[256,256]{1,0:T(8,128)(2,1)S(1)}, bf16[256,256]{1,0:T(8,128)(2,1)S(1)}, u32[]{:S(2)}, u32[]{:S(2)}) collective-permute-start(bf16[256,256]{1,0:T(8,128)(2,1)S(1)} %get-tuple-element.31), channel_id=1, source_target_pairs={{0,1},{1,0},{2,3},{3,2},{4,8},{5,9},{6,10},{7,11},{8,4},{9,5},{10,... | collective-permute-start | bytes 393224 | tf_op jit(solution)/shard_map/ppermute | solution.py:565
  20.2 14.7 %slice-start = ((s8[7340032]{0:T(1024)(128)(4,1)}), s8[4194304]{0:T(1024)(128)(4,1)S(1)}, s32[]{:S(2)}) async-start(s8[7340032]{0:T(1024)(128)(4,1)} %bitcast.8), calls=%async_computation | async-start | bytes 8388608
  20.2 5.3 %copy-start.5 = (f32[64]{0:T(128)S(1)}, f32[64]{0:T(128)}, u32[]{:S(2)}) copy-start(f32[64]{0:T(128)} %param.15) | copy-start | bytes 772
  20.2 9.8 %copy-start.6 = (bf16[256,128]{1,0:T(8,128)(2,1)S(1)}, bf16[256,128]{1,0:T(8,128)(2,1)}, u32[]{:S(2)}) copy-start(bf16[256,128]{1,0:T(8,128)(2,1)} %down_ref.1) | copy-start | bytes 196612
  20.2 9.8 %copy-start.7 = (bf16[128,64]{0,1:T(8,128)(2,1)S(1)}, bf16[128,64]{0,1:T(8,128)(2,1)}, u32[]{:S(2)}) copy-start(bf16[128,64]{0,1:T(8,128)(2,1)} %param.17) | copy-start | bytes 49156
  20.2 14.7 %slice-start.1 = ((s8[7340032]{0:T(1024)(128)(4,1)}), s8[3145728]{0:T(1024)(128)(4,1)S(1)}, s32[]{:S(2)}) async-start(s8[7340032]{0:T(1024)(128)(4,1)} %bitcast.8), calls=%async_computation.1 | async-start | bytes 6291456
  26.2 5.6 %collective-permute-start.5 = (bf16[112,512]{1,0:T(8,128)(2,1)S(1)}, bf16[112,512]{1,0:T(8,128)(2,1)S(1)}, u32[]{:S(2)}, u32[]{:S(2)}) collective-permute-start(bf16[112,512]{1,0:T(8,128)(2,1)S(1)} %get-tuple-element.38), channel_id=1, source_target_pairs={{0,2},{1,3},{2,0},{3,1},{4,6},{5,7},{6,4},{7,5},{8,10},{9,11},{10,... | collective-permute-start | bytes 344072 | tf_op jit(solution)/shard_map/ppermute | solution.py:571
  27.5 7.4 %collective-permute-start.6 = (bf16[112,512]{1,0:T(8,128)(2,1)S(1)}, bf16[112,512]{1,0:T(8,128)(2,1)S(1)}, u32[]{:S(2)}, u32[]{:S(2)}) collective-permute-start(bf16[112,512]{1,0:T(8,128)(2,1)S(1)} %get-tuple-element.39), channel_id=1, source_target_pairs={{0,3},{1,2},{2,1},{3,0},{4,7},{5,6},{6,5},{7,4},{8,11},{9,10},{10,... | collective-permute-start | bytes 344072 | tf_op jit(solution)/shard_map/ppermute | solution.py:571
  30.0 4.9 %collective-permute-start.7 = (bf16[112,512]{1,0:T(8,128)(2,1)S(1)}, bf16[112,512]{1,0:T(8,128)(2,1)S(1)}, u32[]{:S(2)}, u32[]{:S(2)}) collective-permute-start(bf16[112,512]{1,0:T(8,128)(2,1)S(1)} %get-tuple-element.40), channel_id=1, source_target_pairs={{0,1},{1,0},{2,3},{3,2},{4,5},{5,4},{6,7},{7,6},{8,9},{9,8},{10,11... | collective-permute-start | bytes 344072 | tf_op jit(solution)/shard_map/ppermute | solution.py:571

commit v6 on v5

--- a/solution.py
+++ b/solution.py
@@ -19,6 +19,7 @@
 OUTER = (0, 3)
 BORDERED = PLANE + 2 * OCT
 SUBS = 8
+HALVES = SUBS // 2
 META = 16
 BF16 = jnp.bfloat16
 F32 = jnp.float32
@@ -73,7 +74,7 @@
 
 
 def fine_in_kernel(
-    child_hbm, block_hbm, fine_hbm, w_hbm, turned_hbm, pooled_ref,
+    child_hbm, block_hbm, fine_hbm, w_hbm, turned_hbm, pooled_ref, rest_ref,
     fine_ref, child_ref, block_ref, w_ref, pool, weights, turned, tops, meta, fine_sems, turned_sems, sems, *, total, padded
 ):
     _, width, voxels = fine_ref.shape
@@ -112,10 +113,22 @@
     meta[0:1, 0:total] = (child_ref[...] >> 3).astype(F32)
     meta[1:2, 0:total] = (child_ref[...] & 7).astype(F32)
     meta[2:3, 0 : block_ref.shape[1]] = block_ref[...].astype(F32)
-    pooled_ref[SUBS * padded : SUBS * padded + META, :] = meta[...].astype(BF16)
+    pooled_ref[HALVES * padded : HALVES * padded + META, :] = meta[...].astype(BF16)
+
+    def project(low, high):
+        rows = turned[low * sets * cells : high * sets * cells, :]
+        hidden = jnp.maximum(dot(rows, weights[...]), 0.0).astype(BF16)
+        cubes = hidden.astype(F32).reshape((high - low) * sets, SUBS, SUBS, group * depth)
+        top = jnp.sum(cubes, axis=1) * (1.0 / SUBS)
+        for g in range((high - low) * sets):
+            for s in range(group):
+                at = (low * chunk + g * group + s) * SUBS
+                tops[at : at + SUBS, :] = top[g, :, s * depth : (s + 1) * depth]
 
     runs = run_bounds(total // chunk)
     for low, high in runs:
+        if low and high == total // chunk:
+            project(0, low)
         for i in range(low, high):
             fetch(i).wait()
         cube = fine_ref[low * chunk : high * chunk].reshape((high - low) * chunk * width, voxels)
@@ -124,19 +137,13 @@
             at = (low * sets + g) * cells
             turned[at : at + cells, :] = octants[g * group * width : (g + 1) * group * width].T
         store(low, high).start()
-    for low, high in runs:
-        rows = turned[low * sets * cells : high * sets * cells, :]
-        hidden = jnp.maximum(dot(rows, weights[...]), 0.0).astype(BF16)
-        cubes = hidden.astype(F32).reshape((high - low) * sets, SUBS, SUBS, group * depth)
-        top = jnp.sum(cubes, axis=1) * (1.0 / SUBS)
-        for g in range((high - low) * sets):
-            for s in range(group):
-                at = (low * chunk + g * group + s) * SUBS
-                tops[at : at + SUBS, :] = top[g, :, s * depth : (s + 1) * depth]
+    project(*runs[-1])
     if padded != total:
         tops[total * SUBS :, :] = jnp.zeros(((padded - total) * SUBS, depth), F32)
     for v in range(SUBS):
-        pooled_ref[v * padded : (v + 1) * padded, :] = tops[pl.ds(v, padded, stride=SUBS), :].astype(BF16)
+        half_ref = pooled_ref if v < HALVES else rest_ref
+        first = v % HALVES * padded
+        half_ref[first : first + padded, :] = tops[pl.ds(v, padded, stride=SUBS), :].astype(BF16)
     for low, high in runs:
         store(low, high).wait()
 
@@ -151,10 +158,11 @@
     return pl.pallas_call(
         functools.partial(fine_in_kernel, total=total, padded=padded),
         in_specs=[ANY] * 4,
-        out_specs=[ANY, VMEM],
+        out_specs=[ANY, VMEM, VMEM],
         out_shape=[
             jax.ShapeDtypeStruct((total // group * cells, group * width), BF16),
-            jax.ShapeDtypeStruct((SUBS * padded + META, depth), BF16),
+            jax.ShapeDtypeStruct((HALVES * padded + META, depth), BF16),
+            jax.ShapeDtypeStruct((HALVES * padded, depth), BF16),
         ],
         scratch_shapes=[
             pltpu.VMEM(fine_feats.shape, BF16),
@@ -257,14 +265,14 @@
 
 def place_kernel(offsets, padded, pairs, *refs):
     groups = len(offsets)
-    pooled_refs, w_ref = refs[:groups], refs[groups]
-    faces_ref, table, place_ref, pair_ref, step_ref = refs[groups + 1 : groups + 6]
+    pooled_refs, rest_refs, w_ref = refs[:groups], refs[groups : 2 * groups], refs[2 * groups]
+    faces_ref, table, place_ref, pair_ref, step_ref = refs[2 * groups + 1 :]
     depth = pooled_refs[0].shape[1]
     lane_count = groups * 128
     me = lax.axis_index("ga")
     row = lax.axis_index("row")
 
-    metas = [r[SUBS * padded : SUBS * padded + META, :] for r in pooled_refs]
+    metas = [r[HALVES * padded : HALVES * padded + META, :] for r in pooled_refs]
     parent = jnp.concatenate([m[0:1].astype(F32) for m in metas], axis=1).astype(jnp.int32)
     octant = jnp.concatenate([m[1:2].astype(F32) for m in metas], axis=1).astype(jnp.int32)
     found = jnp.zeros((META, lane_count), F32)
@@ -281,11 +289,12 @@
     place = jnp.where(live, (z * OCT + y) * OCT + x, -1)
     place_ref[...] = jnp.broadcast_to(place, place_ref.shape)
 
-    for k, pooled_ref in enumerate(pooled_refs):
+    for k in range(groups):
         for v in range(SUBS):
+            half_ref, first = (pooled_refs, rest_refs)[v // HALVES][k], v % HALVES * padded
             vz, vy, vx = v >> 2, v >> 1 & 1, v & 1
             lanes = slice((vx * 4 + vz * 2 + vy) * depth, (vx * 4 + vz * 2 + vy + 1) * depth)
-            table[k * 128 : k * 128 + padded, lanes] = pooled_ref[v * padded : (v + 1) * padded, :]
+            table[k * 128 : k * 128 + padded, lanes] = half_ref[first : first + padded, :]
             if padded < 128:
                 table[k * 128 + padded : (k + 1) * 128, lanes] = jnp.zeros((128 - padded, depth), BF16)
 
@@ -303,13 +312,13 @@
         out_ref[...] = total.astype(BF16)
 
 
-def place(pooled, offsets, folded, padded, pairs):
+def place(pooled, rest, offsets, folded, padded, pairs):
     groups = len(offsets)
     depth = pooled[0].shape[1]
     wide = folded.shape[3]
     return pl.pallas_call(
         functools.partial(place_kernel, offsets, padded, pairs),
-        in_specs=[VMEM] * (groups + 1),
+        in_specs=[VMEM] * (2 * groups + 1),
         out_specs=[VMEM] * 5,
         out_shape=[
             jax.ShapeDtypeStruct((2, LAYERS, BORDERED, 4 * depth), BF16),
@@ -321,7 +330,7 @@
         compiler_params=params(16),
         cost_estimate=cost(1 << 28, 6 << 20),
         name="place",
-    )(*pooled, folded)
+    )(*pooled, *rest, folded)
 
 
 def conv_kernel(faces_ref, table_ref, place_ref, w_ref, out_ref, inside):
@@ -537,23 +546,24 @@
     padded = -(-slots // META) * META
     pairs = parent_block.shape[0]
 
-    turned, pooled = fine_in(fine_feats, fine_child, parent_block, w_parent, padded)
+    turned, pooled, rest = fine_in(fine_feats, fine_child, parent_block, w_parent, padded)
 
     hidden = hide(turned, w_parent)
     folded = fold(w_root, w_root_in)
 
-    gathered, offsets = [pooled], [0]
+    gathered, others, offsets = [pooled], [rest], [0]
     bit = groups // 2
     while bit:
         swap = [(i, i ^ bit) for i in range(groups)]
         gathered += [lax.ppermute(part, "ga", swap) for part in gathered]
+        others += [lax.ppermute(part, "ga", swap) for part in others]
         offsets += [offset ^ bit for offset in offsets]
         if bit == groups // 2:
-            gathered[1], folded, hidden = lax.optimization_barrier((gathered[1], folded, hidden))
+            others[1], folded, hidden = lax.optimization_barrier((others[1], folded, hidden))
         bit //= 2
     offsets = tuple(offsets)
 
-    faces, table, places, pair, step = place(gathered, offsets, folded, padded, pairs)
+    faces, table, places, pair, step = place(gathered, others, offsets, folded, padded, pairs)
     pair_swap = [(i, i ^ 1) for i in range(rows) if i ^ 1 < rows]
     step_swap = []
     for i in range(rows):

time: 39.7 us -> 39.4 us (level)
  waiting for transfers between devices: 9.17 us -> 5.89 us
  starting transfers between devices: 9.01 us -> 10.9 us
  local copies, waits for them, and re-layouts: 0.04 us -> 1.22 us
    ppermute x3, waiting for transfers between devices: 4.27 us -> 0.01 us  [shards(): gathered += [lax.ppermute(part, 'ga', swap) for part in gathered]]
    ppermute x0 -> x3, starting transfers between devices: none -> 2.01 us  [shards(): others += [lax.ppermute(part, 'ga', swap) for part in others]]
    unnamed x20 -> x22, local copies, waits for them, and re-layouts: 0.04 us -> 1.22 us
    ppermute x0 -> x3, waiting for transfers between devices: none -> 0.96 us  [shards(): others += [lax.ppermute(part, 'ga', swap) for part in others]]
  transfers between devices with their start and end apart: 8 -> 11, of which waited for: 4 -> 3; matrix products, arithmetic and copies ran while one was open for 0% -> 0% of each run, Pallas kernels for 17% -> 17%
where the time goes in v6:
time: 39.4 us; the launch traced here: 39.1 us
  Pallas kernels  20.3 us (52%)
  starting transfers between devices  10.9 us (28%)
  waiting for transfers between devices  5.89 us (15%)
  local copies, waits for them, and re-layouts  1.22 us (3%)
  between operations  0.76 us (2%)
    pallas_call x1, Pallas kernels, fine_in(): pl.pallas_call(functools.partial(fine_in_kernel, total=total, padded=padd...  6.99 us
    pallas_call x1, Pallas kernels, fine_out(): pl.pallas_call(functools.partial(fine_out_kernel, groups), in_specs=[VMEM...  4.35 us
    ppermute x3, starting transfers between devices, shards(): lax.ppermute(send, 'ga', [(i, i ^ offsets[k]) for i in range(groups)])  3.79 us
    ppermute x3, starting transfers between devices, shards(): gathered += [lax.ppermute(part, 'ga', swap) for part in gathered]  3.73 us
    pallas_call x1, Pallas kernels, conv(): pl.pallas_call(conv_kernel, in_specs=[VMEM] * 4, out_specs=VMEM, out_shap...  3.45 us
    ppermute x3, waiting for transfers between devices, shards(): lax.ppermute(send, 'ga', [(i, i ^ offsets[k]) for i in range(groups)])  3.12 us
    ppermute x3, starting transfers between devices, shards(): others += [lax.ppermute(part, 'ga', swap) for part in others]  2.01 us
    pallas_call x1, Pallas kernels, unravel(): pl.pallas_call(functools.partial(unravel_kernel, offsets), in_specs=[VMEM...  1.79 us
  transfers between devices with their start and end apart: 11, of which 3 were waited for; matrix products, arithmetic and copies ran while one was open for 0% of the time, Pallas kernels for 17%

profile of v6, /device:TPU:25, one launch (start us, length us, event | category | flops | bytes accessed | tf_op | source)
XLA Modules:
  0.0 39.1 jit_solution(10177398033125357347)
XLA Ops:
  0.6 0.0 copy-start.5
  0.6 0.0 copy-start.1
  0.7 0.0 copy-start.4
  0.7 7.0 %fine_in.1 = (bf16[1792,256]{1,0:T(8,128)(2,1)}, bf16[464,128]{1,0:T(8,128)(2,1)}, bf16[448,128]{1,0:T(8,128)(2,1)}) custom-call(s32[1,112]{1,0:T(1,128)} %bitcast.13, s32[1,8]{1,0:T(1,128)} %bitcast.14, bf16[112,64,512]{2,1,0:T(8,128)(2,1)} %refs_0_.1, bf16[64,128]{1,0:T(8,128)(2,1)} %w_ref.1), custom_call_target="tpu_custom_call" | custom-call | flops 1879048192 | bytes 7340032 | tf_op jit(solution)/shard_map/fine_in/pallas_call | solution.py:158
  7.7 1.3 %collective-permute-start.1 = (bf16[464,128]{1,0:T(8,128)(2,1)}, bf16[464,128]{1,0:T(8,128)(2,1)S(1)}, u32[]{:S(2)}, u32[]{:S(2)}) collective-permute-start(bf16[464,128]{1,0:T(8,128)(2,1)} %get-tuple-element.26.refs_0_), channel_id=1, source_target_pairs={{0,2},{1,3},{2,0},{3,1},{4,6},{5,7},{6,4},{7,5},{8,10},{9,11},{10,... | collective-permute-start | bytes 356360 | tf_op jit(solution)/shard_map/ppermute | solution.py:558
  8.9 0.3 collective-permute-start
  9.2 1.2 %collective-permute-start.4 = (bf16[448,128]{1,0:T(8,128)(2,1)}, bf16[448,128]{1,0:T(8,128)(2,1)S(1)}, u32[]{:S(2)}, u32[]{:S(2)}) collective-permute-start(bf16[448,128]{1,0:T(8,128)(2,1)} %get-tuple-element.23.refs_4_), channel_id=1, source_target_pairs={{0,1},{1,0},{2,3},{3,2},{4,5},{5,4},{6,7},{7,6},{8,9},{9,8},{10,11... | collective-permute-start | bytes 344072 | tf_op jit(solution)/shard_map/ppermute | solution.py:559
  10.4 0.0 collective-permute-start.2
  10.4 0.0 copy-done.5
  10.4 0.0 copy-start
  10.4 1.2 %copy-done = bf16[1792,256]{1,0:T(8,128)(2,1)S(1)} copy-done((bf16[1792,256]{1,0:T(8,128)(2,1)S(1)}, bf16[1792,256]{1,0:T(8,128)(2,1)}, u32[]{:S(2)}) %copy-start) | copy-done | bytes 917528
  11.6 0.0 copy-start.2
  11.6 0.0 copy-start.3
  11.6 0.7 %hide.1.refs_1_ = bf16[1792,512]{1,0:T(8,128)(2,1)S(1)} custom-call(bf16[1792,256]{1,0:T(8,128)(2,1)S(1)} %copy-done, bf16[64,128]{1,0:T(8,128)(2,1)S(1)} %copy-done.5), custom_call_target="tpu_custom_call" | custom-call | flops 469762048 | bytes 2752512 | tf_op jit(solution)/shard_map/hide/pallas_call | solution.py:195
  12.3 0.0 collective-permute-done.1.refs_1_
  12.3 2.4 %collective-permute-start.3 = (bf16[464,128]{1,0:T(8,128)(2,1)S(1)}, bf16[464,128]{1,0:T(8,128)(2,1)S(1)}, u32[]{:S(2)}, u32[]{:S(2)}) collective-permute-start(bf16[464,128]{1,0:T(8,128)(2,1)S(1)} %collective-permute-done.1.refs_1_), channel_id=1, source_target_pairs={{0,1},{1,0},{2,3},{3,2},{4,5},{5,4},{6,7},{7,6},{8,9},{9,8},{10,11... | collective-permute-start | bytes 356360 | tf_op jit(solution)/shard_map/ppermute | solution.py:558
  14.7 0.0 copy-done.1
  14.7 0.0 copy-done.4
  14.7 0.8 %fold.1.refs_8_.w_ref = bf16[3,4,512,256]{3,2,1,0:T(8,128)(2,1)S(1)} custom-call(bf16[3,3,3,64,256]{4,3,2,1,0:T(8,128)(2,1)S(1)} %bitcast.10, bf16[128,256]{1,0:T(8,128)(2,1)S(1)} %copy-done.4), custom_call_target="tpu_custom_call" | custom-call | flops 301989888 | bytes 6291456 | tf_op jit(solution)/shard_map/fold/pallas_call | solution.py:228
  15.5 0.0 collective-permute-done.refs_5_
  15.5 0.5 %collective-permute-start.5 = (bf16[448,128]{1,0:T(8,128)(2,1)S(1)}, bf16[448,128]{1,0:T(8,128)(2,1)S(1)}, u32[]{:S(2)}, u32[]{:S(2)}) collective-permute-start(bf16[448,128]{1,0:T(8,128)(2,1)S(1)} %collective-permute-done.refs_5_), channel_id=1, source_target_pairs={{0,1},{1,0},{2,3},{3,2},{4,5},{5,4},{6,7},{7,6},{8,9},{9,8},{10,11... | collective-permute-start | bytes 344072 | tf_op jit(solution)/shard_map/ppermute | solution.py:559
  16.0 0.0 collective-permute-done.4.refs_6_
  16.1 0.0 collective-permute-done.2.refs_2_
  16.1 1.0 %collective-permute-done.5.refs_7_ = bf16[448,128]{1,0:T(8,128)(2,1)S(1)} collective-permute-done((bf16[448,128]{1,0:T(8,128)(2,1)S(1)}, bf16[448,128]{1,0:T(8,128)(2,1)S(1)}, u32[]{:S(2)}, u32[]{:S(2)}) %collective-permute-start.5) | collective-permute-done | bytes 114720 | tf_op jit(solution)/shard_map/ppermute | solution.py:559
  17.0 0.0 collective-permute-done.3.refs_3_
  17.0 0.0 copy-done.2
  17.0 0.0 copy-done.3
  17.0 1.6 %place.1 = (bf16[2,2,288,512]{3,2,1,0:T(8,128)(2,1)S(1)}, bf16[512,1024]{1,0:T(8,128)(2,1)S(1)}, s32[8,512]{1,0:T(8,128)S(1)}, bf16[256,256]{1,0:T(8,128)(2,1)S(1)}, bf16[256,256]{1,0:T(8,128)(2,1)S(1)}) custom-call(bf16[464,128]{1,0:T(8,128)(2,1)S(1)} %copy-done.2, bf16[464,128]{1,0:T(8,128)(2,1)S(1)} %collective-permute-done.1.refs_1_, ...), custom_call_target="tpu_custom_call" | custom-call | flops 536870912 | bytes 6291456 | tf_op jit(solution)/shard_map/place/pallas_call | solution.py:319
  18.6 1.3 %collective-permute-start.6 = (bf16[256,256]{1,0:T(8,128)(2,1)S(1)}, bf16[256,256]{1,0:T(8,128)(2,1)S(1)}, u32[]{:S(2)}, u32[]{:S(2)}) collective-permute-start(bf16[256,256]{1,0:T(8,128)(2,1)S(1)} %get-tuple-element.32), channel_id=1, source_target_pairs={{0,4},{4,0},{8,12},{12,8},{16,20},{20,16},{24,28},{28,24},{1,5},{5... | collective-permute-start | bytes 393224 | tf_op jit(solution)/shard_map/ppermute | solution.py:574
  19.9 0.1 collective-permute-start.7
  20.0 0.0 slice-start
  20.0 0.0 copy-start.6
  20.0 0.0 copy-start.7
  20.0 0.0 copy-start.8
  20.0 0.0 slice-start.1
  20.0 3.5 %conv.1.sums_ref = f32[4,256,256]{2,1,0:T(8,128)S(1)} custom-call(bf16[2,2,288,512]{3,2,1,0:T(8,128)(2,1)S(1)} %get-tuple-element.30.faces_ref, bf16[512,1024]{1,0:T(8,128)(2,1)S(1)} %get-tuple-element.31.table_ref, s32[8,512]{1,0:T(8,128)S(1)} %get-tuple-element.29.place_ref, bf16[3,4,512,256]{3,2,1,0:T(8,128)(2,1)S(1)} %fold.1.refs_8_.w_ref), custom_call_target="tpu_custom_call" | custom-call | flops 2684354560 | bytes 6291456 | tf_op jit(solution)/shard_map/conv/pallas_call | solution.py:354
  23.5 0.0 collective-permute-done.6.pair_ref
  23.5 1.8 %collective-permute-done.7.step_ref = bf16[256,256]{1,0:T(8,128)(2,1)S(1)} collective-permute-done((bf16[256,256]{1,0:T(8,128)(2,1)S(1)}, bf16[256,256]{1,0:T(8,128)(2,1)S(1)}, u32[]{:S(2)}, u32[]{:S(2)}) %collective-permute-start.7) | collective-permute-done | bytes 131104 | tf_op jit(solution)/shard_map/ppermute | solution.py:575
  25.3 0.0 copy-done.6
  25.3 0.7 %finish.1 = (bf16[2,512,256]{2,1,0:T(8,128)(2,1)S(1)}, f32[112,128]{1,0:T(8,128)S(1)}, bf16[112,512]{1,0:T(8,128)(2,1)S(1)}, bf16[112,512]{1,0:T(8,128)(2,1)S(1)...) custom-call(s32[8,512]{1,0:T(8,128)S(1)} %get-tuple-element.29.place_ref, f32[4,256,256]{2,1,0:T(8,128)S(1)} %conv.1.sums_ref, ...), custom_call_target="tpu_custom_call" | custom-call | flops 268435456 | bytes 3145728 | tf_op jit(solution)/shard_map/finish/pallas_call | solution.py:399
  26.0 1.3 %collective-permute-start.8 = (bf16[112,512]{1,0:T(8,128)(2,1)S(1)}, bf16[112,512]{1,0:T(8,128)(2,1)S(1)}, u32[]{:S(2)}, u32[]{:S(2)}) collective-permute-start(bf16[112,512]{1,0:T(8,128)(2,1)S(1)} %get-tuple-element.40), channel_id=1, source_target_pairs={{0,2},{1,3},{2,0},{3,1},{4,6},{5,7},{6,4},{7,5},{8,10},{9,11},{10,... | collective-permute-start | bytes 344072 | tf_op jit(solution)/shard_map/ppermute | solution.py:581
  27.3 2.5 %collective-permute-start.9 = (bf16[112,512]{1,0:T(8,128)(2,1)S(1)}, bf16[112,512]{1,0:T(8,128)(2,1)S(1)}, u32[]{:S(2)}, u32[]{:S(2)}) collective-permute-start(bf16[112,512]{1,0:T(8,128)(2,1)S(1)} %get-tuple-element.41), channel_id=1, source_target_pairs={{0,3},{1,2},{2,1},{3,0},{4,7},{5,6},{6,5},{7,4},{8,11},{9,10},{10,... | collective-permute-start | bytes 344072 | tf_op jit(solution)/shard_map/ppermute | solution.py:581
  29.8 0.0 collective-permute-start.10
  29.8 0.0 copy-done.7
  29.8 0.0 copy-done.8
  29.8 1.8 %unravel.1 = (bf16[4,16,2,32,64]{4,3,2,1,0:T(8,128)(2,1)}, bf16[512,256]{1,0:T(8,128)(2,1)S(1)}, bf16[512,256]{1,0:T(8,128)(2,1)S(1)}, bf16[64,512]{1,0:T(8,128)(2,1)S(1)}) custom-call(bf16[2,512,256]{2,1,0:T(8,128)(2,1)S(1)} %get-tuple-element.35.root_ref, bf16[256,128]{1,0:T(8,128)(2,1)S(1)} %copy-done.7, bf16[64,128]{1,0:T(8,128)(2,1)S(1)} %bitcast.12), custom_call_target="tpu_custom_call" | custom-call | flops 536870912 | bytes 2097152 | tf_op jit(solution)/shard_map/unravel/pallas_call | solution.py:450
  31.6 0.0 collective-permute-done.8.refs_7_
  31.6 3.1 %collective-permute-done.9.refs_8_ = bf16[112,512]{1,0:T(8,128)(2,1)S(1)} collective-permute-done((bf16[112,512]{1,0:T(8,128)(2,1)S(1)}, bf16[112,512]{1,0:T(8,128)(2,1)S(1)}, u32[]{:S(2)}, u32[]{:S(2)}) %collective-permute-start.9) | collective-permute-done | bytes 114720 | tf_op jit(solution)/shard_map/ppermute | solution.py:581
  34.7 0.0 collective-permute-done.10.refs_9_
  34.7 0.0 slice-done
  34.7 0.0 slice-done.1
  34.8 4.4 %fine_out.1 = bf16[112,64,512]{2,1,0:T(8,128)(2,1)} custom-call(bf16[112,64,512]{2,1,0:T(8,128)(2,1)S(1)} %bitcast.9, bf16[1792,512]{1,0:T(8,128)(2,1)S(1)} %hide.1.refs_1_, f32[112,128]{1,0:T(8,128)S(1)} %get-tuple-element.34.refs_2_, bf16[512,256]{1,0:T(8,128)(2,1)S(1)} %get-tuple-element.36.refs_3_, bf16[512,256]{1,0:T(8,128)(2,1)S(1)} %get-tuple-element.37.refs_4_, ...), custom_call_target="tpu_custom_call" | custom-call | flops 1879048192 | bytes 14680064 | tf_op jit(solution)/shard_map/fine_out/pallas_call | solution.py:523
  (1 shorter events, 0.0 us)
Async XLA Ops:
  0.6 9.8 %copy-start.5 = (bf16[64,128]{1,0:T(8,128)(2,1)S(1)}, bf16[64,128]{1,0:T(8,128)(2,1)}, u32[]{:S(2)}) copy-start(bf16[64,128]{1,0:T(8,128)(2,1)} %w_ref.1) | copy-start | bytes 49156
  0.6 14.1 %copy-start.1 = (bf16[64,256,3,3,3]{1,0,4,3,2:T(8,128)(2,1)S(1)}, bf16[64,256,3,3,3]{1,0,4,3,2:T(8,128)(2,1)}, u32[]{:S(2)}) copy-start(bf16[64,256,3,3,3]{1,0,4,3,2:T(8,128)(2,1)} %param.14) | copy-start | bytes 2654212
  0.7 14.1 %copy-start.4 = (bf16[128,256]{1,0:T(8,128)(2,1)S(1)}, bf16[128,256]{1,0:T(8,128)(2,1)}, u32[]{:S(2)}) copy-start(bf16[128,256]{1,0:T(8,128)(2,1)} %in_ref.1) | copy-start | bytes 196612
  7.7 4.6 %collective-permute-start.1 = (bf16[464,128]{1,0:T(8,128)(2,1)}, bf16[464,128]{1,0:T(8,128)(2,1)S(1)}, u32[]{:S(2)}, u32[]{:S(2)}) collective-permute-start(bf16[464,128]{1,0:T(8,128)(2,1)} %get-tuple-element.26.refs_0_), channel_id=1, source_target_pairs={{0,2},{1,3},{2,0},{3,1},{4,6},{5,7},{6,4},{7,5},{8,10},{9,11},{10,... | collective-permute-start | bytes 356360 | tf_op jit(solution)/shard_map/ppermute | solution.py:558
  8.9 6.6 %collective-permute-start = (bf16[448,128]{1,0:T(8,128)(2,1)}, bf16[448,128]{1,0:T(8,128)(2,1)S(1)}, u32[]{:S(2)}, u32[]{:S(2)}) collective-permute-start(bf16[448,128]{1,0:T(8,128)(2,1)} %get-tuple-element.23.refs_4_), channel_id=1, source_target_pairs={{0,2},{1,3},{2,0},{3,1},{4,6},{5,7},{6,4},{7,5},{8,10},{9,11},{10,... | collective-permute-start | bytes 344072 | tf_op jit(solution)/shard_map/ppermute | solution.py:559
  9.2 6.9 %collective-permute-start.4 = (bf16[448,128]{1,0:T(8,128)(2,1)}, bf16[448,128]{1,0:T(8,128)(2,1)S(1)}, u32[]{:S(2)}, u32[]{:S(2)}) collective-permute-start(bf16[448,128]{1,0:T(8,128)(2,1)} %get-tuple-element.23.refs_4_), channel_id=1, source_target_pairs={{0,1},{1,0},{2,3},{3,2},{4,5},{5,4},{6,7},{7,6},{8,9},{9,8},{10,11... | collective-permute-start | bytes 344072 | tf_op jit(solution)/shard_map/ppermute | solution.py:559
  10.4 5.6 %collective-permute-start.2 = (bf16[464,128]{1,0:T(8,128)(2,1)}, bf16[464,128]{1,0:T(8,128)(2,1)S(1)}, u32[]{:S(2)}, u32[]{:S(2)}) collective-permute-start(bf16[464,128]{1,0:T(8,128)(2,1)} %get-tuple-element.26.refs_0_), channel_id=1, source_target_pairs={{0,1},{1,0},{2,3},{3,2},{4,5},{5,4},{6,7},{7,6},{8,9},{9,8},{10,11... | collective-permute-start | bytes 356360 | tf_op jit(solution)/shard_map/ppermute | solution.py:558
  10.4 1.2 %copy-start = (bf16[1792,256]{1,0:T(8,128)(2,1)S(1)}, bf16[1792,256]{1,0:T(8,128)(2,1)}, u32[]{:S(2)}) copy-start(bf16[1792,256]{1,0:T(8,128)(2,1)} %get-tuple-element.24.turned_ref) | copy-start | bytes 2752516
  11.6 5.4 %copy-start.2 = (bf16[464,128]{1,0:T(8,128)(2,1)S(1)}, bf16[464,128]{1,0:T(8,128)(2,1)}, u32[]{:S(2)}) copy-start(bf16[464,128]{1,0:T(8,128)(2,1)} %get-tuple-element.26.refs_0_) | copy-start | bytes 356356
  11.6 5.4 %copy-start.3 = (bf16[448,128]{1,0:T(8,128)(2,1)S(1)}, bf16[448,128]{1,0:T(8,128)(2,1)}, u32[]{:S(2)}) copy-start(bf16[448,128]{1,0:T(8,128)(2,1)} %get-tuple-element.23.refs_4_) | copy-start | bytes 344068
  12.3 4.7 %collective-permute-start.3 = (bf16[464,128]{1,0:T(8,128)(2,1)S(1)}, bf16[464,128]{1,0:T(8,128)(2,1)S(1)}, u32[]{:S(2)}, u32[]{:S(2)}) collective-permute-start(bf16[464,128]{1,0:T(8,128)(2,1)S(1)} %collective-permute-done.1.refs_1_), channel_id=1, source_target_pairs={{0,1},{1,0},{2,3},{3,2},{4,5},{5,4},{6,7},{7,6},{8,9},{9,8},{10,11... | collective-permute-start | bytes 356360 | tf_op jit(solution)/shard_map/ppermute | solution.py:558
  15.5 1.5 %collective-permute-start.5 = (bf16[448,128]{1,0:T(8,128)(2,1)S(1)}, bf16[448,128]{1,0:T(8,128)(2,1)S(1)}, u32[]{:S(2)}, u32[]{:S(2)}) collective-permute-start(bf16[448,128]{1,0:T(8,128)(2,1)S(1)} %collective-permute-done.refs_5_), channel_id=1, source_target_pairs={{0,1},{1,0},{2,3},{3,2},{4,5},{5,4},{6,7},{7,6},{8,9},{9,8},{10,11... | collective-permute-start | bytes 344072 | tf_op jit(solution)/shard_map/ppermute | solution.py:559
  18.6 4.9 %collective-permute-start.6 = (bf16[256,256]{1,0:T(8,128)(2,1)S(1)}, bf16[256,256]{1,0:T(8,128)(2,1)S(1)}, u32[]{:S(2)}, u32[]{:S(2)}) collective-permute-start(bf16[256,256]{1,0:T(8,128)(2,1)S(1)} %get-tuple-element.32), channel_id=1, source_target_pairs={{0,4},{4,0},{8,12},{12,8},{16,20},{20,16},{24,28},{28,24},{1,5},{5... | collective-permute-start | bytes 393224 | tf_op jit(solution)/shard_map/ppermute | solution.py:574
  19.9 5.4 %collective-permute-start.7 = (bf16[256,256]{1,0:T(8,128)(2,1)S(1)}, bf16[256,256]{1,0:T(8,128)(2,1)S(1)}, u32[]{:S(2)}, u32[]{:S(2)}) collective-permute-start(bf16[256,256]{1,0:T(8,128)(2,1)S(1)} %get-tuple-element.33), channel_id=1, source_target_pairs={{0,1},{1,0},{2,3},{3,2},{4,8},{5,9},{6,10},{7,11},{8,4},{9,5},{10,... | collective-permute-start | bytes 393224 | tf_op jit(solution)/shard_map/ppermute | solution.py:575
  20.0 14.7 %slice-start = ((s8[7340032]{0:T(1024)(128)(4,1)}), s8[4194304]{0:T(1024)(128)(4,1)S(1)}, s32[]{:S(2)}) async-start(s8[7340032]{0:T(1024)(128)(4,1)} %bitcast.8), calls=%async_computation | async-start | bytes 8388608
  20.0 5.3 %copy-start.6 = (f32[64]{0:T(128)S(1)}, f32[64]{0:T(128)}, u32[]{:S(2)}) copy-start(f32[64]{0:T(128)} %param.15) | copy-start | bytes 772
  20.0 9.8 %copy-start.7 = (bf16[256,128]{1,0:T(8,128)(2,1)S(1)}, bf16[256,128]{1,0:T(8,128)(2,1)}, u32[]{:S(2)}) copy-start(bf16[256,128]{1,0:T(8,128)(2,1)} %down_ref.1) | copy-start | bytes 196612
  20.0 9.8 %copy-start.8 = (bf16[128,64]{0,1:T(8,128)(2,1)S(1)}, bf16[128,64]{0,1:T(8,128)(2,1)}, u32[]{:S(2)}) copy-start(bf16[128,64]{0,1:T(8,128)(2,1)} %param.17) | copy-start | bytes 49156
  20.0 14.7 %slice-start.1 = ((s8[7340032]{0:T(1024)(128)(4,1)}), s8[3145728]{0:T(1024)(128)(4,1)S(1)}, s32[]{:S(2)}) async-start(s8[7340032]{0:T(1024)(128)(4,1)} %bitcast.8), calls=%async_computation.1 | async-start | bytes 6291456
  26.0 5.6 %collective-permute-start.8 = (bf16[112,512]{1,0:T(8,128)(2,1)S(1)}, bf16[112,512]{1,0:T(8,128)(2,1)S(1)}, u32[]{:S(2)}, u32[]{:S(2)}) collective-permute-start(bf16[112,512]{1,0:T(8,128)(2,1)S(1)} %get-tuple-element.40), channel_id=1, source_target_pairs={{0,2},{1,3},{2,0},{3,1},{4,6},{5,7},{6,4},{7,5},{8,10},{9,11},{10,... | collective-permute-start | bytes 344072 | tf_op jit(solution)/shard_map/ppermute | solution.py:581
  27.3 7.4 %collective-permute-start.9 = (bf16[112,512]{1,0:T(8,128)(2,1)S(1)}, bf16[112,512]{1,0:T(8,128)(2,1)S(1)}, u32[]{:S(2)}, u32[]{:S(2)}) collective-permute-start(bf16[112,512]{1,0:T(8,128)(2,1)S(1)} %get-tuple-element.41), channel_id=1, source_target_pairs={{0,3},{1,2},{2,1},{3,0},{4,7},{5,6},{6,5},{7,4},{8,11},{9,10},{10,... | collective-permute-start | bytes 344072 | tf_op jit(solution)/shard_map/ppermute | solution.py:581
  29.8 4.9 %collective-permute-start.10 = (bf16[112,512]{1,0:T(8,128)(2,1)S(1)}, bf16[112,512]{1,0:T(8,128)(2,1)S(1)}, u32[]{:S(2)}, u32[]{:S(2)}) collective-permute-start(bf16[112,512]{1,0:T(8,128)(2,1)S(1)} %get-tuple-element.42), channel_id=1, source_target_pairs={{0,1},{1,0},{2,3},{3,2},{4,5},{5,4},{6,7},{7,6},{8,9},{9,8},{10,11... | collective-permute-start | bytes 344072 | tf_op jit(solution)/shard_map/ppermute | solution.py:581

commit v7 on v6

--- a/solution.py
+++ b/solution.py
@@ -519,7 +519,7 @@
     depth = lift.shape[1] // 2
     group = 256 // width
     groups = len(come)
-    chunk = parts_of(total, group, 16)
+    chunk = parts_of(total, group, 8)
     return pl.pallas_call(
         functools.partial(fine_out_kernel, groups),
         in_specs=[VMEM] * (6 + groups),

time: 39.4 us -> 39.4 us (level)
  no operation moved by 1% of the time
where the time goes in v7:
time: 39.4 us; the launch traced here: 39 us
  Pallas kernels  20.2 us (51%)
  starting transfers between devices  10.9 us (28%)
  waiting for transfers between devices  5.89 us (15%)
  local copies, waits for them, and re-layouts  1.22 us (3%)
  between operations  0.76 us (2%)
    pallas_call x1, Pallas kernels, fine_in(): pl.pallas_call(functools.partial(fine_in_kernel, total=total, padded=padd...  6.99 us
    pallas_call x1, Pallas kernels, fine_out(): pl.pallas_call(functools.partial(fine_out_kernel, groups), in_specs=[VMEM...  4.29 us
    ppermute x3, starting transfers between devices, shards(): lax.ppermute(send, 'ga', [(i, i ^ offsets[k]) for i in range(groups)])  3.79 us
    ppermute x3, starting transfers between devices, shards(): gathered += [lax.ppermute(part, 'ga', swap) for part in gathered]  3.73 us
    pallas_call x1, Pallas kernels, conv(): pl.pallas_call(conv_kernel, in_specs=[VMEM] * 4, out_specs=VMEM, out_shap...  3.45 us
    ppermute x3, waiting for transfers between devices, shards(): lax.ppermute(send, 'ga', [(i, i ^ offsets[k]) for i in range(groups)])  3.12 us
    ppermute x3, starting transfers between devices, shards(): others += [lax.ppermute(part, 'ga', swap) for part in others]  2.01 us
    pallas_call x1, Pallas kernels, unravel(): pl.pallas_call(functools.partial(unravel_kernel, offsets), in_specs=[VMEM...  1.79 us
  transfers between devices with their start and end apart: 11, of which 3 were waited for; matrix products, arithmetic and copies ran while one was open for 0% of the time, Pallas kernels for 17%

profile of v7, /device:TPU:25, one launch (start us, length us, event | category | flops | bytes accessed | tf_op | source)
XLA Modules:
  0.0 39.0 jit_solution(17199034665822564926)
XLA Ops:
  0.6 0.0 copy-start.5
  0.6 0.0 copy-start.1
  0.7 0.0 copy-start.4
  0.7 7.0 %fine_in.1 = (bf16[1792,256]{1,0:T(8,128)(2,1)}, bf16[464,128]{1,0:T(8,128)(2,1)}, bf16[448,128]{1,0:T(8,128)(2,1)}) custom-call(s32[1,112]{1,0:T(1,128)} %bitcast.13, s32[1,8]{1,0:T(1,128)} %bitcast.14, bf16[112,64,512]{2,1,0:T(8,128)(2,1)} %refs_0_.1, bf16[64,128]{1,0:T(8,128)(2,1)} %w_ref.1), custom_call_target="tpu_custom_call" | custom-call | flops 1879048192 | bytes 7340032 | tf_op jit(solution)/shard_map/fine_in/pallas_call | solution.py:158
  7.7 1.3 %collective-permute-start.1 = (bf16[464,128]{1,0:T(8,128)(2,1)}, bf16[464,128]{1,0:T(8,128)(2,1)S(1)}, u32[]{:S(2)}, u32[]{:S(2)}) collective-permute-start(bf16[464,128]{1,0:T(8,128)(2,1)} %get-tuple-element.26.refs_0_), channel_id=1, source_target_pairs={{0,2},{1,3},{2,0},{3,1},{4,6},{5,7},{6,4},{7,5},{8,10},{9,11},{10,... | collective-permute-start | bytes 356360 | tf_op jit(solution)/shard_map/ppermute | solution.py:558
  8.9 0.3 collective-permute-start
  9.2 1.2 %collective-permute-start.4 = (bf16[448,128]{1,0:T(8,128)(2,1)}, bf16[448,128]{1,0:T(8,128)(2,1)S(1)}, u32[]{:S(2)}, u32[]{:S(2)}) collective-permute-start(bf16[448,128]{1,0:T(8,128)(2,1)} %get-tuple-element.23.refs_4_), channel_id=1, source_target_pairs={{0,1},{1,0},{2,3},{3,2},{4,5},{5,4},{6,7},{7,6},{8,9},{9,8},{10,11... | collective-permute-start | bytes 344072 | tf_op jit(solution)/shard_map/ppermute | solution.py:559
  10.4 0.0 collective-permute-start.2
  10.4 0.0 copy-done.5
  10.4 0.0 copy-start
  10.4 1.2 %copy-done = bf16[1792,256]{1,0:T(8,128)(2,1)S(1)} copy-done((bf16[1792,256]{1,0:T(8,128)(2,1)S(1)}, bf16[1792,256]{1,0:T(8,128)(2,1)}, u32[]{:S(2)}) %copy-start) | copy-done | bytes 917528
  11.6 0.0 copy-start.2
  11.6 0.0 copy-start.3
  11.6 0.7 %hide.1.refs_1_ = bf16[1792,512]{1,0:T(8,128)(2,1)S(1)} custom-call(bf16[1792,256]{1,0:T(8,128)(2,1)S(1)} %copy-done, bf16[64,128]{1,0:T(8,128)(2,1)S(1)} %copy-done.5), custom_call_target="tpu_custom_call" | custom-call | flops 469762048 | bytes 2752512 | tf_op jit(solution)/shard_map/hide/pallas_call | solution.py:195
  12.3 0.0 collective-permute-done.1.refs_1_
  12.3 2.4 %collective-permute-start.3 = (bf16[464,128]{1,0:T(8,128)(2,1)S(1)}, bf16[464,128]{1,0:T(8,128)(2,1)S(1)}, u32[]{:S(2)}, u32[]{:S(2)}) collective-permute-start(bf16[464,128]{1,0:T(8,128)(2,1)S(1)} %collective-permute-done.1.refs_1_), channel_id=1, source_target_pairs={{0,1},{1,0},{2,3},{3,2},{4,5},{5,4},{6,7},{7,6},{8,9},{9,8},{10,11... | collective-permute-start | bytes 356360 | tf_op jit(solution)/shard_map/ppermute | solution.py:558
  14.7 0.0 copy-done.1
  14.7 0.0 copy-done.4
  14.7 0.8 %fold.1.refs_8_.w_ref = bf16[3,4,512,256]{3,2,1,0:T(8,128)(2,1)S(1)} custom-call(bf16[3,3,3,64,256]{4,3,2,1,0:T(8,128)(2,1)S(1)} %bitcast.10, bf16[128,256]{1,0:T(8,128)(2,1)S(1)} %copy-done.4), custom_call_target="tpu_custom_call" | custom-call | flops 301989888 | bytes 6291456 | tf_op jit(solution)/shard_map/fold/pallas_call | solution.py:228
  15.5 0.0 collective-permute-done.refs_5_
  15.5 0.5 %collective-permute-start.5 = (bf16[448,128]{1,0:T(8,128)(2,1)S(1)}, bf16[448,128]{1,0:T(8,128)(2,1)S(1)}, u32[]{:S(2)}, u32[]{:S(2)}) collective-permute-start(bf16[448,128]{1,0:T(8,128)(2,1)S(1)} %collective-permute-done.refs_5_), channel_id=1, source_target_pairs={{0,1},{1,0},{2,3},{3,2},{4,5},{5,4},{6,7},{7,6},{8,9},{9,8},{10,11... | collective-permute-start | bytes 344072 | tf_op jit(solution)/shard_map/ppermute | solution.py:559
  16.0 0.0 collective-permute-done.4.refs_6_
  16.1 0.0 collective-permute-done.2.refs_2_
  16.1 1.0 %collective-permute-done.5.refs_7_ = bf16[448,128]{1,0:T(8,128)(2,1)S(1)} collective-permute-done((bf16[448,128]{1,0:T(8,128)(2,1)S(1)}, bf16[448,128]{1,0:T(8,128)(2,1)S(1)}, u32[]{:S(2)}, u32[]{:S(2)}) %collective-permute-start.5) | collective-permute-done | bytes 114720 | tf_op jit(solution)/shard_map/ppermute | solution.py:559
  17.0 0.0 collective-permute-done.3.refs_3_
  17.0 0.0 copy-done.2
  17.0 0.0 copy-done.3
  17.0 1.6 %place.1 = (bf16[2,2,288,512]{3,2,1,0:T(8,128)(2,1)S(1)}, bf16[512,1024]{1,0:T(8,128)(2,1)S(1)}, s32[8,512]{1,0:T(8,128)S(1)}, bf16[256,256]{1,0:T(8,128)(2,1)S(1)}, bf16[256,256]{1,0:T(8,128)(2,1)S(1)}) custom-call(bf16[464,128]{1,0:T(8,128)(2,1)S(1)} %copy-done.2, bf16[464,128]{1,0:T(8,128)(2,1)S(1)} %collective-permute-done.1.refs_1_, ...), custom_call_target="tpu_custom_call" | custom-call | flops 536870912 | bytes 6291456 | tf_op jit(solution)/shard_map/place/pallas_call | solution.py:319
  18.6 1.3 %collective-permute-start.6 = (bf16[256,256]{1,0:T(8,128)(2,1)S(1)}, bf16[256,256]{1,0:T(8,128)(2,1)S(1)}, u32[]{:S(2)}, u32[]{:S(2)}) collective-permute-start(bf16[256,256]{1,0:T(8,128)(2,1)S(1)} %get-tuple-element.32), channel_id=1, source_target_pairs={{0,4},{4,0},{8,12},{12,8},{16,20},{20,16},{24,28},{28,24},{1,5},{5... | collective-permute-start | bytes 393224 | tf_op jit(solution)/shard_map/ppermute | solution.py:574
  19.9 0.1 collective-permute-start.7
  20.0 0.0 slice-start
  20.0 0.0 copy-start.6
  20.0 0.0 copy-start.7
  20.0 0.0 copy-start.8
  20.0 0.0 slice-start.1
  20.0 3.5 %conv.1.sums_ref = f32[4,256,256]{2,1,0:T(8,128)S(1)} custom-call(bf16[2,2,288,512]{3,2,1,0:T(8,128)(2,1)S(1)} %get-tuple-element.30.faces_ref, bf16[512,1024]{1,0:T(8,128)(2,1)S(1)} %get-tuple-element.31.table_ref, s32[8,512]{1,0:T(8,128)S(1)} %get-tuple-element.29.place_ref, bf16[3,4,512,256]{3,2,1,0:T(8,128)(2,1)S(1)} %fold.1.refs_8_.w_ref), custom_call_target="tpu_custom_call" | custom-call | flops 2684354560 | bytes 6291456 | tf_op jit(solution)/shard_map/conv/pallas_call | solution.py:354
  23.5 0.0 collective-permute-done.6.pair_ref
  23.5 1.8 %collective-permute-done.7.step_ref = bf16[256,256]{1,0:T(8,128)(2,1)S(1)} collective-permute-done((bf16[256,256]{1,0:T(8,128)(2,1)S(1)}, bf16[256,256]{1,0:T(8,128)(2,1)S(1)}, u32[]{:S(2)}, u32[]{:S(2)}) %collective-permute-start.7) | collective-permute-done | bytes 131104 | tf_op jit(solution)/shard_map/ppermute | solution.py:575
  25.3 0.0 copy-done.6
  25.3 0.7 %finish.1 = (bf16[2,512,256]{2,1,0:T(8,128)(2,1)S(1)}, f32[112,128]{1,0:T(8,128)S(1)}, bf16[112,512]{1,0:T(8,128)(2,1)S(1)}, bf16[112,512]{1,0:T(8,128)(2,1)S(1)...) custom-call(s32[8,512]{1,0:T(8,128)S(1)} %get-tuple-element.29.place_ref, f32[4,256,256]{2,1,0:T(8,128)S(1)} %conv.1.sums_ref, ...), custom_call_target="tpu_custom_call" | custom-call | flops 268435456 | bytes 3145728 | tf_op jit(solution)/shard_map/finish/pallas_call | solution.py:399
  26.0 1.3 %collective-permute-start.8 = (bf16[112,512]{1,0:T(8,128)(2,1)S(1)}, bf16[112,512]{1,0:T(8,128)(2,1)S(1)}, u32[]{:S(2)}, u32[]{:S(2)}) collective-permute-start(bf16[112,512]{1,0:T(8,128)(2,1)S(1)} %get-tuple-element.40), channel_id=1, source_target_pairs={{0,2},{1,3},{2,0},{3,1},{4,6},{5,7},{6,4},{7,5},{8,10},{9,11},{10,... | collective-permute-start | bytes 344072 | tf_op jit(solution)/shard_map/ppermute | solution.py:581
  27.3 2.5 %collective-permute-start.9 = (bf16[112,512]{1,0:T(8,128)(2,1)S(1)}, bf16[112,512]{1,0:T(8,128)(2,1)S(1)}, u32[]{:S(2)}, u32[]{:S(2)}) collective-permute-start(bf16[112,512]{1,0:T(8,128)(2,1)S(1)} %get-tuple-element.41), channel_id=1, source_target_pairs={{0,3},{1,2},{2,1},{3,0},{4,7},{5,6},{6,5},{7,4},{8,11},{9,10},{10,... | collective-permute-start | bytes 344072 | tf_op jit(solution)/shard_map/ppermute | solution.py:581
  29.8 0.0 collective-permute-start.10
  29.8 0.0 copy-done.7
  29.8 0.0 copy-done.8
  29.8 1.8 %unravel.1 = (bf16[4,16,2,32,64]{4,3,2,1,0:T(8,128)(2,1)}, bf16[512,256]{1,0:T(8,128)(2,1)S(1)}, bf16[512,256]{1,0:T(8,128)(2,1)S(1)}, bf16[64,512]{1,0:T(8,128)(2,1)S(1)}) custom-call(bf16[2,512,256]{2,1,0:T(8,128)(2,1)S(1)} %get-tuple-element.35.root_ref, bf16[256,128]{1,0:T(8,128)(2,1)S(1)} %copy-done.7, bf16[64,128]{1,0:T(8,128)(2,1)S(1)} %bitcast.12), custom_call_target="tpu_custom_call" | custom-call | flops 536870912 | bytes 2097152 | tf_op jit(solution)/shard_map/unravel/pallas_call | solution.py:450
  31.6 0.0 collective-permute-done.8.refs_7_
  31.6 3.1 %collective-permute-done.9.refs_8_ = bf16[112,512]{1,0:T(8,128)(2,1)S(1)} collective-permute-done((bf16[112,512]{1,0:T(8,128)(2,1)S(1)}, bf16[112,512]{1,0:T(8,128)(2,1)S(1)}, u32[]{:S(2)}, u32[]{:S(2)}) %collective-permute-start.9) | collective-permute-done | bytes 114720 | tf_op jit(solution)/shard_map/ppermute | solution.py:581
  34.7 0.0 collective-permute-done.10.refs_9_
  34.7 0.0 slice-done
  34.7 0.0 slice-done.1
  34.8 4.3 %fine_out.1 = bf16[112,64,512]{2,1,0:T(8,128)(2,1)} custom-call(bf16[112,64,512]{2,1,0:T(8,128)(2,1)S(1)} %bitcast.9, bf16[1792,512]{1,0:T(8,128)(2,1)S(1)} %hide.1.refs_1_, f32[112,128]{1,0:T(8,128)S(1)} %get-tuple-element.34.refs_2_, bf16[512,256]{1,0:T(8,128)(2,1)S(1)} %get-tuple-element.36.refs_3_, bf16[512,256]{1,0:T(8,128)(2,1)S(1)} %get-tuple-element.37.refs_4_, ...), custom_call_target="tpu_custom_call" | custom-call | flops 1879048192 | bytes 14680064 | tf_op jit(solution)/shard_map/fine_out/pallas_call | solution.py:523
  (1 shorter events, 0.0 us)
Async XLA Ops:
  0.6 9.8 %copy-start.5 = (bf16[64,128]{1,0:T(8,128)(2,1)S(1)}, bf16[64,128]{1,0:T(8,128)(2,1)}, u32[]{:S(2)}) copy-start(bf16[64,128]{1,0:T(8,128)(2,1)} %w_ref.1) | copy-start | bytes 49156
  0.6 14.1 %copy-start.1 = (bf16[64,256,3,3,3]{1,0,4,3,2:T(8,128)(2,1)S(1)}, bf16[64,256,3,3,3]{1,0,4,3,2:T(8,128)(2,1)}, u32[]{:S(2)}) copy-start(bf16[64,256,3,3,3]{1,0,4,3,2:T(8,128)(2,1)} %param.14) | copy-start | bytes 2654212
  0.7 14.1 %copy-start.4 = (bf16[128,256]{1,0:T(8,128)(2,1)S(1)}, bf16[128,256]{1,0:T(8,128)(2,1)}, u32[]{:S(2)}) copy-start(bf16[128,256]{1,0:T(8,128)(2,1)} %in_ref.1) | copy-start | bytes 196612
  7.7 4.6 %collective-permute-start.1 = (bf16[464,128]{1,0:T(8,128)(2,1)}, bf16[464,128]{1,0:T(8,128)(2,1)S(1)}, u32[]{:S(2)}, u32[]{:S(2)}) collective-permute-start(bf16[464,128]{1,0:T(8,128)(2,1)} %get-tuple-element.26.refs_0_), channel_id=1, source_target_pairs={{0,2},{1,3},{2,0},{3,1},{4,6},{5,7},{6,4},{7,5},{8,10},{9,11},{10,... | collective-permute-start | bytes 356360 | tf_op jit(solution)/shard_map/ppermute | solution.py:558
  8.9 6.6 %collective-permute-start = (bf16[448,128]{1,0:T(8,128)(2,1)}, bf16[448,128]{1,0:T(8,128)(2,1)S(1)}, u32[]{:S(2)}, u32[]{:S(2)}) collective-permute-start(bf16[448,128]{1,0:T(8,128)(2,1)} %get-tuple-element.23.refs_4_), channel_id=1, source_target_pairs={{0,2},{1,3},{2,0},{3,1},{4,6},{5,7},{6,4},{7,5},{8,10},{9,11},{10,... | collective-permute-start | bytes 344072 | tf_op jit(solution)/shard_map/ppermute | solution.py:559
  9.2 6.9 %collective-permute-start.4 = (bf16[448,128]{1,0:T(8,128)(2,1)}, bf16[448,128]{1,0:T(8,128)(2,1)S(1)}, u32[]{:S(2)}, u32[]{:S(2)}) collective-permute-start(bf16[448,128]{1,0:T(8,128)(2,1)} %get-tuple-element.23.refs_4_), channel_id=1, source_target_pairs={{0,1},{1,0},{2,3},{3,2},{4,5},{5,4},{6,7},{7,6},{8,9},{9,8},{10,11... | collective-permute-start | bytes 344072 | tf_op jit(solution)/shard_map/ppermute | solution.py:559
  10.4 5.6 %collective-permute-start.2 = (bf16[464,128]{1,0:T(8,128)(2,1)}, bf16[464,128]{1,0:T(8,128)(2,1)S(1)}, u32[]{:S(2)}, u32[]{:S(2)}) collective-permute-start(bf16[464,128]{1,0:T(8,128)(2,1)} %get-tuple-element.26.refs_0_), channel_id=1, source_target_pairs={{0,1},{1,0},{2,3},{3,2},{4,5},{5,4},{6,7},{7,6},{8,9},{9,8},{10,11... | collective-permute-start | bytes 356360 | tf_op jit(solution)/shard_map/ppermute | solution.py:558
  10.4 1.2 %copy-start = (bf16[1792,256]{1,0:T(8,128)(2,1)S(1)}, bf16[1792,256]{1,0:T(8,128)(2,1)}, u32[]{:S(2)}) copy-start(bf16[1792,256]{1,0:T(8,128)(2,1)} %get-tuple-element.24.turned_ref) | copy-start | bytes 2752516
  11.6 5.4 %copy-start.2 = (bf16[464,128]{1,0:T(8,128)(2,1)S(1)}, bf16[464,128]{1,0:T(8,128)(2,1)}, u32[]{:S(2)}) copy-start(bf16[464,128]{1,0:T(8,128)(2,1)} %get-tuple-element.26.refs_0_) | copy-start | bytes 356356
  11.6 5.4 %copy-start.3 = (bf16[448,128]{1,0:T(8,128)(2,1)S(1)}, bf16[448,128]{1,0:T(8,128)(2,1)}, u32[]{:S(2)}) copy-start(bf16[448,128]{1,0:T(8,128)(2,1)} %get-tuple-element.23.refs_4_) | copy-start | bytes 344068
  12.3 4.7 %collective-permute-start.3 = (bf16[464,128]{1,0:T(8,128)(2,1)S(1)}, bf16[464,128]{1,0:T(8,128)(2,1)S(1)}, u32[]{:S(2)}, u32[]{:S(2)}) collective-permute-start(bf16[464,128]{1,0:T(8,128)(2,1)S(1)} %collective-permute-done.1.refs_1_), channel_id=1, source_target_pairs={{0,1},{1,0},{2,3},{3,2},{4,5},{5,4},{6,7},{7,6},{8,9},{9,8},{10,11... | collective-permute-start | bytes 356360 | tf_op jit(solution)/shard_map/ppermute | solution.py:558
  15.5 1.5 %collective-permute-start.5 = (bf16[448,128]{1,0:T(8,128)(2,1)S(1)}, bf16[448,128]{1,0:T(8,128)(2,1)S(1)}, u32[]{:S(2)}, u32[]{:S(2)}) collective-permute-start(bf16[448,128]{1,0:T(8,128)(2,1)S(1)} %collective-permute-done.refs_5_), channel_id=1, source_target_pairs={{0,1},{1,0},{2,3},{3,2},{4,5},{5,4},{6,7},{7,6},{8,9},{9,8},{10,11... | collective-permute-start | bytes 344072 | tf_op jit(solution)/shard_map/ppermute | solution.py:559
  18.6 4.9 %collective-permute-start.6 = (bf16[256,256]{1,0:T(8,128)(2,1)S(1)}, bf16[256,256]{1,0:T(8,128)(2,1)S(1)}, u32[]{:S(2)}, u32[]{:S(2)}) collective-permute-start(bf16[256,256]{1,0:T(8,128)(2,1)S(1)} %get-tuple-element.32), channel_id=1, source_target_pairs={{0,4},{4,0},{8,12},{12,8},{16,20},{20,16},{24,28},{28,24},{1,5},{5... | collective-permute-start | bytes 393224 | tf_op jit(solution)/shard_map/ppermute | solution.py:574
  19.9 5.4 %collective-permute-start.7 = (bf16[256,256]{1,0:T(8,128)(2,1)S(1)}, bf16[256,256]{1,0:T(8,128)(2,1)S(1)}, u32[]{:S(2)}, u32[]{:S(2)}) collective-permute-start(bf16[256,256]{1,0:T(8,128)(2,1)S(1)} %get-tuple-element.33), channel_id=1, source_target_pairs={{0,1},{1,0},{2,3},{3,2},{4,8},{5,9},{6,10},{7,11},{8,4},{9,5},{10,... | collective-permute-start | bytes 393224 | tf_op jit(solution)/shard_map/ppermute | solution.py:575
  20.0 14.7 %slice-start = ((s8[7340032]{0:T(1024)(128)(4,1)}), s8[4194304]{0:T(1024)(128)(4,1)S(1)}, s32[]{:S(2)}) async-start(s8[7340032]{0:T(1024)(128)(4,1)} %bitcast.8), calls=%async_computation | async-start | bytes 8388608
  20.0 5.3 %copy-start.6 = (f32[64]{0:T(128)S(1)}, f32[64]{0:T(128)}, u32[]{:S(2)}) copy-start(f32[64]{0:T(128)} %param.15) | copy-start | bytes 772
  20.0 9.8 %copy-start.7 = (bf16[256,128]{1,0:T(8,128)(2,1)S(1)}, bf16[256,128]{1,0:T(8,128)(2,1)}, u32[]{:S(2)}) copy-start(bf16[256,128]{1,0:T(8,128)(2,1)} %down_ref.1) | copy-start | bytes 196612
  20.0 9.8 %copy-start.8 = (bf16[128,64]{0,1:T(8,128)(2,1)S(1)}, bf16[128,64]{0,1:T(8,128)(2,1)}, u32[]{:S(2)}) copy-start(bf16[128,64]{0,1:T(8,128)(2,1)} %param.17) | copy-start | bytes 49156
  20.0 14.7 %slice-start.1 = ((s8[7340032]{0:T(1024)(128)(4,1)}), s8[3145728]{0:T(1024)(128)(4,1)S(1)}, s32[]{:S(2)}) async-start(s8[7340032]{0:T(1024)(128)(4,1)} %bitcast.8), calls=%async_computation.1 | async-start | bytes 6291456
  26.0 5.6 %collective-permute-start.8 = (bf16[112,512]{1,0:T(8,128)(2,1)S(1)}, bf16[112,512]{1,0:T(8,128)(2,1)S(1)}, u32[]{:S(2)}, u32[]{:S(2)}) collective-permute-start(bf16[112,512]{1,0:T(8,128)(2,1)S(1)} %get-tuple-element.40), channel_id=1, source_target_pairs={{0,2},{1,3},{2,0},{3,1},{4,6},{5,7},{6,4},{7,5},{8,10},{9,11},{10,... | collective-permute-start | bytes 344072 | tf_op jit(solution)/shard_map/ppermute | solution.py:581
  27.3 7.4 %collective-permute-start.9 = (bf16[112,512]{1,0:T(8,128)(2,1)S(1)}, bf16[112,512]{1,0:T(8,128)(2,1)S(1)}, u32[]{:S(2)}, u32[]{:S(2)}) collective-permute-start(bf16[112,512]{1,0:T(8,128)(2,1)S(1)} %get-tuple-element.41), channel_id=1, source_target_pairs={{0,3},{1,2},{2,1},{3,0},{4,7},{5,6},{6,5},{7,4},{8,11},{9,10},{10,... | collective-permute-start | bytes 344072 | tf_op jit(solution)/shard_map/ppermute | solution.py:581
  29.8 4.9 %collective-permute-start.10 = (bf16[112,512]{1,0:T(8,128)(2,1)S(1)}, bf16[112,512]{1,0:T(8,128)(2,1)S(1)}, u32[]{:S(2)}, u32[]{:S(2)}) collective-permute-start(bf16[112,512]{1,0:T(8,128)(2,1)S(1)} %get-tuple-element.42), channel_id=1, source_target_pairs={{0,1},{1,0},{2,3},{3,2},{4,5},{5,4},{6,7},{7,6},{8,9},{9,8},{10,11... | collective-permute-start | bytes 344072 | tf_op jit(solution)/shard_map/ppermute | solution.py:581
